TPU v7x, 32 devices: a whole 2x2x4 slice. The times are simulated.
32 devices in a mesh: groups: 2 (over y), wide: 4 (over z), narrow: 4 (over x, core).
Axes of the slice: x: 2, y: 2, z: 4, core: 2. Of those that a mesh axis runs over, the one named last changes fastest.
Arguments:
- tokens: bfloat16 [8192, 8192], P(('groups', 'wide'), 'narrow'), parts along dimension 0, may hold values from -6 to 6
- value_weight: bfloat16 [8192, 1024], P('narrow'), may hold values from -0.0625 to 0.0625
- adapter_down_factors: bfloat16 [16, 8192, 64], P(('groups', 'wide'), 'narrow'), parts along dimension 0, may hold values from -0.0625 to 0.0625
- adapter_up_factors: bfloat16 [16, 64, 1024], P(('groups', 'wide'), None, 'narrow'), parts along dimension 0, may hold values from -0.75 to 0.75
- adapter_choice_index: int32 [256], P('groups'), parts along dimension 0, may hold values from 0 to 7
- adapter_mask: int32 [256], P('groups'), parts along dimension 0, may hold values 0 or 1
- prompt_token_length: int32 [256], P('groups'), parts along dimension 0, may hold values from 1 to 32, 2560 in all
Outputs:
- values: bfloat16 [8192, 1024], P(('groups', 'wide'), 'narrow'), parts along dimension 0
There are 2 independent parts, one for each index of `groups`. A program takes and returns all parts, laid end to end along the dimension named above; an argument that names none is the same for every part. Nothing has to cross between parts.
All inputs are finite; a program needn't handle non-finite values.
Results may differ from a plain program's by a relative error of at most 0.001.
Values may be sent and summed in bfloat16 or wider, within the bound.
No kernel may reach another device: no remote copies, remote signals or barrier semaphores. Data moves between devices by JAX's collectives and lax.ppermute only.
A program may use at most 64 MiB of HBM per device.

v0:
```python
import jax
import jax.numpy as jnp
from jax import lax
from jax.sharding import PartitionSpec as P

LEN = 32


def request_table(adapter_choice_index, adapter_mask, wide_count, per_device, owner_portion):
    requests = adapter_choice_index.reshape(wide_count, per_device)
    wanted = adapter_mask.reshape(wide_count, per_device) == 1
    owners = requests // owner_portion
    owner_range = jnp.arange(wide_count, dtype=jnp.int32)
    matches = wanted[:, None, :] & (owners[:, None, :] == owner_range[None, :, None])
    earliest = jnp.argmax(matches.astype(jnp.int32), axis=2)
    prompt_range = jnp.arange(per_device, dtype=jnp.int32)
    chosen = jnp.sum(
        jnp.where(prompt_range[None, None, :] == earliest[:, :, None], requests[:, None, :], 0),
        axis=2,
    )
    granted = jnp.where(jnp.any(matches, axis=2), chosen, -1)
    applied_delta = jnp.any(matches & (requests[:, None, :] == granted[:, :, None]), axis=1)
    return (granted, applied_delta)


def on_device(
    tokens,
    value_weight,
    adapter_down_factors,
    adapter_up_factors,
    adapter_choice_index,
    adapter_mask,
    prompt_token_length,
):
    wide_count = lax.axis_size("wide")
    token_position = lax.axis_index("wide")
    owner_portion = adapter_down_factors.shape[0]
    row_total = tokens.shape[0]
    per_device = row_total // LEN
    feature_share = tokens.shape[1]
    column_portion = adapter_up_factors.shape[2]
    granted, applied_delta = request_table(
        adapter_choice_index, adapter_mask, wide_count, per_device, owner_portion
    )
    partial_value = jnp.dot(tokens, value_weight, preferred_element_type=jnp.float32)
    base_sums = lax.psum_scatter(partial_value, "narrow", scatter_dimension=1, tiled=True)
    requests = adapter_choice_index.reshape(wide_count, per_device)
    my_requests = lax.dynamic_index_in_dim(requests, token_position, 0, keepdims=False)
    pieces = (
        lax.all_gather(adapter_down_factors, "wide", axis=0, tiled=True),
        lax.all_gather(adapter_up_factors, "wide", axis=0, tiled=True),
    )
    count = pieces[0].shape[0]
    picker = (my_requests[:, None] == jnp.arange(count, dtype=jnp.int32)[None, :]).astype(
        jnp.bfloat16
    )
    down_add = jnp.einsum(
        "pj,jkr->pkr", picker, pieces[0], preferred_element_type=jnp.float32
    ).astype(jnp.bfloat16)
    up_add = jnp.einsum(
        "pj,jrc->prc", picker, pieces[1], preferred_element_type=jnp.float32
    ).astype(jnp.bfloat16)
    prompt_rows = tokens.reshape(per_device, LEN, feature_share)
    shrunk = jnp.einsum("pld,pdr->plr", prompt_rows, down_add, preferred_element_type=jnp.float32)
    shrunk = lax.psum(shrunk, "narrow")
    delta_outputs = jnp.einsum(
        "plr,prc->plc", shrunk, up_add.astype(jnp.float32), precision=lax.Precision.HIGHEST
    )
    adapter_gate = lax.dynamic_index_in_dim(
        applied_delta, token_position, 0, keepdims=False
    ).astype(jnp.float32)
    delta_outputs = delta_outputs * adapter_gate[:, None, None]
    my_lengths = lax.dynamic_slice_in_dim(
        prompt_token_length, token_position * per_device, per_device
    )
    inside = jnp.arange(LEN, dtype=jnp.int32)[None, :] < my_lengths[:, None]
    summed = base_sums.reshape(per_device, LEN, column_portion) + delta_outputs
    values = jnp.where(inside[:, :, None], summed, jnp.float32(0.0))
    return values.reshape(row_total, column_portion).astype(jnp.bfloat16)


def solution(mesh):
    placed = (
        P(("groups", "wide"), "narrow"),
        P("narrow", None),
        P(("groups", "wide"), "narrow", None),
        P(("groups", "wide"), None, "narrow"),
        P("groups"),
        P("groups"),
        P("groups"),
    )
    return jax.shard_map(
        on_device,
        mesh=mesh,
        in_specs=placed,
        out_specs=P(("groups", "wide"), "narrow"),
        check_vma=False,
    )
```

profile of v0, /device:TPU:9, one launch (start us, length us, event | category | flops | bytes accessed | tf_op | source)
XLA Modules:
  0.0 155.2 jit_solution(4066027257412657707)
XLA Ops:
  6.5 0.0 all-gather.2.cloned.1.call-start
  6.5 0.7 all-gather.2.cloned.1.call-update
  7.3 0.0 all-reduce.2.cloned.1.call-start
  7.3 0.7 reshape.86
  8.1 46.1 %all-gather.2.cloned.1.call-done = bf16[8,2048,64]{1,2,0:T(8,128)(2,1)} async-done(((bf16[2,2048,64]{1,2,0:T(8,128)(2,1)}), bf16[8,2048,64]{1,2,0:T(8,128)(2,1)}) %all-gather.2.cloned.1.call-update) | async-done | bytes 2097168 | tf_op jit(solution)/shard_map/all_gather | solution.py:50
  54.2 0.0 copy-start.1
  54.2 4.1 %convolution_convert_fusion = bf16[32,2048,64]{1,0,2:T(8,128)(2,1)S(1)} fusion(bf16[8,2048,64]{1,2,0:T(8,128)(2,1)} %all-gather.2.cloned.1.call-done, s32[32]{0:T(128)S(1)} %dynamic-slice_bitcast_fusion), kind=kOutput, calls=%fused_computation.2 | convolution fusion | flops 71303424 | bytes 10485888 | tf_op jit(solution)/shard_map/pj,jkr->pkr/dot_general | solution.py:57
  58.3 0.0 copy-done.1
  58.3 5.9 %fusion.6 = f32[32,32,64]{2,1,0:T(8,128)} fusion(bf16[32,32,2048]{2,1,0:T(8,128)(2,1)S(1)} %bitcast.18, bf16[32,2048,64]{1,0,2:T(8,128)(2,1)S(1)} %convolution_convert_fusion), kind=kOutput, calls=%fused_computation.9 | convolution fusion | flops 268435456 | bytes 12845056 | tf_op jit(solution)/shard_map/pld,pdr->plr/dot_general | solution.py:64
  64.2 0.0 all-reduce.2.cloned.1.call-update
  64.2 0.0 reduce-scatter.2.cloned.1.call-start
  64.3 9.9 %fusion.21 = f32[1024,1024]{1,0:T(8,128)} fusion(bf16[1024,2048]{1,0:T(8,128)(2,1)} %param.7, bf16[2048,1024]{1,0:T(8,128)(2,1)} %param.8), kind=kOutput, calls=%fused_computation.36 | convolution fusion | flops 4294967296 | bytes 12582912 | tf_op jit(solution)/shard_map/dot_general | solution.py:45
  74.2 0.0 copy-start.2
  74.2 0.0 copy-start.3
  74.2 0.0 copy-start
  74.2 0.0 reduce-scatter.2.cloned.1.call-update
  74.2 0.6 copy-done.2
  74.8 0.1 eq.77
  74.9 0.0 copy-done.3
  74.9 0.1 dynamic_slice.11
  75.0 0.0 copy-done
  75.0 11.3 %all_gather.7 = bf16[8,64,256]{2,1,0:T(8,128)(2,1)S(1)} all-gather(bf16[2,64,256]{2,1,0:T(8,128)(2,1)S(1)} %copy-done), channel_id=1, replica_groups=mesh['groups'=2,'wide'=4,'narrow'=4] {'wide'}, dimensions={0}, use_global_device_ids=true | all-gather | bytes 327680 | tf_op jit(solution)/shard_map/all_gather | solution.py:51
  86.4 0.2 fusion.20
  86.5 0.8 iota_reduce_fusion
  87.3 0.2 select_reduce_fusion
  87.6 0.1 and_reduce_fusion
  87.7 0.1 iota_compare_fusion
  87.8 0.5 convolution_convert_fusion.1
  88.2 9.0 %all-reduce.2.cloned.1.call-done = f32[32,32,64]{2,1,0:T(8,128)} async-done(((f32[32,32,64]{2,1,0:T(8,128)}), f32[32,32,64]{2,1,0:T(8,128)}) %all-reduce.2.cloned.1.call-update) | async-done | bytes 262160 | tf_op jit(solution)/shard_map/psum | solution.py:65
  97.2 48.0 %reduce-scatter.2.cloned.1.call-done = f32[1024,256]{1,0:T(8,128)} async-done(((f32[1024,1024]{1,0:T(8,128)}), f32[1024,256]{1,0:T(8,128)}) %reduce-scatter.2.cloned.1.call-update) | async-done | bytes 1048592 | tf_op jit(solution)/shard_map/reduce_scatter | solution.py:46
  145.3 3.4 %fusion.5 = bf16[32,32,256]{2,1,0:T(8,128)(2,1)} fusion(f32[32,32,256]{2,1,0:T(8,128)} %bitcast.17, f32[32,32,64]{2,1,0:T(8,128)} %all-reduce.2.cloned.1.call-done, bf16[32,64,256]{2,0,1:T(8,128)(2,1)S(1)} %convolution_convert_fusion.1, f32[32]{0:T(128)S(1)} %fusion.19, pred[32,32]{1,0:T(8,128)(4,1)S(1)} %iota_compare_fusion), kind=kOutput, calls=%fused_computation.8 | convolution fusion | flops 202375168 | bytes 2884736 | tf_op jit(solution)/shard_map/plr,prc->plc/dot_general | solution.py:66
  (5 shorter events, 0.0 us)
Async XLA Ops:
  6.5 47.7 %all-gather.2.cloned.1.call-start = ((), (), s32[]{:S(2)}) async-start(), calls=%async_computation.2 | async-start | bytes 2621440 | tf_op jit(solution)/shard_map/all_gather | solution.py:50
  7.3 90.0 %all-reduce.2.cloned.1.call-start = ((), (), s32[]{:S(2)}) async-start(), calls=%async_computation.3 | async-start | bytes 1048576 | tf_op jit(solution)/shard_map/psum | solution.py:65
  54.2 4.1 %copy-start.1 = (bf16[1024,2048]{1,0:T(8,128)(2,1)S(1)}, bf16[1024,2048]{1,0:T(8,128)(2,1)}, u32[]{:S(2)}) copy-start(bf16[1024,2048]{1,0:T(8,128)(2,1)} %param.7) | copy-start | bytes 12582916
  64.2 81.0 %reduce-scatter.2.cloned.1.call-start = ((), (), s32[]{:S(2)}) async-start(), calls=%async_computation.1 | async-start | bytes 5242880 | tf_op jit(solution)/shard_map/reduce_scatter | solution.py:46
  74.2 0.7 copy-start.2
  74.2 0.8 copy-start.3
  74.2 0.9 copy-start
Sparse Core Ops, SparseCore 0:
  8.9 45.2 all-gather.1
  64.3 32.8 all-reduce.1
  99.8 45.4 reduce-scatter.1
where the time goes:
time: 157 us; the launch traced here: 155 us
  waiting for transfers between devices  104 us (66%)
  matrix products  23.7 us (15%)
  between operations  13.2 us (8%)
  blocking collectives  11.3 us (7%)
  local copies, waits for them, and re-layouts  1.59 us (1%)
    reduce_scatter x1, waiting for transfers between devices, on_device(): lax.psum_scatter(partial_value, 'narrow', scatter_dimension=1, tiled=True)  48 us
    all_gather x1, waiting for transfers between devices, on_device(): lax.all_gather(adapter_down_factors, 'wide', axis=0, tiled=True)  46.1 us
    all_gather x1, blocking collectives, on_device(): lax.all_gather(adapter_up_factors, 'wide', axis=0, tiled=True)  11.3 us
    dot_general x1, matrix products, on_device(): jnp.dot(tokens, value_weight, preferred_element_type=jnp.float32)  9.88 us
    psum x1, waiting for transfers between devices, on_device(): shrunk = lax.psum(shrunk, 'narrow')  8.99 us
    dot_general x1, matrix products, on_device(): jnp.einsum('pld,pdr->plr', prompt_rows, down_add, preferred_element_type=...  5.86 us
    dot_general x1, matrix products, on_device(): jnp.einsum('pj,jkr->pkr', picker, pieces[0], preferred_element_type=jnp.f...  4.12 us
    dot_general x1, matrix products, on_device(): jnp.einsum('plr,prc->plc', shrunk, up_add.astype(jnp.float32), precision=...  3.4 us
  transfers between devices with their start and end apart: 3, of which 3 were waited for; matrix products, arithmetic and copies ran while one was open for 8% of the time, Pallas kernels for 0%

commit v1 on v0

v1 whole, which is shorter than its diff:
```python
import functools

import jax
import jax.numpy as jnp
from jax import lax
from jax.experimental import pallas as pl
from jax.experimental.pallas import tpu as pltpu
from jax.sharding import PartitionSpec as P

LEN = 32
CHUNKS = 2
VMEM = pltpu.VMEM
F32 = jnp.float32
BF16 = jnp.bfloat16


def whole_block(array_memory=VMEM):
    return pl.BlockSpec(memory_space=array_memory)


def pack_kernel(wide_count, per_device, place_ref, choice_ref, mask_ref, down_ref, up_ref, *messages):
    owner_portion, rank, features = down_ref.shape
    rows = rank // CHUNKS
    me = place_ref[0]
    choice = choice_ref[...]
    prompt = lax.broadcasted_iota(jnp.int32, choice.shape, 1)
    local = choice - me * owner_portion
    wanted = (mask_ref[...] == 1) & (local >= 0) & (local < owner_portion)
    top = jnp.float32(2.0**24)
    key = jnp.where(wanted, (prompt * owner_portion + local).astype(F32), top)
    for shift in range(wide_count):
        reader = lax.rem(me + shift, wide_count)
        low = reader * per_device
        inside = (prompt >= low) & (prompt < low + per_device)
        first = jnp.min(jnp.where(inside, key, top))
        found = jnp.where(first < top, first, 0.0).astype(jnp.int32)
        adapter = lax.rem(found, owner_portion)
        for chunk in range(CHUNKS):
            out = messages[shift * CHUNKS + chunk]
            out[:, :features] = down_ref[adapter, pl.ds(chunk * rows, rows), :]
            out[:, features:] = up_ref[adapter, pl.ds(chunk * rows, rows), :]


def pack_messages(place, choice, mask, down, up, wide_count, per_device):
    rank, features = down.shape[1:]
    columns = up.shape[2]
    message = jax.ShapeDtypeStruct((rank // CHUNKS, features + columns), BF16)
    count = wide_count * CHUNKS
    out = pl.pallas_call(
        functools.partial(pack_kernel, wide_count, per_device),
        out_shape=[message] * count,
        in_specs=[whole_block(pltpu.SMEM)] + [whole_block()] * 4,
        out_specs=[whole_block()] * count,
        compiler_params=pltpu.CompilerParams(vmem_limit_bytes=24 * 2**20),
        cost_estimate=pl.CostEstimate(flops=0, bytes_accessed=2 * 2**20, transcendentals=0),
        name="pack_messages",
    )(place, choice, mask, down, up)
    return [out[shift * CHUNKS : (shift + 1) * CHUNKS] for shift in range(wide_count)]


def pair_kernel(order_ref, tokens_ref, first_ref, second_ref, send_ref, keep_ref):
    rows = tokens_ref[...]
    send_ref[...] = jnp.dot(rows, first_ref[...], preferred_element_type=F32)
    keep_ref[...] = jnp.dot(rows, second_ref[...], preferred_element_type=F32)


def matmul_pair(tokens, weight, order, columns, name):
    row_total, features = tokens.shape
    block = 256
    out = jax.ShapeDtypeStruct((row_total, columns), F32)
    out_spec = pl.BlockSpec((block, columns), lambda r, order: (r, 0))
    return pl.pallas_call(
        pair_kernel,
        out_shape=[out, out],
        grid_spec=pltpu.PrefetchScalarGridSpec(
            num_scalar_prefetch=1,
            grid=(row_total // block,),
            in_specs=[
                pl.BlockSpec((block, features), lambda r, order: (r, 0)),
                pl.BlockSpec((features, columns), lambda r, order: (0, order[0])),
                pl.BlockSpec((features, columns), lambda r, order: (0, order[1])),
            ],
            out_specs=[out_spec, out_spec],
        ),
        compiler_params=pltpu.CompilerParams(vmem_limit_bytes=24 * 2**20),
        cost_estimate=pl.CostEstimate(
            flops=4 * row_total * features * columns,
            bytes_accessed=row_total * features * 2 + features * columns * 4 + row_total * columns * 8,
            transcendentals=0,
        ),
        name=name,
    )(order, tokens, weight, weight)


def shrink_kernel(tokens_ref, chosen_ref, *refs):
    messages, out_ref, stacked = refs[:-2], refs[-2], refs[-1]
    rows = out_ref.shape[0]
    features = tokens_ref.shape[1]

    @pl.when(pl.program_id(0) == 0)
    def _():
        for at, message in enumerate(messages):
            stacked[pl.ds(at * rows, rows), :] = message[:, :features]

    sums = lax.dot_general(
        stacked[...], tokens_ref[...], (((1,), (1,)), ((), ())), preferred_element_type=F32
    )
    total = None
    for at in range(len(messages)):
        term = jnp.where(chosen_ref[pl.ds(at, 1), :] > 0, sums[at * rows : (at + 1) * rows, :], 0.0)
        total = term if total is None else total + term
    out_ref[...] = total


def shrink(tokens, chosen, messages, columns):
    row_total, features = tokens.shape
    count = len(messages)
    rows = messages[0].shape[0]
    block = 256
    return pl.pallas_call(
        shrink_kernel,
        out_shape=jax.ShapeDtypeStruct((rows, row_total), F32),
        grid=(row_total // block,),
        in_specs=[
            pl.BlockSpec((block, features), lambda r: (r, 0)),
            pl.BlockSpec((count, block), lambda r: (0, r)),
        ]
        + [pl.BlockSpec((rows, features + columns), lambda r: (0, 0))] * count,
        out_specs=pl.BlockSpec((rows, block), lambda r: (0, r)),
        scratch_shapes=[VMEM((count * rows, features), BF16)],
        compiler_params=pltpu.CompilerParams(vmem_limit_bytes=32 * 2**20),
        cost_estimate=pl.CostEstimate(
            flops=2 * row_total * features * count * rows,
            bytes_accessed=row_total * features * 2 + count * rows * (features + columns) * 2,
            transcendentals=0,
        ),
        name="shrink",
    )(tokens, chosen, *messages)


def finish_kernel(base_count, shrunk_counts, count, features, length_ref, chosen_ref, *refs):
    refs = list(refs)
    factors = refs[len(refs) - len(shrunk_counts) :]
    out_ref = refs[len(refs) - len(shrunk_counts) - 1]
    bases = [refs.pop(0) for _ in range(base_count)]
    total = bases[0][...]
    for base in bases[1:]:
        total = total + base[...]
    per_block = out_ref.shape[0] // LEN
    for terms, stacked in zip(shrunk_counts, factors):
        parts = [refs.pop(0) for _ in range(terms)]
        messages = [refs.pop(0) for _ in range(count)]
        rows = messages[0].shape[0]
        half = count * rows

        @pl.when(pl.program_id(0) == 0)
        def _(messages=messages, rows=rows, half=half, stacked=stacked):
            for at, message in enumerate(messages):
                factor = message[:, features:]
                stacked[pl.ds(at * rows, rows), :] = factor
                stacked[pl.ds(half + at * rows, rows), :] = factor

        shrunk = parts[0][...]
        for part in parts[1:]:
            shrunk = shrunk + part[...]
        spread = jnp.concatenate(
            [jnp.where(chosen_ref[pl.ds(at, 1), :] > 0, shrunk, 0.0) for at in range(count)], axis=0
        )
        high = spread.astype(BF16)
        low = (spread - high.astype(F32)).astype(BF16)
        both = jnp.concatenate([high, low], axis=0)
        total = total + lax.dot_general(
            both, stacked[...], (((0,), (0,)), ((), ())), preferred_element_type=F32
        )
    position = lax.broadcasted_iota(jnp.int32, (LEN, out_ref.shape[1]), 0)
    first = pl.program_id(0) * per_block
    for prompt in range(per_block):
        piece = total[prompt * LEN : (prompt + 1) * LEN, :]
        live = position < length_ref[first + prompt]
        out_ref[pl.ds(prompt * LEN, LEN), :] = jnp.where(live, piece, 0.0).astype(out_ref.dtype)


def finish(lengths, chosen, bases, shrunk, messages, features, out_dtype=BF16):
    row_total, columns = bases[0].shape
    count = len(messages[0])
    rows = messages[0][0].shape[0]
    block = 512
    wide_rows = pl.BlockSpec((block, columns), lambda r: (r, 0))
    in_specs = [whole_block(pltpu.SMEM), pl.BlockSpec((count, block), lambda r: (0, r))]
    in_specs += [wide_rows] * len(bases)
    operands = list(bases)
    for parts, sent in zip(shrunk, messages):
        in_specs += [pl.BlockSpec((rows, block), lambda r: (0, r))] * len(parts)
        in_specs += [pl.BlockSpec((rows, features + columns), lambda r: (0, 0))] * count
        operands += list(parts) + list(sent)
    return pl.pallas_call(
        functools.partial(finish_kernel, len(bases), [len(parts) for parts in shrunk], count, features),
        out_shape=jax.ShapeDtypeStruct((row_total, columns), out_dtype),
        grid=(row_total // block,),
        in_specs=in_specs,
        out_specs=wide_rows,
        scratch_shapes=[VMEM((2 * count * rows, columns), BF16)] * len(shrunk),
        compiler_params=pltpu.CompilerParams(vmem_limit_bytes=32 * 2**20),
        cost_estimate=pl.CostEstimate(
            flops=4 * row_total * columns * count * rows * len(shrunk),
            bytes_accessed=row_total * columns * 4 * (len(bases) + 1),
            transcendentals=0,
        ),
        name="finish",
    )(lengths, chosen, *operands)


def on_device(
    tokens,
    value_weight,
    adapter_down_factors,
    adapter_up_factors,
    adapter_choice_index,
    adapter_mask,
    prompt_token_length,
):
    wide_count = lax.axis_size("wide")
    narrow_count = lax.axis_size("narrow")
    wide_at = lax.axis_index("wide")
    narrow_at = lax.axis_index("narrow")
    owner_portion = adapter_down_factors.shape[0]
    row_total, features = tokens.shape
    per_device = row_total // LEN
    columns = adapter_up_factors.shape[2]

    place = jnp.full((1,), wide_at, jnp.int32)
    down = jnp.swapaxes(adapter_down_factors, 1, 2)
    sent = pack_messages(
        place,
        adapter_choice_index.reshape(1, -1),
        adapter_mask.reshape(1, -1),
        down,
        adapter_up_factors,
        wide_count,
        per_device,
    )
    held = [[sent[0][chunk]] for chunk in range(CHUNKS)]
    for chunk in range(CHUNKS):
        for shift in range(1, wide_count):
            ring = [(at, (at + shift) % wide_count) for at in range(wide_count)]
            held[chunk].append(lax.ppermute(sent[shift][chunk], "wide", ring))

    my_choice = lax.dynamic_slice_in_dim(adapter_choice_index, wide_at * per_device, per_device)
    my_mask = lax.dynamic_slice_in_dim(adapter_mask, wide_at * per_device, per_device)
    my_lengths = lax.dynamic_slice_in_dim(prompt_token_length, wide_at * per_device, per_device)
    owners = (wide_at - jnp.arange(wide_count, dtype=jnp.int32) + wide_count) % wide_count
    local = my_choice[None, :] - owners[:, None] * owner_portion
    matches = (my_mask[None, :] == 1) & (local >= 0) & (local < owner_portion)
    order = jnp.arange(per_device, dtype=jnp.int32)[None, :]
    first = jnp.min(
        jnp.where(matches, order * owner_portion + local, per_device * owner_portion), axis=1
    )
    granted = first % owner_portion
    chosen_prompt = (matches & (local == granted[:, None])).astype(F32)
    chosen = jnp.repeat(chosen_prompt, LEN, axis=1)

    if narrow_count == 4:
        core = [(at, at ^ 1) for at in range(4)]
        across = [(at, at ^ 2) for at in range(4)]
        other_chip, other_core = narrow_at ^ 2, narrow_at ^ 1
        far = jnp.stack([other_chip ^ 1, other_chip]).astype(jnp.int32)
        near = jnp.stack([other_core, narrow_at]).astype(jnp.int32)
        far_send, far_keep = matmul_pair(tokens, value_weight, far, columns, "far_columns")
        far_sum = far_keep + lax.ppermute(far_send, "narrow", core)
        crossed = lax.ppermute(far_sum, "narrow", across)
        near_send, near_keep = matmul_pair(tokens, value_weight, near, columns, "near_columns")
        bases = [near_keep, lax.ppermute(near_send, "narrow", core), crossed]
    else:
        partial_value = jnp.dot(tokens, value_weight, preferred_element_type=F32)
        bases = [lax.psum_scatter(partial_value, "narrow", scatter_dimension=1, tiled=True)]

    shrunk = []
    for chunk in range(CHUNKS):
        part = shrink(tokens, chosen, held[chunk], columns)
        if narrow_count == 4:
            part = part + lax.ppermute(part, "narrow", core)
            shrunk.append([part, lax.ppermute(part, "narrow", across)])
        else:
            shrunk.append([lax.psum(part, "narrow")])
    return finish(my_lengths, chosen, bases, shrunk, held, features)


def solution(mesh):
    placed = (
        P(("groups", "wide"), "narrow"),
        P("narrow", None),
        P(("groups", "wide"), "narrow", None),
        P(("groups", "wide"), None, "narrow"),
        P("groups"),
        P("groups"),
        P("groups"),
    )
    return jax.shard_map(
        on_device,
        mesh=mesh,
        in_specs=placed,
        out_specs=P(("groups", "wide"), "narrow"),
        check_vma=False,
    )
```

time: 157 us -> 67.8 us (0.43)
  the two profiles are of different devices: /device:TPU:9 before, /device:TPU:0 now
where the time goes in v1:
time: 67.8 us; the launch traced here: 67.3 us
  starting transfers between devices  21.4 us (32%)
  Pallas kernels  19.5 us (29%)
  local copies, waits for them, and re-layouts  12.3 us (18%)
  waiting for transfers between devices  11.1 us (16%)
  other arithmetic  2.89 us (4%)
    ppermute x6, starting transfers between devices, on_device(): held[chunk].append(lax.ppermute(sent[shift][chunk], 'wide', ring))  16.4 us
    unnamed x26, local copies, waits for them, and re-layouts  12 us
    pallas_call x2, Pallas kernels, matmul_pair(): pl.pallas_call(pair_kernel, out_shape=[out, out], grid_spec=pltpu.Prefetc...  8.86 us
    pallas_call x2, Pallas kernels, shrink(): pl.pallas_call(shrink_kernel, out_shape=jax.ShapeDtypeStruct((rows, row_t...  6.22 us
    ppermute x2, waiting for transfers between devices, on_device(): shrunk.append([part, lax.ppermute(part, 'narrow', across)])  5.81 us
    ppermute x6, waiting for transfers between devices, on_device(): held[chunk].append(lax.ppermute(sent[shift][chunk], 'wide', ring))  5.26 us
    pallas_call x1, Pallas kernels, finish(): pl.pallas_call(functools.partial(finish_kernel, len(bases), [len(parts) f...  3.53 us
    ppermute x2, starting transfers between devices, on_device(): shrunk.append([part, lax.ppermute(part, 'narrow', across)])  2.84 us
  transfers between devices with their start and end apart: 13, of which 5 were waited for; matrix products, arithmetic and copies ran while one was open for 5% of the time, Pallas kernels for 17%

profile of v1, /device:TPU:0, one launch (start us, length us, event | category | flops | bytes accessed | tf_op | source)
XLA Modules:
  0.0 67.3 jit_solution(16258669700264192080)
XLA Ops:
  0.0 0.1 pad_add_fusion.1.order_ref
  0.1 0.0 copy-start
  0.1 2.2 %copy-done = bf16[1024,2048]{1,0:T(8,128)(2,1)S(1)} copy-done((bf16[1024,2048]{1,0:T(8,128)(2,1)S(1)}, bf16[1024,2048]{1,0:T(8,128)(2,1)}, u32[]{:S(2)}) %copy-start) | copy-done | bytes 4194328
  2.3 0.0 copy-start.3
  2.3 2.2 %copy-done.3 = bf16[2048,1024]{1,0:T(8,128)(2,1)S(1)} copy-done((bf16[2048,1024]{1,0:T(8,128)(2,1)S(1)}, bf16[2048,1024]{1,0:T(8,128)(2,1)}, u32[]{:S(2)}) %copy-start.3) | copy-done | bytes 4194328
  4.5 4.4 %far_columns.1 = (f32[1024,256]{1,0:T(8,128)}, f32[1024,256]{1,0:T(8,128)S(1)}) custom-call(s32[2]{0:T(128)S(1)} %pad_add_fusion.1.order_ref, bf16[1024,2048]{1,0:T(8,128)(2,1)S(1)} %copy-done, bf16[2048,1024]{1,0:T(8,128)(2,1)S(1)} %copy-done.3, bf16[2048,1024]{1,0:T(8,128)(2,1)S(1)} %copy-done.3), custom_call_target="tpu_custom_call" | custom-call | flops 2147483648 | bytes 8388608 | tf_op jit(solution)/shard_map/far_columns/pallas_call | solution.py:72
  8.9 0.5 collective-permute-start.1
  9.3 0.1 pad_add_fusion.order_ref
  9.4 0.0 copy-start.1
  9.4 2.2 %copy-done.1 = bf16[1024,2048]{1,0:T(8,128)(2,1)S(1)} copy-done((bf16[1024,2048]{1,0:T(8,128)(2,1)S(1)}, bf16[1024,2048]{1,0:T(8,128)(2,1)}, u32[]{:S(2)}) %copy-start.1) | copy-done | bytes 4194328
  11.6 0.0 copy-start.4
  11.6 2.2 %copy-done.4 = bf16[2048,1024]{1,0:T(8,128)(2,1)S(1)} copy-done((bf16[2048,1024]{1,0:T(8,128)(2,1)S(1)}, bf16[2048,1024]{1,0:T(8,128)(2,1)}, u32[]{:S(2)}) %copy-start.4) | copy-done | bytes 4194328
  13.8 0.0 copy-start.6
  13.8 0.0 copy-start.7
  13.8 0.0 copy-start.8
  13.8 4.4 %near_columns.1 = (f32[1024,256]{1,0:T(8,128)}, f32[1024,256]{1,0:T(8,128)S(1)}) custom-call(s32[2]{0:T(128)S(1)} %pad_add_fusion.order_ref, bf16[1024,2048]{1,0:T(8,128)(2,1)S(1)} %copy-done.1, bf16[2048,1024]{1,0:T(8,128)(2,1)S(1)} %copy-done.4, bf16[2048,1024]{1,0:T(8,128)(2,1)S(1)} %copy-done.4), custom_call_target="tpu_custom_call" | custom-call | flops 2147483648 | bytes 8388608 | tf_op jit(solution)/shard_map/near_columns/pallas_call | solution.py:72
  18.2 0.1 collective-permute-start
  18.3 0.0 copy-done.6
  18.3 0.0 copy-done.7
  18.3 0.0 copy-done.8
  18.3 0.0 copy-start.5
  18.3 1.0 %copy-done.5 = bf16[2,2048,64]{1,2,0:T(8,128)(2,1)S(1)} copy-done((bf16[2,2048,64]{1,2,0:T(8,128)(2,1)S(1)}, bf16[2,2048,64]{1,2,0:T(8,128)(2,1)}, u32[]{:S(2)}) %copy-start.5) | copy-done | bytes 524312
  19.3 0.9 %pack_messages.1 = (bf16[32,2304]{1,0:T(8,128)(2,1)S(1)}, bf16[32,2304]{1,0:T(8,128)(2,1)S(1)}, bf16[32,2304]{1,0:T(8,128)(2,1)}, bf16[32,2304]{1,0:T(8,128)(2,1...) custom-call(s32[1]{0:T(128)} %bitcast.4.place_ref, ...), custom_call_target="tpu_custom_call" | custom-call | bytes 2097152 | tf_op jit(solution)/shard_map/pack_messages/pallas_call | solution.py:49
  20.3 3.0 %collective-permute-start.3 = (bf16[32,2304]{1,0:T(8,128)(2,1)}, bf16[32,2304]{1,0:T(8,128)(2,1)}, u32[]{:S(2)}, u32[]{:S(2)}) collective-permute-start(bf16[32,2304]{1,0:T(8,128)(2,1)} %get-tuple-element.22), channel_id=1, source_target_pairs={{0,4},{4,8},{8,12},{12,0},{1,5},{5,9},{9,13},{13,1},{2,6},{6,10},{... | collective-permute-start | bytes 442376 | tf_op jit(solution)/shard_map/ppermute | solution.py:246
  23.3 2.6 %collective-permute-start.4 = (bf16[32,2304]{1,0:T(8,128)(2,1)}, bf16[32,2304]{1,0:T(8,128)(2,1)}, u32[]{:S(2)}, u32[]{:S(2)}) collective-permute-start(bf16[32,2304]{1,0:T(8,128)(2,1)} %get-tuple-element.23), channel_id=1, source_target_pairs={{0,8},{4,12},{8,0},{12,4},{1,9},{5,13},{9,1},{13,5},{2,10},{6,14},... | collective-permute-start | bytes 442376 | tf_op jit(solution)/shard_map/ppermute | solution.py:246
  25.9 1.3 %collective-permute-start.5 = (bf16[32,2304]{1,0:T(8,128)(2,1)}, bf16[32,2304]{1,0:T(8,128)(2,1)}, u32[]{:S(2)}, u32[]{:S(2)}) collective-permute-start(bf16[32,2304]{1,0:T(8,128)(2,1)} %get-tuple-element.24), channel_id=1, source_target_pairs={{0,12},{4,0},{8,4},{12,8},{1,13},{5,1},{9,5},{13,9},{2,14},{6,2},{... | collective-permute-start | bytes 442376 | tf_op jit(solution)/shard_map/ppermute | solution.py:246
  27.3 0.0 collective-permute-done.1
  27.3 2.3 %add.53 = f32[1024,256]{1,0:T(8,128)} add(f32[1024,256]{1,0:T(8,128)S(1)} %get-tuple-element.19, f32[1024,256]{1,0:T(8,128)} %collective-permute-done.1) | non-fusion elementwise | flops 262144 | bytes 3145728 | tf_op jit(solution)/shard_map/add | solution.py:269
  29.6 0.0 copy-done.9
  29.6 1.5 %collective-permute-start.2 = (f32[1024,256]{1,0:T(8,128)}, f32[1024,256]{1,0:T(8,128)S(1)}, u32[]{:S(2)}, u32[]{:S(2)}) collective-permute-start(f32[1024,256]{1,0:T(8,128)} %add.53), channel_id=1, source_target_pairs={{0,2},{1,3},{2,0},{3,1},{4,6},{5,7},{6,4},{7,5},{8,10},{9,11},{10,... | collective-permute-start | bytes 3145736 | tf_op jit(solution)/shard_map/ppermute | solution.py:270
  31.1 0.0 copy-done.10
  31.1 0.0 copy-done.11
  31.1 0.1 dynamic_slice.11
  31.2 0.1 dynamic-slice_compare_fusion
  31.3 0.2 fusion.1
  31.5 0.0 collective-permute-done.3.refs_1_.refs_6_
  31.5 4.1 %collective-permute-start.8 = (bf16[32,2304]{1,0:T(8,128)(2,1)}, bf16[32,2304]{1,0:T(8,128)(2,1)}, u32[]{:S(2)}, u32[]{:S(2)}) collective-permute-start(bf16[32,2304]{1,0:T(8,128)(2,1)} %copy-done.11), channel_id=1, source_target_pairs={{0,4},{4,8},{8,12},{12,0},{1,5},{5,9},{9,13},{13,1},{2,6},{6,10},{... | collective-permute-start | bytes 442376 | tf_op jit(solution)/shard_map/ppermute | solution.py:246
  35.6 1.2 %collective-permute-done.4.refs_2_.refs_7_ = bf16[32,2304]{1,0:T(8,128)(2,1)} collective-permute-done((bf16[32,2304]{1,0:T(8,128)(2,1)}, bf16[32,2304]{1,0:T(8,128)(2,1)}, u32[]{:S(2)}, u32[]{:S(2)}) %collective-permute-start.4) | collective-permute-done | bytes 147488 | tf_op jit(solution)/shard_map/ppermute | solution.py:246
  36.7 1.0 %collective-permute-start.9 = (bf16[32,2304]{1,0:T(8,128)(2,1)}, bf16[32,2304]{1,0:T(8,128)(2,1)}, u32[]{:S(2)}, u32[]{:S(2)}) collective-permute-start(bf16[32,2304]{1,0:T(8,128)(2,1)} %copy-done.10), channel_id=1, source_target_pairs={{0,8},{4,12},{8,0},{12,4},{1,9},{5,13},{9,1},{13,5},{2,10},{6,14},... | collective-permute-start | bytes 442376 | tf_op jit(solution)/shard_map/ppermute | solution.py:246
  37.7 0.0 collective-permute-done.5.refs_3_.refs_8_
  37.7 4.3 %collective-permute-start.10 = (bf16[32,2304]{1,0:T(8,128)(2,1)}, bf16[32,2304]{1,0:T(8,128)(2,1)}, u32[]{:S(2)}, u32[]{:S(2)}) collective-permute-start(bf16[32,2304]{1,0:T(8,128)(2,1)} %copy-done.9), channel_id=1, source_target_pairs={{0,12},{4,0},{8,4},{12,8},{1,13},{5,1},{9,5},{13,9},{2,14},{6,2},{... | collective-permute-start | bytes 442376 | tf_op jit(solution)/shard_map/ppermute | solution.py:246
  42.1 0.1 fusion.5
  42.1 0.1 broadcast_in_dim.16
  42.2 0.1 reshape.48.chosen_ref
  42.3 0.0 copy-start.2
  42.3 2.2 %copy-done.2 = bf16[1024,2048]{1,0:T(8,128)(2,1)S(1)} copy-done((bf16[1024,2048]{1,0:T(8,128)(2,1)S(1)}, bf16[1024,2048]{1,0:T(8,128)(2,1)}, u32[]{:S(2)}) %copy-start.2) | copy-done | bytes 4194328
  44.5 3.1 %shrink.2 = f32[32,1024]{1,0:T(8,128)S(1)} custom-call(bf16[1024,2048]{1,0:T(8,128)(2,1)S(1)} %copy-done.2, f32[4,1024]{1,0:T(4,128)S(1)} %reshape.48.chosen_ref, bf16[32,2304]{1,0:T(8,128)(2,1)S(1)} %get-tuple-element.21.refs_0_.refs_5_, bf16[32,2304]{1,0:T(8,128)(2,1)} %collective-permute-done.3.refs_1_.refs_6_, ...), custom_call_target="tpu_custom_call" | custom-call | flops 536870912 | bytes 4784128 | tf_op jit(solution)/shard_map/shrink/pallas_call | solution.py:120
  47.7 0.0 collective-permute-done.8.refs_1_.refs_12_
  47.7 0.1 collective-permute-start.6
  47.7 1.1 %collective-permute-done.9.refs_2_.refs_13_ = bf16[32,2304]{1,0:T(8,128)(2,1)} collective-permute-done((bf16[32,2304]{1,0:T(8,128)(2,1)}, bf16[32,2304]{1,0:T(8,128)(2,1)}, u32[]{:S(2)}, u32[]{:S(2)}) %collective-permute-start.9) | collective-permute-done | bytes 147488 | tf_op jit(solution)/shard_map/ppermute | solution.py:246
  48.8 3.0 %collective-permute-done.10.refs_3_.refs_14_ = bf16[32,2304]{1,0:T(8,128)(2,1)} collective-permute-done((bf16[32,2304]{1,0:T(8,128)(2,1)}, bf16[32,2304]{1,0:T(8,128)(2,1)}, u32[]{:S(2)}, u32[]{:S(2)}) %collective-permute-start.10) | collective-permute-done | bytes 147488 | tf_op jit(solution)/shard_map/ppermute | solution.py:246
  51.8 3.1 %shrink.3 = f32[32,1024]{1,0:T(8,128)S(1)} custom-call(bf16[1024,2048]{1,0:T(8,128)(2,1)S(1)} %copy-done.2, f32[4,1024]{1,0:T(4,128)S(1)} %reshape.48.chosen_ref, bf16[32,2304]{1,0:T(8,128)(2,1)S(1)} %get-tuple-element.25.refs_0_.refs_11_, bf16[32,2304]{1,0:T(8,128)(2,1)} %collective-permute-done.8.refs_1_.refs_12_, ...), custom_call_target="tpu_custom_call" | custom-call | flops 536870912 | bytes 4784128 | tf_op jit(solution)/shard_map/shrink/pallas_call | solution.py:120
  54.9 0.1 collective-permute-start.11
  55.0 0.0 collective-permute-done.6
  55.1 1.6 %collective-permute-start.7 = (f32[32,1024]{1,0:T(8,128)S(1)}, f32[32,1024]{1,0:T(8,128)S(1)}, u32[]{:S(2)}, u32[]{:S(2)}) collective-permute-start(f32[32,1024]{1,0:T(8,128)S(1)} %add.54.refs_3_), channel_id=1, source_target_pairs={{0,2},{1,3},{2,0},{3,1},{4,6},{5,7},{6,4},{7,5},{8,10},{9,11},{10,... | collective-permute-start | bytes 393224 | tf_op jit(solution)/shard_map/ppermute | solution.py:282
  56.6 0.0 collective-permute-done.11
  56.6 1.3 %collective-permute-start.12 = (f32[32,1024]{1,0:T(8,128)S(1)}, f32[32,1024]{1,0:T(8,128)S(1)}, u32[]{:S(2)}, u32[]{:S(2)}) collective-permute-start(f32[32,1024]{1,0:T(8,128)S(1)} %add.55.refs_9_), channel_id=1, source_target_pairs={{0,2},{1,3},{2,0},{3,1},{4,6},{5,7},{6,4},{7,5},{8,10},{9,11},{10,... | collective-permute-start | bytes 393224 | tf_op jit(solution)/shard_map/ppermute | solution.py:282
  57.9 0.0 copy-done.12
  57.9 0.1 dynamic_slice.9.length_ref
  58.0 3.4 %collective-permute-done.7.refs_4_ = f32[32,1024]{1,0:T(8,128)S(1)} collective-permute-done((f32[32,1024]{1,0:T(8,128)S(1)}, f32[32,1024]{1,0:T(8,128)S(1)}, u32[]{:S(2)}, u32[]{:S(2)}) %collective-permute-start.7) | collective-permute-done | bytes 131104 | tf_op jit(solution)/shard_map/ppermute | solution.py:282
  61.4 2.4 %collective-permute-done.12.refs_10_ = f32[32,1024]{1,0:T(8,128)S(1)} collective-permute-done((f32[32,1024]{1,0:T(8,128)S(1)}, f32[32,1024]{1,0:T(8,128)S(1)}, u32[]{:S(2)}, u32[]{:S(2)}) %collective-permute-start.12) | collective-permute-done | bytes 131104 | tf_op jit(solution)/shard_map/ppermute | solution.py:282
  63.8 0.0 collective-permute-done.refs_1_
  63.8 0.0 collective-permute-done.2.refs_2_
  63.8 3.5 %finish.1 = bf16[1024,256]{1,0:T(8,128)(2,1)} custom-call(s32[32]{0:T(128)S(1)} %dynamic_slice.9.length_ref, f32[4,1024]{1,0:T(4,128)S(1)} %reshape.48.chosen_ref, f32[1024,256]{1,0:T(8,128)S(1)} %get-tuple-element.17.refs_0_, f32[1024,256]{1,0:T(8,128)S(1)} %collective-permute-done.refs_1_, f32[1024,256]{1,0:T(8,128)S(1)} %collective-permute-done.2.refs_2_, ...), custom_call_target="tpu_custom_call" | custom-call | flops 268435456 | bytes 4194304 | tf_op jit(solution)/shard_map/finish/pallas_call | solution.py:196
  (9 shorter events, 0.1 us)
Async XLA Ops:
  0.1 2.2 %copy-start = (bf16[1024,2048]{1,0:T(8,128)(2,1)S(1)}, bf16[1024,2048]{1,0:T(8,128)(2,1)}, u32[]{:S(2)}) copy-start(bf16[1024,2048]{1,0:T(8,128)(2,1)} %tokens_ref.7) | copy-start | bytes 12582916
  2.3 2.2 %copy-start.3 = (bf16[2048,1024]{1,0:T(8,128)(2,1)S(1)}, bf16[2048,1024]{1,0:T(8,128)(2,1)}, u32[]{:S(2)}) copy-start(bf16[2048,1024]{1,0:T(8,128)(2,1)} %second_ref.3) | copy-start | bytes 12582916
  8.9 18.4 %collective-permute-start.1 = (f32[1024,256]{1,0:T(8,128)}, f32[1024,256]{1,0:T(8,128)}, u32[]{:S(2)}, u32[]{:S(2)}) collective-permute-start(f32[1024,256]{1,0:T(8,128)} %get-tuple-element.20), channel_id=1, source_target_pairs={{0,1},{1,0},{2,3},{3,2},{4,5},{5,4},{6,7},{7,6},{8,9},{9,8},{10,11... | collective-permute-start | bytes 3145736 | tf_op jit(solution)/shard_map/ppermute | solution.py:269
  9.4 2.2 %copy-start.1 = (bf16[1024,2048]{1,0:T(8,128)(2,1)S(1)}, bf16[1024,2048]{1,0:T(8,128)(2,1)}, u32[]{:S(2)}) copy-start(bf16[1024,2048]{1,0:T(8,128)(2,1)} %tokens_ref.7) | copy-start | bytes 12582916
  11.6 2.2 %copy-start.4 = (bf16[2048,1024]{1,0:T(8,128)(2,1)S(1)}, bf16[2048,1024]{1,0:T(8,128)(2,1)}, u32[]{:S(2)}) copy-start(bf16[2048,1024]{1,0:T(8,128)(2,1)} %second_ref.3) | copy-start | bytes 12582916
  13.8 4.5 %copy-start.6 = (bf16[2,64,256]{2,1,0:T(8,128)(2,1)S(1)}, bf16[2,64,256]{2,1,0:T(8,128)(2,1)}, u32[]{:S(2)}) copy-start(bf16[2,64,256]{2,1,0:T(8,128)(2,1)} %up_ref.1) | copy-start | bytes 196612
  13.8 4.5 %copy-start.7 = (s32[128]{0:T(128)S(1)}, s32[128]{0:T(128)}, u32[]{:S(2)}) copy-start(s32[128]{0:T(128)} %param.11) | copy-start | bytes 1540
  13.8 4.5 %copy-start.8 = (s32[128]{0:T(128)S(1)}, s32[128]{0:T(128)}, u32[]{:S(2)}) copy-start(s32[128]{0:T(128)} %param.12) | copy-start | bytes 1540
  18.2 45.6 %collective-permute-start = (f32[1024,256]{1,0:T(8,128)}, f32[1024,256]{1,0:T(8,128)S(1)}, u32[]{:S(2)}, u32[]{:S(2)}) collective-permute-start(f32[1024,256]{1,0:T(8,128)} %get-tuple-element.18), channel_id=1, source_target_pairs={{0,1},{1,0},{2,3},{3,2},{4,5},{5,4},{6,7},{7,6},{8,9},{9,8},{10,11... | collective-permute-start | bytes 3145736 | tf_op jit(solution)/shard_map/ppermute | solution.py:272
  18.3 1.0 %copy-start.5 = (bf16[2,2048,64]{1,2,0:T(8,128)(2,1)S(1)}, bf16[2,2048,64]{1,2,0:T(8,128)(2,1)}, u32[]{:S(2)}) copy-start(bf16[2,2048,64]{1,2,0:T(8,128)(2,1)} %param.9) | copy-start | bytes 1572868
  20.3 9.3 %copy-start.9 = (bf16[32,2304]{1,0:T(8,128)(2,1)}, bf16[32,2304]{1,0:T(8,128)(2,1)S(1)}, u32[]{:S(2)}) copy-start(bf16[32,2304]{1,0:T(8,128)(2,1)S(1)} %get-tuple-element.28) | copy-start | bytes 442372
  20.3 10.8 %copy-start.10 = (bf16[32,2304]{1,0:T(8,128)(2,1)}, bf16[32,2304]{1,0:T(8,128)(2,1)S(1)}, u32[]{:S(2)}) copy-start(bf16[32,2304]{1,0:T(8,128)(2,1)S(1)} %get-tuple-element.27) | copy-start | bytes 442372
  20.3 10.8 %copy-start.11 = (bf16[32,2304]{1,0:T(8,128)(2,1)}, bf16[32,2304]{1,0:T(8,128)(2,1)S(1)}, u32[]{:S(2)}) copy-start(bf16[32,2304]{1,0:T(8,128)(2,1)S(1)} %get-tuple-element.26) | copy-start | bytes 442372
  20.3 11.2 %collective-permute-start.3 = (bf16[32,2304]{1,0:T(8,128)(2,1)}, bf16[32,2304]{1,0:T(8,128)(2,1)}, u32[]{:S(2)}, u32[]{:S(2)}) collective-permute-start(bf16[32,2304]{1,0:T(8,128)(2,1)} %get-tuple-element.22), channel_id=1, source_target_pairs={{0,4},{4,8},{8,12},{12,0},{1,5},{5,9},{9,13},{13,1},{2,6},{6,10},{... | collective-permute-start | bytes 442376 | tf_op jit(solution)/shard_map/ppermute | solution.py:246
  23.3 13.4 %collective-permute-start.4 = (bf16[32,2304]{1,0:T(8,128)(2,1)}, bf16[32,2304]{1,0:T(8,128)(2,1)}, u32[]{:S(2)}, u32[]{:S(2)}) collective-permute-start(bf16[32,2304]{1,0:T(8,128)(2,1)} %get-tuple-element.23), channel_id=1, source_target_pairs={{0,8},{4,12},{8,0},{12,4},{1,9},{5,13},{9,1},{13,5},{2,10},{6,14},... | collective-permute-start | bytes 442376 | tf_op jit(solution)/shard_map/ppermute | solution.py:246
  25.9 11.8 %collective-permute-start.5 = (bf16[32,2304]{1,0:T(8,128)(2,1)}, bf16[32,2304]{1,0:T(8,128)(2,1)}, u32[]{:S(2)}, u32[]{:S(2)}) collective-permute-start(bf16[32,2304]{1,0:T(8,128)(2,1)} %get-tuple-element.24), channel_id=1, source_target_pairs={{0,12},{4,0},{8,4},{12,8},{1,13},{5,1},{9,5},{13,9},{2,14},{6,2},{... | collective-permute-start | bytes 442376 | tf_op jit(solution)/shard_map/ppermute | solution.py:246
  29.6 34.2 %collective-permute-start.2 = (f32[1024,256]{1,0:T(8,128)}, f32[1024,256]{1,0:T(8,128)S(1)}, u32[]{:S(2)}, u32[]{:S(2)}) collective-permute-start(f32[1024,256]{1,0:T(8,128)} %add.53), channel_id=1, source_target_pairs={{0,2},{1,3},{2,0},{3,1},{4,6},{5,7},{6,4},{7,5},{8,10},{9,11},{10,... | collective-permute-start | bytes 3145736 | tf_op jit(solution)/shard_map/ppermute | solution.py:270
  31.5 16.2 %collective-permute-start.8 = (bf16[32,2304]{1,0:T(8,128)(2,1)}, bf16[32,2304]{1,0:T(8,128)(2,1)}, u32[]{:S(2)}, u32[]{:S(2)}) collective-permute-start(bf16[32,2304]{1,0:T(8,128)(2,1)} %copy-done.11), channel_id=1, source_target_pairs={{0,4},{4,8},{8,12},{12,0},{1,5},{5,9},{9,13},{13,1},{2,6},{6,10},{... | collective-permute-start | bytes 442376 | tf_op jit(solution)/shard_map/ppermute | solution.py:246
  36.7 12.0 %collective-permute-start.9 = (bf16[32,2304]{1,0:T(8,128)(2,1)}, bf16[32,2304]{1,0:T(8,128)(2,1)}, u32[]{:S(2)}, u32[]{:S(2)}) collective-permute-start(bf16[32,2304]{1,0:T(8,128)(2,1)} %copy-done.10), channel_id=1, source_target_pairs={{0,8},{4,12},{8,0},{12,4},{1,9},{5,13},{9,1},{13,5},{2,10},{6,14},... | collective-permute-start | bytes 442376 | tf_op jit(solution)/shard_map/ppermute | solution.py:246
  37.7 14.1 %collective-permute-start.10 = (bf16[32,2304]{1,0:T(8,128)(2,1)}, bf16[32,2304]{1,0:T(8,128)(2,1)}, u32[]{:S(2)}, u32[]{:S(2)}) collective-permute-start(bf16[32,2304]{1,0:T(8,128)(2,1)} %copy-done.9), channel_id=1, source_target_pairs={{0,12},{4,0},{8,4},{12,8},{1,13},{5,1},{9,5},{13,9},{2,14},{6,2},{... | collective-permute-start | bytes 442376 | tf_op jit(solution)/shard_map/ppermute | solution.py:246
  42.3 2.2 %copy-start.2 = (bf16[1024,2048]{1,0:T(8,128)(2,1)S(1)}, bf16[1024,2048]{1,0:T(8,128)(2,1)}, u32[]{:S(2)}) copy-start(bf16[1024,2048]{1,0:T(8,128)(2,1)} %tokens_ref.7) | copy-start | bytes 12582916
  44.5 13.4 %copy-start.12 = (s32[128]{0:T(128)S(1)}, s32[128]{0:T(128)}, u32[]{:S(2)}) copy-start(s32[128]{0:T(128)} %param.13) | copy-start | bytes 1540
  47.7 7.4 %collective-permute-start.6 = (f32[32,1024]{1,0:T(8,128)S(1)}, f32[32,1024]{1,0:T(8,128)S(1)}, u32[]{:S(2)}, u32[]{:S(2)}) collective-permute-start(f32[32,1024]{1,0:T(8,128)S(1)} %shrink.2), channel_id=1, source_target_pairs={{0,1},{1,0},{2,3},{3,2},{4,5},{5,4},{6,7},{7,6},{8,9},{9,8},{10,11... | collective-permute-start | bytes 393224 | tf_op jit(solution)/shard_map/ppermute | solution.py:281
  54.9 1.7 %collective-permute-start.11 = (f32[32,1024]{1,0:T(8,128)S(1)}, f32[32,1024]{1,0:T(8,128)S(1)}, u32[]{:S(2)}, u32[]{:S(2)}) collective-permute-start(f32[32,1024]{1,0:T(8,128)S(1)} %shrink.3), channel_id=1, source_target_pairs={{0,1},{1,0},{2,3},{3,2},{4,5},{5,4},{6,7},{7,6},{8,9},{9,8},{10,11... | collective-permute-start | bytes 393224 | tf_op jit(solution)/shard_map/ppermute | solution.py:281
  55.1 6.4 %collective-permute-start.7 = (f32[32,1024]{1,0:T(8,128)S(1)}, f32[32,1024]{1,0:T(8,128)S(1)}, u32[]{:S(2)}, u32[]{:S(2)}) collective-permute-start(f32[32,1024]{1,0:T(8,128)S(1)} %add.54.refs_3_), channel_id=1, source_target_pairs={{0,2},{1,3},{2,0},{3,1},{4,6},{5,7},{6,4},{7,5},{8,10},{9,11},{10,... | collective-permute-start | bytes 393224 | tf_op jit(solution)/shard_map/ppermute | solution.py:282
  56.6 7.2 %collective-permute-start.12 = (f32[32,1024]{1,0:T(8,128)S(1)}, f32[32,1024]{1,0:T(8,128)S(1)}, u32[]{:S(2)}, u32[]{:S(2)}) collective-permute-start(f32[32,1024]{1,0:T(8,128)S(1)} %add.55.refs_9_), channel_id=1, source_target_pairs={{0,2},{1,3},{2,0},{3,1},{4,6},{5,7},{6,4},{7,5},{8,10},{9,11},{10,... | collective-permute-start | bytes 393224 | tf_op jit(solution)/shard_map/ppermute | solution.py:282

commit v2 on v0

v2 whole, which is shorter than its diff:
```python
import functools

import jax
import jax.numpy as jnp
from jax import lax
from jax.experimental import pallas as pl
from jax.experimental.pallas import tpu as pltpu
from jax.sharding import PartitionSpec as P

LEN = 32
CHUNKS = 1
LIMIT = 20 * 2**20
VMEM = pltpu.VMEM
F32 = jnp.float32
BF16 = jnp.bfloat16
STEPS = 32767.0
SMALL = pl.CostEstimate(flops=1, bytes_accessed=1, transcendentals=0)


def whole_block(array_memory=VMEM):
    return pl.BlockSpec(memory_space=array_memory)


def in_hbm(array):
    return pltpu.with_memory_space_constraint(array, pltpu.HBM)


def half_columns(weight_ref, chip, half):
    return weight_ref.at[:, pl.ds(pl.multiple_of(chip * half, half), half)]


def first_kernel(wide_count, per_device, paired, *refs):
    message_count = wide_count * CHUNKS
    loads_in, refs = refs[:4], refs[4:]
    if paired:
        tokens_hbm, weight_hbm, *refs = refs
    messages, refs = refs[:message_count], refs[message_count:]
    if paired:
        sums, refs = refs[:4], refs[4:]
    choice_ref, mask_ref, down_ref, up_ref, load_sem, message_sem = refs[:6]
    owner_portion, rank, features = down_ref.shape
    columns = up_ref.shape[2]
    rows = rank // CHUNKS
    loads = [
        pltpu.make_async_copy(source, target, load_sem.at[at])
        for at, (source, target) in enumerate(zip(loads_in, refs[:4]))
    ]
    for copy in loads:
        copy.start()
    if paired:
        tokens_ref, weight_ref, token_sem, weight_sem = refs[6:]
        narrow_at = lax.axis_index("narrow")
        mine = lax.rem(narrow_at, 2)
        chips = ((narrow_at // 2) ^ 1, narrow_at // 2)
        weight_copies = [
            pltpu.make_async_copy(
                half_columns(weight_hbm, chip, 2 * columns), weight_ref.at[half], weight_sem.at[half]
            )
            for half, chip in enumerate(chips)
        ]
        blocks = token_sem.shape[0]
        block = tokens_hbm.shape[0] // blocks
        token_copies = [
            pltpu.make_async_copy(
                tokens_hbm.at[pl.ds(at * block, block), :],
                tokens_ref.at[pl.ds(at * block, block), :],
                token_sem.at[at],
            )
            for at in range(blocks)
        ]
        weight_copies[0].start()
        token_copies[0].start()
    loads[0].wait()
    loads[1].wait()
    me = lax.axis_index("wide")
    choice = choice_ref[...]
    prompt = lax.broadcasted_iota(jnp.int32, choice.shape, 1)
    local = choice - me * owner_portion
    wanted = (mask_ref[...] == 1) & (local >= 0) & (local < owner_portion)
    top = jnp.float32(2.0**24)
    key = jnp.where(wanted, (prompt * owner_portion + local).astype(F32), top)
    copies = []
    for shift in range(wide_count):
        reader = lax.rem(me + shift, wide_count)
        low = reader * per_device
        inside = (prompt >= low) & (prompt < low + per_device)
        first = jnp.min(jnp.where(inside, key, top))
        found = jnp.where(first < top, first, 0.0).astype(jnp.int32)
        adapter = lax.rem(found, owner_portion)
        for chunk in range(CHUNKS):
            at = shift * CHUNKS + chunk
            out = messages[at]
            span = pl.ds(chunk * rows, rows)
            copies.append(
                pltpu.make_async_copy(
                    down_ref.at[adapter, span, :], out.at[:, pl.ds(0, features)], message_sem.at[2 * at]
                )
            )
            copies.append(
                pltpu.make_async_copy(
                    up_ref.at[adapter, span, :],
                    out.at[:, pl.ds(features, columns)],
                    message_sem.at[2 * at + 1],
                )
            )
    loads[2].wait()
    loads[3].wait()
    for copy in copies:
        copy.start()
    if paired:
        token_copies[1].start()
        for half in range(2):
            weight_copies[half].wait()
            for at, copy in enumerate(token_copies):
                span = pl.ds(at * block, block)
                if half == 0:
                    copy.wait()
                    if at + 2 < blocks:
                        token_copies[at + 2].start()
                    if at + 2 == blocks:
                        weight_copies[1].start()
                for out_ref, core in ((sums[2 * half], 1 - mine), (sums[2 * half + 1], mine)):
                    low = pl.multiple_of(core * columns, columns)
                    out_ref[span, :] = jnp.dot(
                        tokens_ref[span, :],
                        weight_ref[half, :, pl.ds(low, columns)],
                        preferred_element_type=F32,
                    )
    for copy in copies:
        copy.wait()


def first_step(choice, mask, down, up, tokens, weight, wide_count, per_device, paired):
    rank, features = down.shape[1:]
    columns = up.shape[2]
    row_total = tokens.shape[0]
    count = wide_count * CHUNKS
    hbm = whole_block(pl.ANY)
    operands = [choice, mask, down, up]
    scratch = [VMEM(operand.shape, operand.dtype) for operand in operands]
    scratch += [pltpu.SemaphoreType.DMA((4,)), pltpu.SemaphoreType.DMA((2 * count,))]
    out_shape = [pltpu.HBM((rank // CHUNKS, features + columns), BF16)] * count
    out_specs = [hbm] * count
    if paired:
        operands += [tokens, weight]
        out_shape += [VMEM((row_total, columns), F32)] * 4
        out_specs += [whole_block()] * 4
        scratch += [
            VMEM(tokens.shape, BF16),
            VMEM((2, features, 2 * columns), BF16),
            pltpu.SemaphoreType.DMA((4,)),
            pltpu.SemaphoreType.DMA((2,)),
        ]
    out = pl.pallas_call(
        functools.partial(first_kernel, wide_count, per_device, paired),
        out_shape=out_shape,
        in_specs=[hbm] * len(operands),
        out_specs=out_specs,
        scratch_shapes=scratch,
        compiler_params=pltpu.CompilerParams(vmem_limit_bytes=LIMIT),
        cost_estimate=SMALL,
        name="first_step",
    )(*[in_hbm(operand) for operand in operands])
    return [out[shift * CHUNKS : (shift + 1) * CHUNKS] for shift in range(wide_count)], out[count:]


def code_kernel(keep_ref, arrived_ref, code_ref, size_ref):
    block = 128
    for at in range(keep_ref.shape[0] // block):
        span = pl.ds(at * block, block)
        total = keep_ref[span, :] + arrived_ref[span, :]
        size = jnp.max(jnp.abs(total), axis=1, keepdims=True)
        inverse = jnp.where(size > 0, 1.0 / size, 0.0)
        code_ref[span, :] = jnp.round(total * inverse * STEPS).astype(jnp.int32).astype(jnp.int16)
        size_ref[pl.ds(at, 1), :] = jnp.broadcast_to(size, (block, block)).T[:1, :]


def code_rows(keep, arrived):
    row_total, columns = keep.shape
    return pl.pallas_call(
        code_kernel,
        out_shape=[
            jax.ShapeDtypeStruct((row_total, columns), jnp.int16),
            jax.ShapeDtypeStruct((row_total // 128, 128), F32),
        ],
        in_specs=[whole_block()] * 2,
        out_specs=[whole_block()] * 2,
        compiler_params=pltpu.CompilerParams(vmem_limit_bytes=LIMIT),
        cost_estimate=SMALL,
        name="code_rows",
    )(keep, arrived)


def base_kernel(keep_ref, arrived_ref, code_ref, size_ref, tokens_hbm, out_ref, tokens_ref, token_sem):
    copy = pltpu.make_async_copy(tokens_hbm, tokens_ref, token_sem)
    copy.start()
    block = 128
    columns = out_ref.shape[1]
    for at in range(keep_ref.shape[0] // block):
        span = pl.ds(at * block, block)
        size = jnp.broadcast_to(size_ref[pl.ds(at, 1), :], (block, block)).T * (1.0 / STEPS)
        size = jnp.concatenate([size] * (columns // block), axis=1)
        crossed = code_ref[span, :].astype(jnp.int32).astype(F32) * size
        out_ref[span, :] = keep_ref[span, :] + arrived_ref[span, :] + crossed
    copy.wait()


def base_rows(keep, arrived, code, size, tokens):
    return pl.pallas_call(
        base_kernel,
        out_shape=[VMEM(keep.shape, F32), VMEM(tokens.shape, BF16)],
        in_specs=[whole_block()] * 4 + [whole_block(pl.ANY)],
        out_specs=[whole_block()] * 2,
        scratch_shapes=[pltpu.SemaphoreType.DMA],
        compiler_params=pltpu.CompilerParams(vmem_limit_bytes=LIMIT),
        cost_estimate=SMALL,
        name="base_rows",
    )(keep, arrived, code, size, in_hbm(tokens))


def shrink_kernel(tokens_ref, chosen_ref, *refs):
    messages, out_ref, stacked = refs[:-3], refs[-2], refs[-1]
    rows = out_ref.shape[0]
    row_total, features = tokens_ref.shape
    block = 256
    for at, message in enumerate(messages):
        stacked[pl.ds(at * rows, rows), :] = message[:, :features]
    for low in range(0, row_total, block):
        sums = lax.dot_general(
            tokens_ref[pl.ds(low, block), :],
            stacked[...],
            (((1,), (1,)), ((), ())),
            preferred_element_type=F32,
        ).T
        total = None
        for at in range(len(messages)):
            asked = chosen_ref[pl.ds(at, 1), pl.ds(low, block)] > 0
            term = jnp.where(asked, sums[at * rows : (at + 1) * rows, :], 0.0)
            total = term if total is None else total + term
        out_ref[:, pl.ds(low, block)] = total


def shrink(tokens, chosen, messages, earlier):
    row_total, features = tokens.shape
    count = len(messages)
    rows = messages[0].shape[0]
    return pl.pallas_call(
        shrink_kernel,
        out_shape=jax.ShapeDtypeStruct((rows, row_total), F32),
        in_specs=[whole_block()] * (2 + count) + [whole_block(pl.ANY)],
        out_specs=whole_block(),
        scratch_shapes=[VMEM((count * rows, features), BF16)],
        compiler_params=pltpu.CompilerParams(vmem_limit_bytes=LIMIT),
        cost_estimate=SMALL,
        name="shrink",
    )(tokens, chosen, *messages, earlier)


def lift_kernel(base_count, part_count, features, masked, length_ref, chosen_ref, *refs):
    bases = refs[:base_count]
    parts = refs[base_count : base_count + part_count]
    messages, out_ref, stacked = refs[base_count + part_count : -2], refs[-2], refs[-1]
    rows = parts[0].shape[0]
    count = len(messages)
    half = count * rows
    for at, message in enumerate(messages):
        factor = message[:, features:]
        stacked[pl.ds(at * rows, rows), :] = factor
        stacked[pl.ds(half + at * rows, rows), :] = factor
    row_total, columns = out_ref.shape
    block = 256
    position = lax.broadcasted_iota(jnp.int32, (LEN, columns), 0)
    for low in range(0, row_total, block):
        span = pl.ds(low, block)
        shrunk = parts[0][:, span]
        for part in parts[1:]:
            shrunk = shrunk + part[:, span]
        spread = jnp.concatenate(
            [jnp.where(chosen_ref[pl.ds(at, 1), span] > 0, shrunk, 0.0) for at in range(count)], axis=0
        )
        high = spread.astype(BF16)
        remainder = (spread - high.astype(F32)).astype(BF16)
        both = jnp.concatenate([high, remainder], axis=0)
        total = lax.dot_general(
            both, stacked[...], (((0,), (0,)), ((), ())), preferred_element_type=F32
        )
        for base in bases:
            total = total + base[span, :]
        if not masked:
            out_ref[span, :] = total
            continue
        for prompt in range(block // LEN):
            piece = total[prompt * LEN : (prompt + 1) * LEN, :]
            live = position < length_ref[low // LEN + prompt]
            out_ref[pl.ds(low + prompt * LEN, LEN), :] = jnp.where(live, piece, 0.0).astype(BF16)


def lift(lengths, chosen, bases, parts, messages, features, masked):
    row_total, columns = bases[0].shape
    count = len(messages)
    rows = messages[0].shape[0]
    return pl.pallas_call(
        functools.partial(lift_kernel, len(bases), len(parts), features, masked),
        out_shape=jax.ShapeDtypeStruct((row_total, columns), BF16 if masked else F32),
        in_specs=[whole_block(pltpu.SMEM)] + [whole_block()] * (1 + len(bases) + len(parts) + count),
        out_specs=whole_block(),
        scratch_shapes=[VMEM((2 * count * rows, columns), BF16)],
        compiler_params=pltpu.CompilerParams(vmem_limit_bytes=LIMIT),
        cost_estimate=SMALL,
        name="finish" if masked else "lift",
    )(lengths, chosen, *bases, *parts, *messages)


def on_device(
    tokens,
    value_weight,
    adapter_down_factors,
    adapter_up_factors,
    adapter_choice_index,
    adapter_mask,
    prompt_token_length,
):
    wide_count = lax.axis_size("wide")
    narrow_count = lax.axis_size("narrow")
    wide_at = lax.axis_index("wide")
    owner_portion = adapter_down_factors.shape[0]
    row_total, features = tokens.shape
    per_device = row_total // LEN
    columns = adapter_up_factors.shape[2]

    paired = narrow_count == 4
    sent, sums = first_step(
        adapter_choice_index.reshape(1, -1),
        adapter_mask.reshape(1, -1),
        jnp.swapaxes(adapter_down_factors, 1, 2),
        adapter_up_factors,
        tokens,
        value_weight,
        wide_count,
        per_device,
        paired,
    )
    held = [[sent[0][chunk]] for chunk in range(CHUNKS)]
    for chunk in range(CHUNKS):
        for shift in range(1, wide_count):
            ring = [(at, (at + shift) % wide_count) for at in range(wide_count)]
            held[chunk].append(lax.ppermute(sent[shift][chunk], "wide", ring))

    my_choice = lax.dynamic_slice_in_dim(adapter_choice_index, wide_at * per_device, per_device)
    my_mask = lax.dynamic_slice_in_dim(adapter_mask, wide_at * per_device, per_device)
    my_lengths = lax.dynamic_slice_in_dim(prompt_token_length, wide_at * per_device, per_device)
    owners = (wide_at - jnp.arange(wide_count, dtype=jnp.int32) + wide_count) % wide_count
    local = my_choice[None, :] - owners[:, None] * owner_portion
    matches = (my_mask[None, :] == 1) & (local >= 0) & (local < owner_portion)
    order = jnp.arange(per_device, dtype=jnp.int32)[None, :]
    first = jnp.min(
        jnp.where(matches, order * owner_portion + local, per_device * owner_portion), axis=1
    )
    granted = first % owner_portion
    chosen_prompt = (matches & (local == granted[:, None])).astype(F32)
    chosen = jnp.repeat(chosen_prompt, LEN, axis=1)

    if paired:
        core = [(at, at ^ 1) for at in range(4)]
        across = [(at, at ^ 2) for at in range(4)]
        far_send, far_keep, near_send, near_keep = sums
        code, size = code_rows(far_keep, lax.ppermute(far_send, "narrow", core))
        base, resident = base_rows(
            near_keep,
            lax.ppermute(near_send, "narrow", core),
            lax.ppermute(code, "narrow", across),
            lax.ppermute(size, "narrow", across),
            tokens,
        )
    else:
        partial_value = jnp.dot(tokens, value_weight, preferred_element_type=F32)
        base = lax.psum_scatter(partial_value, "narrow", scatter_dimension=1, tiled=True)
        resident = tokens

    early = [base]
    for chunk in range(CHUNKS):
        part = shrink(resident, chosen, held[chunk], early[0])
        if paired:
            part = part + lax.ppermute(part, "narrow", core)
            parts = [part, lax.ppermute(part, "narrow", across)]
        else:
            parts = [lax.psum(part, "narrow")]
        last = chunk == CHUNKS - 1
        early = [lift(my_lengths, chosen, early, parts, held[chunk], features, last)]
    return early[0]


def solution(mesh):
    placed = (
        P(("groups", "wide"), "narrow"),
        P("narrow", None),
        P(("groups", "wide"), "narrow", None),
        P(("groups", "wide"), None, "narrow"),
        P("groups"),
        P("groups"),
        P("groups"),
    )
    return jax.shard_map(
        on_device,
        mesh=mesh,
        in_specs=placed,
        out_specs=P(("groups", "wide"), "narrow"),
        check_vma=False,
    )
```

time: 157 us -> 53.3 us (0.34)
  waiting for transfers between devices: 104 us -> 24.7 us
  matrix products: 23.7 us -> 0 us
  Pallas kernels: 0 us -> 17 us
  between operations: 13.2 us -> 0.08 us
  blocking collectives: 11.3 us -> 0 us
  starting transfers between devices: 0.08 us -> 7.81 us
    reduce_scatter x1 -> x0, waiting for transfers between devices: 48 us -> none  [on_device(): lax.psum_scatter(partial_value, 'narrow', scatter_dimension=1, tiled=True)]
    all_gather x1 -> x0, waiting for transfers between devices: 46.1 us -> none  [on_device(): lax.all_gather(adapter_down_factors, 'wide', axis=0, tiled=True)]
    ppermute x0 -> x9, waiting for transfers between devices: none -> 24.7 us  [the longest x1 10.4 us: on_device(): lax.ppermute(size, 'narrow', across)]
    dot_general x5 -> x0, matrix products: 23.7 us -> none  [the longest x1 9.88 us: on_device(): jnp.dot(tokens, value_weight, preferred_element_type=jnp.float32)]
    pallas_call x0 -> x5, Pallas kernels: none -> 17 us  [the longest x1 9.28 us: first_step(): pl.pallas_call(functools.partial(first_kernel, wide_count, per_device, pa...]
    all_gather x1 -> x0, blocking collectives: 11.3 us -> none  [on_device(): lax.all_gather(adapter_up_factors, 'wide', axis=0, tiled=True)]
    psum x1 -> x0, waiting for transfers between devices: 8.99 us -> none  [on_device(): shrunk = lax.psum(shrunk, 'narrow')]
    ppermute x0 -> x9, starting transfers between devices: none -> 7.81 us  [the longest x3 3.78 us: on_device(): held[chunk].append(lax.ppermute(sent[shift][chunk], 'wide', ring))]
  transfers between devices with their start and end apart: 3 -> 9, of which waited for: 3 -> 5; matrix products, arithmetic and copies ran while one was open for 8% -> 1% of each run, Pallas kernels for 0% -> 9%
where the time goes in v2:
time: 53.3 us; the launch traced here: 52.5 us
  waiting for transfers between devices  24.7 us (46%)
  Pallas kernels  17 us (32%)
  starting transfers between devices  7.81 us (15%)
  local copies, waits for them, and re-layouts  2.53 us (5%)
    ppermute x1, waiting for transfers between devices, on_device(): lax.ppermute(size, 'narrow', across)  10.4 us
    pallas_call x1, Pallas kernels, first_step(): pl.pallas_call(functools.partial(first_kernel, wide_count, per_device, pa...  9.28 us
    ppermute x3, waiting for transfers between devices, on_device(): held[chunk].append(lax.ppermute(sent[shift][chunk], 'wide', ring))  6.91 us
    ppermute x1, waiting for transfers between devices, on_device(): parts = [part, lax.ppermute(part, 'narrow', across)]  6.23 us
    ppermute x3, starting transfers between devices, on_device(): held[chunk].append(lax.ppermute(sent[shift][chunk], 'wide', ring))  3.78 us
    pallas_call x1, Pallas kernels, base_rows(): pl.pallas_call(base_kernel, out_shape=[VMEM(keep.shape, F32), VMEM(tokens...  3.42 us
    unnamed x12, local copies, waits for them, and re-layouts  2.21 us
    pallas_call x1, Pallas kernels, lift(): pl.pallas_call(functools.partial(lift_kernel, len(bases), len(parts), fea...  1.83 us
  transfers between devices with their start and end apart: 9, of which 5 were waited for; matrix products, arithmetic and copies ran while one was open for 1% of the time, Pallas kernels for 9%

profile of v2, /device:TPU:9, one launch (start us, length us, event | category | flops | bytes accessed | tf_op | source)
XLA Modules:
  0.0 52.5 jit_solution(1451350635911636300)
XLA Ops:
  0.0 0.0 copy-start.3
  0.0 0.0 copy-start.4
  0.0 9.3 %first_step.1 = (bf16[64,2304]{1,0:T(8,128)(2,1)}, bf16[64,2304]{1,0:T(8,128)(2,1)}, bf16[64,2304]{1,0:T(8,128)(2,1)}, bf16[64,2304]{1,0:T(8,128)(2,1)}, f32[102...) custom-call(s32[1,128]{1,0:T(1,128)} %bitcast.4, s32[1,128]{1,0:T(1,128)} %bitcast.5, ...), custom_call_target="tpu_custom_call" | custom-call | flops 1 | bytes 1 | tf_op jit(solution)/shard_map/first_step/pallas_call | solution.py:154
  9.3 0.0 copy-start.1
  9.3 1.0 %copy-done.1 = f32[1024,256]{1,0:T(8,128)} copy-done((f32[1024,256]{1,0:T(8,128)}, f32[1024,256]{1,0:T(8,128)S(1)}, u32[]{:S(2)}) %copy-start.1) | copy-done | bytes 1048600
  10.3 0.7 %collective-permute-start.1 = (f32[1024,256]{1,0:T(8,128)}, f32[1024,256]{1,0:T(8,128)S(1)}, u32[]{:S(2)}, u32[]{:S(2)}) collective-permute-start(f32[1024,256]{1,0:T(8,128)} %get-tuple-element.20), channel_id=1, source_target_pairs={{0,1},{1,0},{2,3},{3,2},{4,5},{5,4},{6,7},{7,6},{8,9},{9,8},{10,11... | collective-permute-start | bytes 3145736 | tf_op jit(solution)/shard_map/ppermute | solution.py:367
  10.9 0.0 collective-permute-start
  10.9 1.3 %collective-permute-start.4 = (bf16[64,2304]{1,0:T(8,128)(2,1)}, bf16[64,2304]{1,0:T(8,128)(2,1)S(1)}, u32[]{:S(2)}, u32[]{:S(2)}) collective-permute-start(bf16[64,2304]{1,0:T(8,128)(2,1)} %get-tuple-element.26), channel_id=1, source_target_pairs={{0,4},{4,8},{8,12},{12,0},{1,5},{5,9},{9,13},{13,1},{2,6},{6,10},{... | collective-permute-start | bytes 884744 | tf_op jit(solution)/shard_map/ppermute | solution.py:347
  12.2 1.0 %collective-permute-start.5 = (bf16[64,2304]{1,0:T(8,128)(2,1)}, bf16[64,2304]{1,0:T(8,128)(2,1)S(1)}, u32[]{:S(2)}, u32[]{:S(2)}) collective-permute-start(bf16[64,2304]{1,0:T(8,128)(2,1)} %get-tuple-element.27), channel_id=1, source_target_pairs={{0,8},{4,12},{8,0},{12,4},{1,9},{5,13},{9,1},{13,5},{2,10},{6,14},... | collective-permute-start | bytes 884744 | tf_op jit(solution)/shard_map/ppermute | solution.py:347
  13.3 1.5 %collective-permute-start.6 = (bf16[64,2304]{1,0:T(8,128)(2,1)}, bf16[64,2304]{1,0:T(8,128)(2,1)S(1)}, u32[]{:S(2)}, u32[]{:S(2)}) collective-permute-start(bf16[64,2304]{1,0:T(8,128)(2,1)} %get-tuple-element.28), channel_id=1, source_target_pairs={{0,12},{4,0},{8,4},{12,8},{1,13},{5,1},{9,5},{13,9},{2,14},{6,2},{... | collective-permute-start | bytes 884744 | tf_op jit(solution)/shard_map/ppermute | solution.py:347
  14.7 0.0 copy-done.3
  14.7 0.1 dynamic_slice.11
  14.8 0.0 copy-done.4
  14.8 0.1 dynamic-slice_compare_fusion
  14.9 0.0 collective-permute-done.1.arrived_ref
  14.9 0.0 copy-start
  14.9 1.1 %code_rows.1 = (s16[1024,256]{1,0:T(8,128)(2,1)}, f32[8,128]{1,0:T(8,128)S(1)}) custom-call(f32[1024,256]{1,0:T(8,128)S(1)} %get-tuple-element.19.keep_ref, f32[1024,256]{1,0:T(8,128)S(1)} %collective-permute-done.1.arrived_ref), custom_call_target="tpu_custom_call" | custom-call | flops 1 | bytes 1 | tf_op jit(solution)/shard_map/code_rows/pallas_call | solution.py:180
  16.0 1.2 %collective-permute-start.2 = (s16[1024,256]{1,0:T(8,128)(2,1)}, s16[1024,256]{1,0:T(8,128)(2,1)S(1)}, u32[]{:S(2)}, u32[]{:S(2)}) collective-permute-start(s16[1024,256]{1,0:T(8,128)(2,1)} %get-tuple-element.21), channel_id=1, source_target_pairs={{0,2},{1,3},{2,0},{3,1},{4,6},{5,7},{6,4},{7,5},{8,10},{9,11},{10,... | collective-permute-start | bytes 1572872 | tf_op jit(solution)/shard_map/ppermute | solution.py:371
  17.2 0.2 fusion.1
  17.4 0.0 collective-permute-done.arrived_ref
  17.4 0.3 collective-permute-start.3
  17.7 0.1 fusion.5
  17.8 0.1 broadcast_in_dim.7
  17.9 0.1 reshape.48.chosen_ref
  18.0 10.4 %collective-permute-done.3.size_ref = f32[8,128]{1,0:T(8,128)S(1)} collective-permute-done((f32[8,128]{1,0:T(8,128)S(1)}, f32[8,128]{1,0:T(8,128)S(1)}, u32[]{:S(2)}, u32[]{:S(2)}) %collective-permute-start.3) | collective-permute-done | bytes 4128 | tf_op jit(solution)/shard_map/ppermute | solution.py:372
  28.3 0.0 collective-permute-done.2.code_ref
  28.4 0.0 copy-start.2
  28.4 1.2 %copy-done.2 = f32[1024,256]{1,0:T(8,128)S(1)} copy-done((f32[1024,256]{1,0:T(8,128)S(1)}, f32[1024,256]{1,0:T(8,128)}, u32[]{:S(2)}) %copy-start.2) | copy-done | bytes 1048600
  29.6 3.4 %base_rows.1 = (f32[1024,256]{1,0:T(8,128)S(1)}, bf16[1024,2048]{1,0:T(8,128)(2,1)S(1)}) custom-call(f32[1024,256]{1,0:T(8,128)S(1)} %copy-done.2, f32[1024,256]{1,0:T(8,128)} %collective-permute-done.arrived_ref, s16[1024,256]{1,0:T(8,128)(2,1)S(1)} %collective-permute-done.2.code_ref, f32[8,128]{1,0:T(8,128)S(1)} %collective-permute-done.3.size_ref, ...), custom_call_target="tpu_custom_call" | custom-call | flops 1 | bytes 1 | tf_op jit(solution)/shard_map/base_rows/pallas_call | solution.py:209
  33.0 0.0 copy-start.5
  33.0 0.0 collective-permute-done.4.refs_1_.refs_4_
  33.0 4.3 %collective-permute-done.5.refs_2_.refs_5_ = bf16[64,2304]{1,0:T(8,128)(2,1)S(1)} collective-permute-done((bf16[64,2304]{1,0:T(8,128)(2,1)}, bf16[64,2304]{1,0:T(8,128)(2,1)S(1)}, u32[]{:S(2)}, u32[]{:S(2)}) %collective-permute-start.5) | collective-permute-done | bytes 294944 | tf_op jit(solution)/shard_map/ppermute | solution.py:347
  37.4 2.6 %collective-permute-done.6.refs_3_.refs_6_ = bf16[64,2304]{1,0:T(8,128)(2,1)S(1)} collective-permute-done((bf16[64,2304]{1,0:T(8,128)(2,1)}, bf16[64,2304]{1,0:T(8,128)(2,1)S(1)}, u32[]{:S(2)}, u32[]{:S(2)}) %collective-permute-start.6) | collective-permute-done | bytes 294944 | tf_op jit(solution)/shard_map/ppermute | solution.py:347
  39.9 0.0 copy-done
  39.9 1.4 %shrink.1 = f32[64,1024]{1,0:T(8,128)S(1)} custom-call(bf16[1024,2048]{1,0:T(8,128)(2,1)S(1)} %get-tuple-element.24.tokens_ref, f32[4,1024]{1,0:T(4,128)S(1)} %reshape.48.chosen_ref, bf16[64,2304]{1,0:T(8,128)(2,1)S(1)} %copy-done, bf16[64,2304]{1,0:T(8,128)(2,1)S(1)} %collective-permute-done.4.refs_1_.refs_4_, ...), custom_call_target="tpu_custom_call" | custom-call | flops 1 | bytes 1 | tf_op jit(solution)/shard_map/shrink/pallas_call | solution.py:247
  41.4 0.6 %collective-permute-start.7 = (f32[64,1024]{1,0:T(8,128)S(1)}, f32[64,1024]{1,0:T(8,128)S(1)}, u32[]{:S(2)}, u32[]{:S(2)}) collective-permute-start(f32[64,1024]{1,0:T(8,128)S(1)} %shrink.1), channel_id=1, source_target_pairs={{0,1},{1,0},{2,3},{3,2},{4,5},{5,4},{6,7},{7,6},{8,9},{9,8},{10,11... | collective-permute-start | bytes 786440 | tf_op jit(solution)/shard_map/ppermute | solution.py:384
  41.9 1.2 %collective-permute-done.7 = f32[64,1024]{1,0:T(8,128)S(1)} collective-permute-done((f32[64,1024]{1,0:T(8,128)S(1)}, f32[64,1024]{1,0:T(8,128)S(1)}, u32[]{:S(2)}, u32[]{:S(2)}) %collective-permute-start.7) | collective-permute-done | bytes 262176 | tf_op jit(solution)/shard_map/ppermute | solution.py:384
  43.1 1.3 %collective-permute-start.8 = (f32[64,1024]{1,0:T(8,128)S(1)}, f32[64,1024]{1,0:T(8,128)S(1)}, u32[]{:S(2)}, u32[]{:S(2)}) collective-permute-start(f32[64,1024]{1,0:T(8,128)S(1)} %add.47.refs_1_), channel_id=1, source_target_pairs={{0,2},{1,3},{2,0},{3,1},{4,6},{5,7},{6,4},{7,5},{8,10},{9,11},{10,... | collective-permute-start | bytes 786440 | tf_op jit(solution)/shard_map/ppermute | solution.py:385
  44.4 0.0 copy-done.5
  44.4 0.1 dynamic_slice.9.length_ref
  44.5 6.2 %collective-permute-done.8.refs_2_ = f32[64,1024]{1,0:T(8,128)S(1)} collective-permute-done((f32[64,1024]{1,0:T(8,128)S(1)}, f32[64,1024]{1,0:T(8,128)S(1)}, u32[]{:S(2)}, u32[]{:S(2)}) %collective-permute-start.8) | collective-permute-done | bytes 262176 | tf_op jit(solution)/shard_map/ppermute | solution.py:385
  50.7 1.8 %finish.1 = bf16[1024,256]{1,0:T(8,128)(2,1)} custom-call(s32[32]{0:T(128)S(1)} %dynamic_slice.9.length_ref, f32[4,1024]{1,0:T(4,128)S(1)} %reshape.48.chosen_ref, f32[1024,256]{1,0:T(8,128)S(1)} %get-tuple-element.23.refs_4_.refs_0_, f32[64,1024]{1,0:T(8,128)S(1)} %add.47.refs_1_, f32[64,1024]{1,0:T(8,128)S(1)} %collective-permute-done.8.refs_2_, ...), custom_call_target="tpu_custom_call" | custom-call | flops 1 | bytes 1 | tf_op jit(solution)/shard_map/finish/pallas_call | solution.py:302
  (4 shorter events, 0.1 us)
Async XLA Ops:
  0.0 14.7 %copy-start.3 = (s32[128]{0:T(128)S(1)}, s32[128]{0:T(128)}, u32[]{:S(2)}) copy-start(s32[128]{0:T(128)} %param.11) | copy-start | bytes 1540
  0.0 14.8 %copy-start.4 = (s32[128]{0:T(128)S(1)}, s32[128]{0:T(128)}, u32[]{:S(2)}) copy-start(s32[128]{0:T(128)} %param.12) | copy-start | bytes 1540
  9.3 1.0 %copy-start.1 = (f32[1024,256]{1,0:T(8,128)}, f32[1024,256]{1,0:T(8,128)S(1)}, u32[]{:S(2)}) copy-start(f32[1024,256]{1,0:T(8,128)S(1)} %get-tuple-element.17.keep_ref) | copy-start | bytes 3145732
  10.3 4.6 %collective-permute-start.1 = (f32[1024,256]{1,0:T(8,128)}, f32[1024,256]{1,0:T(8,128)S(1)}, u32[]{:S(2)}, u32[]{:S(2)}) collective-permute-start(f32[1024,256]{1,0:T(8,128)} %get-tuple-element.20), channel_id=1, source_target_pairs={{0,1},{1,0},{2,3},{3,2},{4,5},{5,4},{6,7},{7,6},{8,9},{9,8},{10,11... | collective-permute-start | bytes 3145736 | tf_op jit(solution)/shard_map/ppermute | solution.py:367
  10.9 6.5 %collective-permute-start = (f32[1024,256]{1,0:T(8,128)}, f32[1024,256]{1,0:T(8,128)}, u32[]{:S(2)}, u32[]{:S(2)}) collective-permute-start(f32[1024,256]{1,0:T(8,128)} %get-tuple-element.18), channel_id=1, source_target_pairs={{0,1},{1,0},{2,3},{3,2},{4,5},{5,4},{6,7},{7,6},{8,9},{9,8},{10,11... | collective-permute-start | bytes 3145736 | tf_op jit(solution)/shard_map/ppermute | solution.py:370
  10.9 22.1 %collective-permute-start.4 = (bf16[64,2304]{1,0:T(8,128)(2,1)}, bf16[64,2304]{1,0:T(8,128)(2,1)S(1)}, u32[]{:S(2)}, u32[]{:S(2)}) collective-permute-start(bf16[64,2304]{1,0:T(8,128)(2,1)} %get-tuple-element.26), channel_id=1, source_target_pairs={{0,4},{4,8},{8,12},{12,0},{1,5},{5,9},{9,13},{13,1},{2,6},{6,10},{... | collective-permute-start | bytes 884744 | tf_op jit(solution)/shard_map/ppermute | solution.py:347
  12.2 25.1 %collective-permute-start.5 = (bf16[64,2304]{1,0:T(8,128)(2,1)}, bf16[64,2304]{1,0:T(8,128)(2,1)S(1)}, u32[]{:S(2)}, u32[]{:S(2)}) collective-permute-start(bf16[64,2304]{1,0:T(8,128)(2,1)} %get-tuple-element.27), channel_id=1, source_target_pairs={{0,8},{4,12},{8,0},{12,4},{1,9},{5,13},{9,1},{13,5},{2,10},{6,14},... | collective-permute-start | bytes 884744 | tf_op jit(solution)/shard_map/ppermute | solution.py:347
  13.3 26.7 %collective-permute-start.6 = (bf16[64,2304]{1,0:T(8,128)(2,1)}, bf16[64,2304]{1,0:T(8,128)(2,1)S(1)}, u32[]{:S(2)}, u32[]{:S(2)}) collective-permute-start(bf16[64,2304]{1,0:T(8,128)(2,1)} %get-tuple-element.28), channel_id=1, source_target_pairs={{0,12},{4,0},{8,4},{12,8},{1,13},{5,1},{9,5},{13,9},{2,14},{6,2},{... | collective-permute-start | bytes 884744 | tf_op jit(solution)/shard_map/ppermute | solution.py:347
  14.9 25.0 %copy-start = (bf16[64,2304]{1,0:T(8,128)(2,1)S(1)}, bf16[64,2304]{1,0:T(8,128)(2,1)}, u32[]{:S(2)}) copy-start(bf16[64,2304]{1,0:T(8,128)(2,1)} %get-tuple-element.25.refs_0_.refs_3_) | copy-start | bytes 884740
  16.0 12.4 %collective-permute-start.2 = (s16[1024,256]{1,0:T(8,128)(2,1)}, s16[1024,256]{1,0:T(8,128)(2,1)S(1)}, u32[]{:S(2)}, u32[]{:S(2)}) collective-permute-start(s16[1024,256]{1,0:T(8,128)(2,1)} %get-tuple-element.21), channel_id=1, source_target_pairs={{0,2},{1,3},{2,0},{3,1},{4,6},{5,7},{6,4},{7,5},{8,10},{9,11},{10,... | collective-permute-start | bytes 1572872 | tf_op jit(solution)/shard_map/ppermute | solution.py:371
  17.4 10.9 %collective-permute-start.3 = (f32[8,128]{1,0:T(8,128)S(1)}, f32[8,128]{1,0:T(8,128)S(1)}, u32[]{:S(2)}, u32[]{:S(2)}) collective-permute-start(f32[8,128]{1,0:T(8,128)S(1)} %get-tuple-element.22), channel_id=1, source_target_pairs={{0,2},{1,3},{2,0},{3,1},{4,6},{5,7},{6,4},{7,5},{8,10},{9,11},{10,... | collective-permute-start | bytes 12296 | tf_op jit(solution)/shard_map/ppermute | solution.py:372
  28.4 1.2 %copy-start.2 = (f32[1024,256]{1,0:T(8,128)S(1)}, f32[1024,256]{1,0:T(8,128)}, u32[]{:S(2)}) copy-start(f32[1024,256]{1,0:T(8,128)} %copy-done.1) | copy-start | bytes 3145732
  33.0 11.4 %copy-start.5 = (s32[128]{0:T(128)S(1)}, s32[128]{0:T(128)}, u32[]{:S(2)}) copy-start(s32[128]{0:T(128)} %param.13) | copy-start | bytes 1540
  41.4 1.7 %collective-permute-start.7 = (f32[64,1024]{1,0:T(8,128)S(1)}, f32[64,1024]{1,0:T(8,128)S(1)}, u32[]{:S(2)}, u32[]{:S(2)}) collective-permute-start(f32[64,1024]{1,0:T(8,128)S(1)} %shrink.1), channel_id=1, source_target_pairs={{0,1},{1,0},{2,3},{3,2},{4,5},{5,4},{6,7},{7,6},{8,9},{9,8},{10,11... | collective-permute-start | bytes 786440 | tf_op jit(solution)/shard_map/ppermute | solution.py:384
  43.1 7.6 %collective-permute-start.8 = (f32[64,1024]{1,0:T(8,128)S(1)}, f32[64,1024]{1,0:T(8,128)S(1)}, u32[]{:S(2)}, u32[]{:S(2)}) collective-permute-start(f32[64,1024]{1,0:T(8,128)S(1)} %add.47.refs_1_), channel_id=1, source_target_pairs={{0,2},{1,3},{2,0},{3,1},{4,6},{5,7},{6,4},{7,5},{8,10},{9,11},{10,... | collective-permute-start | bytes 786440 | tf_op jit(solution)/shard_map/ppermute | solution.py:385

commit v3 on v2

v3 whole, which is shorter than its diff:
```python
import functools
import math

import jax
import jax.numpy as jnp
from jax import lax
from jax.experimental import pallas as pl
from jax.experimental.pallas import tpu as pltpu
from jax.sharding import PartitionSpec as P

LEN = 32
CHUNKS = 1
LIMIT = 24 * 2**20
VMEM = pltpu.VMEM
F32 = jnp.float32
BF16 = jnp.bfloat16
STEPS = 32767.0
GRADES = 128.0
SMALL = pl.CostEstimate(flops=1, bytes_accessed=1, transcendentals=0)


def whole_block(array_memory=VMEM):
    return pl.BlockSpec(memory_space=array_memory)


def in_hbm(array):
    return pltpu.with_memory_space_constraint(array, pltpu.HBM)


def quarter_copies(weight_hbm, weight_ref, weight_sem, quarters):
    columns = weight_ref.shape[2]
    return [
        pltpu.make_async_copy(
            weight_hbm.at[:, pl.ds(pl.multiple_of(quarter * columns, columns), columns)],
            weight_ref.at[at],
            weight_sem.at[at],
        )
        for at, quarter in enumerate(quarters)
    ]


def first_kernel(wide_count, per_device, paired, *refs):
    message_count = wide_count * CHUNKS
    loads_in, refs = refs[:4], refs[4:]
    if paired:
        tokens_hbm, weight_hbm, *refs = refs
    messages, refs = refs[:message_count], refs[message_count:]
    if paired:
        sums, refs = refs[:2], refs[2:]
    choice_ref, mask_ref, down_ref, up_ref, load_sem, message_sem = refs[:6]
    owner_portion, rank, features = down_ref.shape
    columns = up_ref.shape[2]
    rows = rank // CHUNKS
    loads = [
        pltpu.make_async_copy(source, target, load_sem.at[at])
        for at, (source, target) in enumerate(zip(loads_in, refs[:4]))
    ]
    for copy in loads:
        copy.start()
    if paired:
        tokens_ref, weight_ref, send_ref, token_sem, weight_sem, send_sem = refs[6:]
        narrow_at = lax.axis_index("narrow")
        mine = lax.rem(narrow_at, 2)
        chip = 2 * (narrow_at // 2)
        weight_copies = quarter_copies(
            weight_hbm, weight_ref, weight_sem, (2 - chip + 1 - mine, 2 - chip + mine)
        )
        blocks = token_sem.shape[0]
        block = tokens_hbm.shape[0] // blocks
        token_copies = [
            pltpu.make_async_copy(
                tokens_hbm.at[pl.ds(at * block, block), :],
                tokens_ref.at[pl.ds(at * block, block), :],
                token_sem.at[at],
            )
            for at in range(blocks)
        ]
        weight_copies[0].start()
        token_copies[0].start()
    loads[0].wait()
    loads[1].wait()
    me = lax.axis_index("wide")
    choice = choice_ref[...]
    prompt = lax.broadcasted_iota(jnp.int32, choice.shape, 1)
    local = choice - me * owner_portion
    wanted = (mask_ref[...] == 1) & (local >= 0) & (local < owner_portion)
    top = jnp.float32(2.0**24)
    key = jnp.where(wanted, (prompt * owner_portion + local).astype(F32), top)
    copies = []
    for shift in range(wide_count):
        reader = lax.rem(me + shift, wide_count)
        low = reader * per_device
        inside = (prompt >= low) & (prompt < low + per_device)
        first = jnp.min(jnp.where(inside, key, top))
        found = jnp.where(first < top, first, 0.0).astype(jnp.int32)
        adapter = lax.rem(found, owner_portion)
        for chunk in range(CHUNKS):
            at = shift * CHUNKS + chunk
            out = messages[at]
            span = pl.ds(chunk * rows, rows)
            copies.append(
                pltpu.make_async_copy(
                    down_ref.at[adapter, span, :], out.at[:, pl.ds(0, features)], message_sem.at[2 * at]
                )
            )
            copies.append(
                pltpu.make_async_copy(
                    up_ref.at[adapter, span, :],
                    out.at[:, pl.ds(features, columns)],
                    message_sem.at[2 * at + 1],
                )
            )
    loads[2].wait()
    loads[3].wait()
    for copy in copies:
        copy.start()
    if paired:
        weight_copies[1].start()
        for copy in token_copies[1:]:
            copy.start()
        weight_copies[0].wait()
        for at, copy in enumerate(token_copies):
            copy.wait()
            span = pl.ds(at * block, block)
            send_ref[span, :] = jnp.dot(tokens_ref[span, :], weight_ref[0], preferred_element_type=F32)
            copy = pltpu.make_async_copy(send_ref.at[span, :], sums[0].at[span, :], send_sem.at[at])
            copy.start()
            copies.append(copy)
        weight_copies[1].wait()
        for at in range(blocks):
            span = pl.ds(at * block, block)
            sums[1][span, :] = jnp.dot(tokens_ref[span, :], weight_ref[1], preferred_element_type=F32)
    for copy in copies:
        copy.wait()


def first_step(choice, mask, down, up, tokens, weight, wide_count, per_device, paired):
    rank, features = down.shape[1:]
    columns = up.shape[2]
    row_total = tokens.shape[0]
    count = wide_count * CHUNKS
    hbm = whole_block(pl.ANY)
    operands = [choice, mask, down, up]
    scratch = [VMEM(operand.shape, operand.dtype) for operand in operands]
    scratch += [pltpu.SemaphoreType.DMA((4,)), pltpu.SemaphoreType.DMA((2 * count,))]
    out_shape = [pltpu.HBM((rank // CHUNKS, features + columns), BF16)] * count
    out_specs = [hbm] * count
    if paired:
        operands += [tokens, weight]
        out_shape += [pltpu.HBM((row_total, columns), F32), VMEM((row_total, columns), F32)]
        out_specs += [hbm, whole_block()]
        scratch += [
            VMEM(tokens.shape, BF16),
            VMEM((2, features, columns), BF16),
            VMEM((row_total, columns), F32),
            pltpu.SemaphoreType.DMA((4,)),
            pltpu.SemaphoreType.DMA((2,)),
            pltpu.SemaphoreType.DMA((4,)),
        ]
    out = pl.pallas_call(
        functools.partial(first_kernel, wide_count, per_device, paired),
        out_shape=out_shape,
        in_specs=[hbm] * len(operands),
        out_specs=out_specs,
        scratch_shapes=scratch,
        compiler_params=pltpu.CompilerParams(vmem_limit_bytes=LIMIT),
        cost_estimate=SMALL,
        name="first_step",
    )(*[in_hbm(operand) for operand in operands])
    return [out[shift * CHUNKS : (shift + 1) * CHUNKS] for shift in range(wide_count)], out[count:]


def code_kernel(keep_ref, arrived_ref, code_ref):
    block = 128
    row_total, columns = keep_ref.shape
    grades = []
    for at in range(row_total // block):
        span = pl.ds(at * block, block)
        total = keep_ref[span, :] + arrived_ref[span, :]
        size = jnp.max(jnp.abs(total), axis=1, keepdims=True)
        grade = jnp.ceil(jnp.log(jnp.maximum(size, 2.0**-120)) * (GRADES / math.log(2.0)))
        scaled = total * jnp.exp2(grade * (-1.0 / GRADES)) * STEPS
        scaled = jnp.clip(jnp.round(scaled), -STEPS, STEPS)
        code_ref[span, :] = scaled.astype(jnp.int32).astype(jnp.int16)
        grades.append(jnp.broadcast_to(grade, (block, block)).T[:1, :])
    grades = jnp.concatenate(grades + [jnp.zeros((16 - len(grades), block), F32)], axis=0)
    grades = jnp.concatenate([grades, jnp.zeros((16, columns - block), F32)], axis=1)
    code_ref[pl.ds(row_total, 16), :] = grades.astype(jnp.int32).astype(jnp.int16)


def code_rows(keep, arrived):
    row_total, columns = keep.shape
    return pl.pallas_call(
        code_kernel,
        out_shape=jax.ShapeDtypeStruct((row_total + 16, columns), jnp.int16),
        in_specs=[whole_block()] * 2,
        out_specs=whole_block(),
        compiler_params=pltpu.CompilerParams(vmem_limit_bytes=LIMIT),
        cost_estimate=SMALL,
        name="code_rows",
    )(keep, arrived)


def near_kernel(tokens_hbm, weight_hbm, ticket_ref, send_hbm, keep_ref, *scratch):
    tokens_ref, weight_ref, send_ref, token_sem, weight_sem, send_sem = scratch
    narrow_at = lax.axis_index("narrow")
    mine = lax.rem(narrow_at, 2)
    chip = 2 * (narrow_at // 2)
    weight_copies = quarter_copies(weight_hbm, weight_ref, weight_sem, (chip + 1 - mine, chip + mine))
    token_copy = pltpu.make_async_copy(tokens_hbm, tokens_ref, token_sem)
    weight_copies[0].start()
    token_copy.start()
    weight_copies[1].start()
    weight_copies[0].wait()
    token_copy.wait()
    block = 256
    spans = [pl.ds(low, block) for low in range(0, tokens_ref.shape[0], block)]
    for span in spans:
        send_ref[span, :] = jnp.dot(tokens_ref[span, :], weight_ref[0], preferred_element_type=F32)
    send_copy = pltpu.make_async_copy(send_ref, send_hbm, send_sem)
    send_copy.start()
    weight_copies[1].wait()
    for span in spans:
        keep_ref[span, :] = jnp.dot(tokens_ref[span, :], weight_ref[1], preferred_element_type=F32)
    send_copy.wait()


def near_columns(tokens, weight, ticket, columns):
    row_total, features = tokens.shape
    hbm = whole_block(pl.ANY)
    return pl.pallas_call(
        near_kernel,
        out_shape=[
            pltpu.HBM((row_total, columns), F32),
            VMEM((row_total, columns), F32),
        ],
        in_specs=[hbm] * 3,
        out_specs=[hbm, whole_block()],
        scratch_shapes=[
            VMEM(tokens.shape, BF16),
            VMEM((2, features, columns), BF16),
            VMEM((row_total, columns), F32),
            pltpu.SemaphoreType.DMA,
            pltpu.SemaphoreType.DMA((2,)),
            pltpu.SemaphoreType.DMA,
        ],
        compiler_params=pltpu.CompilerParams(vmem_limit_bytes=LIMIT),
        cost_estimate=SMALL,
        name="near_columns",
    )(in_hbm(tokens), in_hbm(weight), ticket)


def reload_kernel(tokens_hbm, ticket_ref, tokens_ref, token_sem):
    copy = pltpu.make_async_copy(tokens_hbm, tokens_ref, token_sem)
    copy.start()
    copy.wait()


def reload_tokens(tokens, ticket):
    return pl.pallas_call(
        reload_kernel,
        out_shape=VMEM(tokens.shape, BF16),
        in_specs=[whole_block(pl.ANY)] * 2,
        out_specs=whole_block(),
        scratch_shapes=[pltpu.SemaphoreType.DMA],
        compiler_params=pltpu.CompilerParams(vmem_limit_bytes=LIMIT),
        cost_estimate=SMALL,
        name="reload_tokens",
    )(in_hbm(tokens), ticket)


def base_kernel(keep_ref, arrived_ref, code_ref, out_ref):
    row_total, columns = out_ref.shape
    block = 128
    grades = code_ref[pl.ds(row_total, 16), :].astype(jnp.int32).astype(F32)
    sizes = jnp.exp2(grades[:, :block] * (1.0 / GRADES)) * (1.0 / STEPS)
    for at in range(row_total // block):
        span = pl.ds(at * block, block)
        size = jnp.broadcast_to(sizes[at : at + 1, :], (block, block)).T
        size = jnp.concatenate([size] * (columns // block), axis=1)
        crossed = code_ref[span, :].astype(jnp.int32).astype(F32) * size
        out_ref[span, :] = keep_ref[span, :] + arrived_ref[span, :] + crossed


def base_rows(keep, arrived, code):
    return pl.pallas_call(
        base_kernel,
        out_shape=VMEM(keep.shape, F32),
        in_specs=[whole_block()] * 3,
        out_specs=whole_block(),
        compiler_params=pltpu.CompilerParams(vmem_limit_bytes=LIMIT),
        cost_estimate=SMALL,
        name="base_rows",
    )(keep, arrived, code)


def row_parts(refs):
    if len(refs) == 1:
        return [(refs[0], 0)]
    mine = lax.rem(lax.axis_index("narrow"), 2)
    length = refs[0].shape[1]
    return [(refs[0], mine * length), (refs[1], (1 - mine) * length)]


def shrink_kernel(part_count, tokens_ref, chosen_ref, *refs):
    messages, outs, stacked = refs[: -part_count - 1], refs[-part_count - 1 : -1], refs[-1]
    rows = outs[0].shape[0]
    features = tokens_ref.shape[1]
    block = 256
    for at, message in enumerate(messages):
        stacked[pl.ds(at * rows, rows), :] = message[:, :features]
    for out_ref, start in row_parts(outs)[::-1]:
        for low in range(0, out_ref.shape[1], block):
            span = pl.ds(pl.multiple_of(start + low, block), block)
            sums = lax.dot_general(
                tokens_ref[span, :], stacked[...], (((1,), (1,)), ((), ())), preferred_element_type=F32
            ).T
            asked = chosen_ref[:, span] > 0
            total = None
            for at in range(len(messages)):
                term = jnp.where(asked[at : at + 1, :], sums[at * rows : (at + 1) * rows, :], 0.0)
                total = term if total is None else total + term
            out_ref[:, pl.ds(low, block)] = total


def shrink(tokens, chosen, messages, part_count):
    row_total, features = tokens.shape
    count = len(messages)
    rows = messages[0].shape[0]
    return pl.pallas_call(
        functools.partial(shrink_kernel, part_count),
        out_shape=[jax.ShapeDtypeStruct((rows, row_total // part_count), F32)] * part_count,
        in_specs=[whole_block()] * (2 + count),
        out_specs=[whole_block()] * part_count,
        scratch_shapes=[VMEM((count * rows, features), BF16)],
        compiler_params=pltpu.CompilerParams(vmem_limit_bytes=LIMIT),
        cost_estimate=SMALL,
        name="shrink",
    )(tokens, chosen, *messages)


def finish_kernel(part_count, features, length_ref, chosen_ref, *refs):
    base_ref, refs = refs[0], refs[1:]
    parts = refs[:part_count]
    messages, out_ref, stacked = refs[part_count:-2], refs[-2], refs[-1]
    rows = parts[0].shape[0]
    count = len(messages)
    half = count * rows
    for at, message in enumerate(messages):
        factor = message[:, features:]
        stacked[pl.ds(at * rows, rows), :] = factor
        stacked[pl.ds(half + at * rows, rows), :] = factor
    columns = out_ref.shape[1]
    block = 256
    position = lax.broadcasted_iota(jnp.int32, (LEN, columns), 0)
    for part_ref, start in row_parts(parts):
        for low in range(0, part_ref.shape[1], block):
            first_row = pl.multiple_of(start + low, block)
            span = pl.ds(first_row, block)
            shrunk = part_ref[:, pl.ds(low, block)]
            asked = chosen_ref[:, span] > 0
            spread = jnp.concatenate(
                [jnp.where(asked[at : at + 1, :], shrunk, 0.0) for at in range(count)], axis=0
            )
            high = spread.astype(BF16)
            remainder = (spread - high.astype(F32)).astype(BF16)
            both = jnp.concatenate([high, remainder], axis=0)
            total = base_ref[span, :] + lax.dot_general(
                both, stacked[...], (((0,), (0,)), ((), ())), preferred_element_type=F32
            )
            for prompt in range(block // LEN):
                piece = total[prompt * LEN : (prompt + 1) * LEN, :]
                live = position < length_ref[first_row // LEN + prompt]
                rows_at = pl.ds(pl.multiple_of(first_row + prompt * LEN, LEN), LEN)
                out_ref[rows_at, :] = jnp.where(live, piece, 0.0).astype(BF16)


def finish(lengths, chosen, base, parts, messages, features):
    row_total, columns = base.shape
    count = len(messages)
    rows = messages[0].shape[0]
    operands = [chosen, base, *parts, *messages]
    return pl.pallas_call(
        functools.partial(finish_kernel, len(parts), features),
        out_shape=jax.ShapeDtypeStruct((row_total, columns), BF16),
        in_specs=[whole_block(pltpu.SMEM)] + [whole_block()] * len(operands),
        out_specs=whole_block(),
        scratch_shapes=[VMEM((2 * count * rows, columns), BF16)],
        compiler_params=pltpu.CompilerParams(vmem_limit_bytes=LIMIT),
        cost_estimate=SMALL,
        name="finish",
    )(lengths, *operands)


def on_device(
    tokens,
    value_weight,
    adapter_down_factors,
    adapter_up_factors,
    adapter_choice_index,
    adapter_mask,
    prompt_token_length,
):
    wide_count = lax.axis_size("wide")
    narrow_count = lax.axis_size("narrow")
    wide_at = lax.axis_index("wide")
    owner_portion = adapter_down_factors.shape[0]
    row_total, features = tokens.shape
    per_device = row_total // LEN
    columns = adapter_up_factors.shape[2]

    paired = narrow_count == 4
    sent, sums = first_step(
        adapter_choice_index.reshape(1, -1),
        adapter_mask.reshape(1, -1),
        jnp.swapaxes(adapter_down_factors, 1, 2),
        adapter_up_factors,
        tokens,
        value_weight,
        wide_count,
        per_device,
        paired,
    )
    held = [[sent[0][chunk]] for chunk in range(CHUNKS)]
    for chunk in range(CHUNKS):
        for shift in range(1, wide_count):
            ring = [(at, (at + shift) % wide_count) for at in range(wide_count)]
            held[chunk].append(lax.ppermute(sent[shift][chunk], "wide", ring))

    my_choice = lax.dynamic_slice_in_dim(adapter_choice_index, wide_at * per_device, per_device)
    my_mask = lax.dynamic_slice_in_dim(adapter_mask, wide_at * per_device, per_device)
    my_lengths = lax.dynamic_slice_in_dim(prompt_token_length, wide_at * per_device, per_device)
    owners = (wide_at - jnp.arange(wide_count, dtype=jnp.int32) + wide_count) % wide_count
    local = my_choice[None, :] - owners[:, None] * owner_portion
    matches = (my_mask[None, :] == 1) & (local >= 0) & (local < owner_portion)
    order = jnp.arange(per_device, dtype=jnp.int32)[None, :]
    first = jnp.min(
        jnp.where(matches, order * owner_portion + local, per_device * owner_portion), axis=1
    )
    granted = first % owner_portion
    chosen_prompt = (matches & (local == granted[:, None])).astype(F32)
    chosen = jnp.repeat(chosen_prompt, LEN, axis=1)

    if paired:
        core = [(at, at ^ 1) for at in range(4)]
        across = [(at, at ^ 2) for at in range(4)]
        far_send, far_keep = sums
        code = code_rows(far_keep, lax.ppermute(far_send, "narrow", core))
        near_send, near_keep = near_columns(tokens, value_weight, code, columns)
        resident = reload_tokens(tokens, near_keep)
        base = base_rows(
            near_keep, lax.ppermute(near_send, "narrow", core), lax.ppermute(code, "narrow", across)
        )
        keep, send = shrink(resident, chosen, held[0], 2)
        part = keep + lax.ppermute(send, "narrow", core)
        part = part + lax.ppermute(part, "narrow", across)
        parts = [part, lax.ppermute(part, "narrow", core)]
    else:
        partial_value = jnp.dot(tokens, value_weight, preferred_element_type=F32)
        base = lax.psum_scatter(partial_value, "narrow", scatter_dimension=1, tiled=True)
        parts = [lax.psum(shrink(tokens, chosen, held[0], 1)[0], "narrow")]
    return finish(my_lengths, chosen, base, parts, held[0], features)


def solution(mesh):
    placed = (
        P(("groups", "wide"), "narrow"),
        P("narrow", None),
        P(("groups", "wide"), "narrow", None),
        P(("groups", "wide"), None, "narrow"),
        P("groups"),
        P("groups"),
        P("groups"),
    )
    return jax.shard_map(
        on_device,
        mesh=mesh,
        in_specs=placed,
        out_specs=P(("groups", "wide"), "narrow"),
        check_vma=False,
    )
```

time: 53.3 us -> 48.8 us (0.916)
  waiting for transfers between devices: 24.7 us -> 17.6 us
  starting transfers between devices: 7.81 us -> 9.83 us
  Pallas kernels: 17 us -> 18.7 us
  local copies, waits for them, and re-layouts: 2.53 us -> 1.81 us
    ppermute x4, waiting for transfers between devices: 17.8 us -> 4.5 us  [the longest x1 3.5 us: on_device(): part = part + lax.ppermute(part, 'narrow', across)]
    ppermute x3, waiting for transfers between devices: 6.91 us -> 13.1 us  [on_device(): held[chunk].append(lax.ppermute(sent[shift][chunk], 'wide', ring))]
    pallas_call x4 -> x6, Pallas kernels: 7.76 us -> 12.3 us  [the longest x1 5.03 us: near_columns(): pl.pallas_call(near_kernel, out_shape=[pltpu.HBM((row_total, columns), F3...]
    pallas_call x1, Pallas kernels: 9.28 us -> 6.44 us  [first_step(): pl.pallas_call(functools.partial(first_kernel, wide_count, per_device, pa...]
    unnamed x12 -> x8, local copies, waits for them, and re-layouts: 2.21 us -> 0.02 us
    ppermute x4, starting transfers between devices: 2.83 us -> 3.81 us  [the longest x1 1.28 us: on_device(): part = part + lax.ppermute(part, 'narrow', across)]
    ppermute x1, starting transfers between devices: 0.01 us -> 0.97 us  [on_device(): lax.ppermute(near_send, 'narrow', core)]
    reshape x1, local copies, waits for them, and re-layouts: 0.1 us -> 0.93 us  [on_device(): chosen = jnp.repeat(chosen_prompt, LEN, axis=1)]
  transfers between devices with their start and end apart: 9 -> 9, of which waited for: 5 -> 4; matrix products, arithmetic and copies ran while one was open for 1% -> 5% of each run, Pallas kernels for 9% -> 22%
where the time goes in v3:
time: 48.8 us; the launch traced here: 48.5 us
  Pallas kernels  18.7 us (38%)
  waiting for transfers between devices  17.6 us (36%)
  starting transfers between devices  9.83 us (20%)
  local copies, waits for them, and re-layouts  1.81 us (4%)
    ppermute x3, waiting for transfers between devices, on_device(): held[chunk].append(lax.ppermute(sent[shift][chunk], 'wide', ring))  13.1 us
    pallas_call x1, Pallas kernels, first_step(): pl.pallas_call(functools.partial(first_kernel, wide_count, per_device, pa...  6.44 us
    pallas_call x1, Pallas kernels, near_columns(): pl.pallas_call(near_kernel, out_shape=[pltpu.HBM((row_total, columns), F3...  5.03 us
    ppermute x3, starting transfers between devices, on_device(): held[chunk].append(lax.ppermute(sent[shift][chunk], 'wide', ring))  3.78 us
    ppermute x1, waiting for transfers between devices, on_device(): part = part + lax.ppermute(part, 'narrow', across)  3.5 us
    pallas_call x1, Pallas kernels, reload_tokens(): pl.pallas_call(reload_kernel, out_shape=VMEM(tokens.shape, BF16), in_spec...  2.24 us
    pallas_call x1, Pallas kernels, finish(): pl.pallas_call(functools.partial(finish_kernel, len(parts), features), ou...  1.84 us
    pallas_call x1, Pallas kernels, shrink(): pl.pallas_call(functools.partial(shrink_kernel, part_count), out_shape=[j...  1.42 us
  transfers between devices with their start and end apart: 9, of which 4 were waited for; matrix products, arithmetic and copies ran while one was open for 5% of the time, Pallas kernels for 22%

profile of v3, /device:TPU:9, one launch (start us, length us, event | category | flops | bytes accessed | tf_op | source)
XLA Modules:
  0.0 48.5 jit_solution(8769293769896752275)
XLA Ops:
  0.0 0.0 copy-start.1
  0.0 0.0 copy-start.2
  0.0 6.4 %first_step.1 = (bf16[64,2304]{1,0:T(8,128)(2,1)}, bf16[64,2304]{1,0:T(8,128)(2,1)}, bf16[64,2304]{1,0:T(8,128)(2,1)}, bf16[64,2304]{1,0:T(8,128)(2,1)}, f32[1024,256]{1,0:T(8,128)}, /*index=5*/f32[1024,256]{1,0:T(8,128)S(1)}) custom-call(s32[1,128]{1,0:T(1,128)} %bitcast.5, s32[1,128]{1,0:T(1,128)} %bitcast.4, bf16[2,64,2048]{2,1,0:T(8,128)(2,1)} %bitcast.3, ...), custom_call_target="tpu_custom_call" | custom-call | flops 1 | bytes 1 | tf_op jit(solution)/shard_map/first_step/pallas_call | solution.py:160
  6.5 0.7 %collective-permute-start = (f32[1024,256]{1,0:T(8,128)}, f32[1024,256]{1,0:T(8,128)S(1)}, u32[]{:S(2)}, u32[]{:S(2)}) collective-permute-start(f32[1024,256]{1,0:T(8,128)} %get-tuple-element.16), channel_id=1, source_target_pairs={{0,1},{1,0},{2,3},{3,2},{4,5},{5,4},{6,7},{7,6},{8,9},{9,8},{10,11... | collective-permute-start | bytes 3145736 | tf_op jit(solution)/shard_map/ppermute | solution.py:448
  7.2 1.3 %collective-permute-start.3 = (bf16[64,2304]{1,0:T(8,128)(2,1)}, bf16[64,2304]{1,0:T(8,128)(2,1)S(1)}, u32[]{:S(2)}, u32[]{:S(2)}) collective-permute-start(bf16[64,2304]{1,0:T(8,128)(2,1)} %get-tuple-element.20), channel_id=1, source_target_pairs={{0,4},{4,8},{8,12},{12,0},{1,5},{5,9},{9,13},{13,1},{2,6},{6,10},{... | collective-permute-start | bytes 884744 | tf_op jit(solution)/shard_map/ppermute | solution.py:428
  8.5 1.0 %collective-permute-start.4 = (bf16[64,2304]{1,0:T(8,128)(2,1)}, bf16[64,2304]{1,0:T(8,128)(2,1)S(1)}, u32[]{:S(2)}, u32[]{:S(2)}) collective-permute-start(bf16[64,2304]{1,0:T(8,128)(2,1)} %get-tuple-element.21), channel_id=1, source_target_pairs={{0,8},{4,12},{8,0},{12,4},{1,9},{5,13},{9,1},{13,5},{2,10},{6,14},... | collective-permute-start | bytes 884744 | tf_op jit(solution)/shard_map/ppermute | solution.py:428
  9.5 1.5 %collective-permute-start.5 = (bf16[64,2304]{1,0:T(8,128)(2,1)}, bf16[64,2304]{1,0:T(8,128)(2,1)S(1)}, u32[]{:S(2)}, u32[]{:S(2)}) collective-permute-start(bf16[64,2304]{1,0:T(8,128)(2,1)} %get-tuple-element.22), channel_id=1, source_target_pairs={{0,12},{4,0},{8,4},{12,8},{1,13},{5,1},{9,5},{13,9},{2,14},{6,2},{... | collective-permute-start | bytes 884744 | tf_op jit(solution)/shard_map/ppermute | solution.py:428
  11.0 0.0 copy-done.1
  11.0 0.1 dynamic-slice_compare_fusion
  11.1 0.0 collective-permute-done.arrived_ref
  11.1 0.5 code_rows.1.ticket_ref
  11.5 0.0 copy-done.2
  11.5 0.1 dynamic_slice.11
  11.6 5.0 %near_columns.1 = (f32[1024,256]{1,0:T(8,128)}, f32[1024,256]{1,0:T(8,128)S(1)}) custom-call(bf16[1024,2048]{1,0:T(8,128)(2,1)} %tokens_hbm.3, bf16[2048,1024]{1,0:T(8,128)(2,1)} %weight_hbm.1, s16[1040,256]{1,0:T(8,128)(2,1)S(1)} %code_rows.1.ticket_ref), custom_call_target="tpu_custom_call" | custom-call | flops 1 | bytes 1 | tf_op jit(solution)/shard_map/near_columns/pallas_call | solution.py:231
  16.6 1.0 %collective-permute-start.1 = (f32[1024,256]{1,0:T(8,128)}, f32[1024,256]{1,0:T(8,128)S(1)}, u32[]{:S(2)}, u32[]{:S(2)}) collective-permute-start(f32[1024,256]{1,0:T(8,128)} %get-tuple-element.18), channel_id=1, source_target_pairs={{0,1},{1,0},{2,3},{3,2},{4,5},{5,4},{6,7},{7,6},{8,9},{9,8},{10,11... | collective-permute-start | bytes 3145736 | tf_op jit(solution)/shard_map/ppermute | solution.py:452
  17.6 0.2 fusion.1
  17.8 1.3 %collective-permute-start.2 = (s16[1040,256]{1,0:T(8,128)(2,1)S(1)}, s16[1040,256]{1,0:T(8,128)(2,1)}, u32[]{:S(2)}, u32[]{:S(2)}) collective-permute-start(s16[1040,256]{1,0:T(8,128)(2,1)S(1)} %code_rows.1.ticket_ref), channel_id=1, source_target_pairs={{0,2},{1,3},{2,0},{3,1},{4,6},{5,7},{6,4},{7,5},{8,10},{9,11},{10,... | collective-permute-start | bytes 1597448 | tf_op jit(solution)/shard_map/ppermute | solution.py:452
  19.1 0.1 fusion.5
  19.2 0.7 %broadcast_in_dim.7 = f32[4,32,32]{2,1,0:T(8,128)} broadcast(f32[4,32]{1,0:T(4,128)S(1)} %fusion.5), dimensions={0,1} | broadcast | bytes 16896 | tf_op jit(solution)/shard_map/broadcast_in_dim | solution.py:442
  19.9 0.9 %reshape.48.chosen_ref = f32[4,1024]{1,0:T(4,128)S(1)} reshape(f32[4,32,32]{2,1,0:T(8,128)} %broadcast_in_dim.7) | data formatting | bytes 32768 | tf_op jit(solution)/shard_map/reshape | solution.py:442
  20.8 0.0 copy-start
  20.8 2.2 %reload_tokens.1.tokens_ref = bf16[1024,2048]{1,0:T(8,128)(2,1)S(1)} custom-call(bf16[1024,2048]{1,0:T(8,128)(2,1)} %tokens_hbm.3, f32[1024,256]{1,0:T(8,128)S(1)} %get-tuple-element.17.keep_ref.ticket_ref), custom_call_target="tpu_custom_call" | custom-call | flops 1 | bytes 1 | tf_op jit(solution)/shard_map/reload_tokens/pallas_call | solution.py:260
  23.1 0.0 copy-start.3
  23.1 0.0 collective-permute-done.3.refs_1_.refs_4_
  23.1 11.0 %collective-permute-done.4.refs_2_.refs_5_ = bf16[64,2304]{1,0:T(8,128)(2,1)S(1)} collective-permute-done((bf16[64,2304]{1,0:T(8,128)(2,1)}, bf16[64,2304]{1,0:T(8,128)(2,1)S(1)}, u32[]{:S(2)}, u32[]{:S(2)}) %collective-permute-start.4) | collective-permute-done | bytes 294944 | tf_op jit(solution)/shard_map/ppermute | solution.py:428
  34.1 2.1 %collective-permute-done.5.refs_3_.refs_6_ = bf16[64,2304]{1,0:T(8,128)(2,1)S(1)} collective-permute-done((bf16[64,2304]{1,0:T(8,128)(2,1)}, bf16[64,2304]{1,0:T(8,128)(2,1)S(1)}, u32[]{:S(2)}, u32[]{:S(2)}) %collective-permute-start.5) | collective-permute-done | bytes 294944 | tf_op jit(solution)/shard_map/ppermute | solution.py:428
  36.2 0.0 copy-done
  36.2 1.4 %shrink.1 = (f32[64,512]{1,0:T(8,128)S(1)}, f32[64,512]{1,0:T(8,128)S(1)}) custom-call(bf16[1024,2048]{1,0:T(8,128)(2,1)S(1)} %reload_tokens.1.tokens_ref, f32[4,1024]{1,0:T(4,128)S(1)} %reshape.48.chosen_ref, bf16[64,2304]{1,0:T(8,128)(2,1)S(1)} %copy-done, bf16[64,2304]{1,0:T(8,128)(2,1)S(1)} %collective-permute-done.3.refs_1_.refs_4_, ...), custom_call_target="tpu_custom_call" | custom-call | flops 1 | bytes 1 | tf_op jit(solution)/shard_map/shrink/pallas_call | solution.py:330
  37.6 0.5 %collective-permute-start.6 = (f32[64,512]{1,0:T(8,128)S(1)}, f32[64,512]{1,0:T(8,128)S(1)}, u32[]{:S(2)}, u32[]{:S(2)}) collective-permute-start(f32[64,512]{1,0:T(8,128)S(1)} %get-tuple-element.24), channel_id=1, source_target_pairs={{0,1},{1,0},{2,3},{3,2},{4,5},{5,4},{6,7},{7,6},{8,9},{9,8},{10,11... | collective-permute-start | bytes 393224 | tf_op jit(solution)/shard_map/ppermute | solution.py:455
  38.2 1.0 %collective-permute-done.6 = f32[64,512]{1,0:T(8,128)S(1)} collective-permute-done((f32[64,512]{1,0:T(8,128)S(1)}, f32[64,512]{1,0:T(8,128)S(1)}, u32[]{:S(2)}, u32[]{:S(2)}) %collective-permute-start.6) | collective-permute-done | bytes 131104 | tf_op jit(solution)/shard_map/ppermute | solution.py:455
  39.2 1.3 %collective-permute-start.7 = (f32[64,512]{1,0:T(8,128)S(1)}, f32[64,512]{1,0:T(8,128)S(1)}, u32[]{:S(2)}, u32[]{:S(2)}) collective-permute-start(f32[64,512]{1,0:T(8,128)S(1)} %add.50), channel_id=1, source_target_pairs={{0,2},{1,3},{2,0},{3,1},{4,6},{5,7},{6,4},{7,5},{8,10},{9,11},{10,... | collective-permute-start | bytes 393224 | tf_op jit(solution)/shard_map/ppermute | solution.py:456
  40.5 3.5 %collective-permute-done.7 = f32[64,512]{1,0:T(8,128)S(1)} collective-permute-done((f32[64,512]{1,0:T(8,128)S(1)}, f32[64,512]{1,0:T(8,128)S(1)}, u32[]{:S(2)}, u32[]{:S(2)}) %collective-permute-start.7) | collective-permute-done | bytes 131104 | tf_op jit(solution)/shard_map/ppermute | solution.py:456
  44.0 1.3 %collective-permute-start.8 = (f32[64,512]{1,0:T(8,128)S(1)}, f32[64,512]{1,0:T(8,128)S(1)}, u32[]{:S(2)}, u32[]{:S(2)}) collective-permute-start(f32[64,512]{1,0:T(8,128)S(1)} %add.51.refs_1_), channel_id=1, source_target_pairs={{0,1},{1,0},{2,3},{3,2},{4,5},{5,4},{6,7},{7,6},{8,9},{9,8},{10,11... | collective-permute-start | bytes 393224 | tf_op jit(solution)/shard_map/ppermute | solution.py:457
  45.2 0.0 copy-done.3
  45.2 0.1 dynamic_slice.9.length_ref
  45.3 0.0 collective-permute-done.2.code_ref
  45.3 0.0 collective-permute-done.1.arrived_ref
  45.3 1.3 %base_rows.1.refs_0_ = f32[1024,256]{1,0:T(8,128)S(1)} custom-call(f32[1024,256]{1,0:T(8,128)S(1)} %get-tuple-element.17.keep_ref.ticket_ref, f32[1024,256]{1,0:T(8,128)S(1)} %collective-permute-done.1.arrived_ref, s16[1040,256]{1,0:T(8,128)(2,1)} %collective-permute-done.2.code_ref), custom_call_target="tpu_custom_call" | custom-call | flops 1 | bytes 1 | tf_op jit(solution)/shard_map/base_rows/pallas_call | solution.py:286
  46.7 0.0 collective-permute-done.8.refs_2_
  46.7 1.8 %finish.1 = bf16[1024,256]{1,0:T(8,128)(2,1)} custom-call(s32[32]{0:T(128)S(1)} %dynamic_slice.9.length_ref, f32[4,1024]{1,0:T(4,128)S(1)} %reshape.48.chosen_ref, f32[1024,256]{1,0:T(8,128)S(1)} %base_rows.1.refs_0_, f32[64,512]{1,0:T(8,128)S(1)} %add.51.refs_1_, f32[64,512]{1,0:T(8,128)S(1)} %collective-permute-done.8.refs_2_, ...), custom_call_target="tpu_custom_call" | custom-call | flops 1 | bytes 1 | tf_op jit(solution)/shard_map/finish/pallas_call | solution.py:383
  (5 shorter events, 0.1 us)
Async XLA Ops:
  0.0 11.0 %copy-start.1 = (s32[128]{0:T(128)S(1)}, s32[128]{0:T(128)}, u32[]{:S(2)}) copy-start(s32[128]{0:T(128)} %param.12) | copy-start | bytes 1540
  0.0 11.5 %copy-start.2 = (s32[128]{0:T(128)S(1)}, s32[128]{0:T(128)}, u32[]{:S(2)}) copy-start(s32[128]{0:T(128)} %param.11) | copy-start | bytes 1540
  6.5 4.6 %collective-permute-start = (f32[1024,256]{1,0:T(8,128)}, f32[1024,256]{1,0:T(8,128)S(1)}, u32[]{:S(2)}, u32[]{:S(2)}) collective-permute-start(f32[1024,256]{1,0:T(8,128)} %get-tuple-element.16), channel_id=1, source_target_pairs={{0,1},{1,0},{2,3},{3,2},{4,5},{5,4},{6,7},{7,6},{8,9},{9,8},{10,11... | collective-permute-start | bytes 3145736 | tf_op jit(solution)/shard_map/ppermute | solution.py:448
  7.2 15.9 %collective-permute-start.3 = (bf16[64,2304]{1,0:T(8,128)(2,1)}, bf16[64,2304]{1,0:T(8,128)(2,1)S(1)}, u32[]{:S(2)}, u32[]{:S(2)}) collective-permute-start(bf16[64,2304]{1,0:T(8,128)(2,1)} %get-tuple-element.20), channel_id=1, source_target_pairs={{0,4},{4,8},{8,12},{12,0},{1,5},{5,9},{9,13},{13,1},{2,6},{6,10},{... | collective-permute-start | bytes 884744 | tf_op jit(solution)/shard_map/ppermute | solution.py:428
  8.5 25.6 %collective-permute-start.4 = (bf16[64,2304]{1,0:T(8,128)(2,1)}, bf16[64,2304]{1,0:T(8,128)(2,1)S(1)}, u32[]{:S(2)}, u32[]{:S(2)}) collective-permute-start(bf16[64,2304]{1,0:T(8,128)(2,1)} %get-tuple-element.21), channel_id=1, source_target_pairs={{0,8},{4,12},{8,0},{12,4},{1,9},{5,13},{9,1},{13,5},{2,10},{6,14},... | collective-permute-start | bytes 884744 | tf_op jit(solution)/shard_map/ppermute | solution.py:428
  9.5 26.7 %collective-permute-start.5 = (bf16[64,2304]{1,0:T(8,128)(2,1)}, bf16[64,2304]{1,0:T(8,128)(2,1)S(1)}, u32[]{:S(2)}, u32[]{:S(2)}) collective-permute-start(bf16[64,2304]{1,0:T(8,128)(2,1)} %get-tuple-element.22), channel_id=1, source_target_pairs={{0,12},{4,0},{8,4},{12,8},{1,13},{5,1},{9,5},{13,9},{2,14},{6,2},{... | collective-permute-start | bytes 884744 | tf_op jit(solution)/shard_map/ppermute | solution.py:428
  16.6 28.7 %collective-permute-start.1 = (f32[1024,256]{1,0:T(8,128)}, f32[1024,256]{1,0:T(8,128)S(1)}, u32[]{:S(2)}, u32[]{:S(2)}) collective-permute-start(f32[1024,256]{1,0:T(8,128)} %get-tuple-element.18), channel_id=1, source_target_pairs={{0,1},{1,0},{2,3},{3,2},{4,5},{5,4},{6,7},{7,6},{8,9},{9,8},{10,11... | collective-permute-start | bytes 3145736 | tf_op jit(solution)/shard_map/ppermute | solution.py:452
  17.8 27.5 %collective-permute-start.2 = (s16[1040,256]{1,0:T(8,128)(2,1)S(1)}, s16[1040,256]{1,0:T(8,128)(2,1)}, u32[]{:S(2)}, u32[]{:S(2)}) collective-permute-start(s16[1040,256]{1,0:T(8,128)(2,1)S(1)} %code_rows.1.ticket_ref), channel_id=1, source_target_pairs={{0,2},{1,3},{2,0},{3,1},{4,6},{5,7},{6,4},{7,5},{8,10},{9,11},{10,... | collective-permute-start | bytes 1597448 | tf_op jit(solution)/shard_map/ppermute | solution.py:452
  20.8 15.4 %copy-start = (bf16[64,2304]{1,0:T(8,128)(2,1)S(1)}, bf16[64,2304]{1,0:T(8,128)(2,1)}, u32[]{:S(2)}) copy-start(bf16[64,2304]{1,0:T(8,128)(2,1)} %get-tuple-element.19.refs_0_.refs_3_) | copy-start | bytes 884740
  23.1 22.2 %copy-start.3 = (s32[128]{0:T(128)S(1)}, s32[128]{0:T(128)}, u32[]{:S(2)}) copy-start(s32[128]{0:T(128)} %param.13) | copy-start | bytes 1540
  37.6 1.5 %collective-permute-start.6 = (f32[64,512]{1,0:T(8,128)S(1)}, f32[64,512]{1,0:T(8,128)S(1)}, u32[]{:S(2)}, u32[]{:S(2)}) collective-permute-start(f32[64,512]{1,0:T(8,128)S(1)} %get-tuple-element.24), channel_id=1, source_target_pairs={{0,1},{1,0},{2,3},{3,2},{4,5},{5,4},{6,7},{7,6},{8,9},{9,8},{10,11... | collective-permute-start | bytes 393224 | tf_op jit(solution)/shard_map/ppermute | solution.py:455
  39.2 4.8 %collective-permute-start.7 = (f32[64,512]{1,0:T(8,128)S(1)}, f32[64,512]{1,0:T(8,128)S(1)}, u32[]{:S(2)}, u32[]{:S(2)}) collective-permute-start(f32[64,512]{1,0:T(8,128)S(1)} %add.50), channel_id=1, source_target_pairs={{0,2},{1,3},{2,0},{3,1},{4,6},{5,7},{6,4},{7,5},{8,10},{9,11},{10,... | collective-permute-start | bytes 393224 | tf_op jit(solution)/shard_map/ppermute | solution.py:456
  44.0 2.7 %collective-permute-start.8 = (f32[64,512]{1,0:T(8,128)S(1)}, f32[64,512]{1,0:T(8,128)S(1)}, u32[]{:S(2)}, u32[]{:S(2)}) collective-permute-start(f32[64,512]{1,0:T(8,128)S(1)} %add.51.refs_1_), channel_id=1, source_target_pairs={{0,1},{1,0},{2,3},{3,2},{4,5},{5,4},{6,7},{7,6},{8,9},{9,8},{10,11... | collective-permute-start | bytes 393224 | tf_op jit(solution)/shard_map/ppermute | solution.py:457

commit v4 on v3

--- a/solution.py
+++ b/solution.py
@@ -39,14 +39,12 @@
     ]
 
 
-def first_kernel(wide_count, per_device, paired, *refs):
+def pack_kernel(wide_count, per_device, *refs):
     message_count = wide_count * CHUNKS
     loads_in, refs = refs[:4], refs[4:]
-    if paired:
-        tokens_hbm, weight_hbm, *refs = refs
     messages, refs = refs[:message_count], refs[message_count:]
-    if paired:
-        sums, refs = refs[:2], refs[2:]
+    ticket_ref, refs = refs[0], refs[1:]
+    ticket_ref[...] = jnp.zeros_like(ticket_ref)
     choice_ref, mask_ref, down_ref, up_ref, load_sem, message_sem = refs[:6]
     owner_portion, rank, features = down_ref.shape
     columns = up_ref.shape[2]
@@ -57,26 +55,6 @@
     ]
     for copy in loads:
         copy.start()
-    if paired:
-        tokens_ref, weight_ref, send_ref, token_sem, weight_sem, send_sem = refs[6:]
-        narrow_at = lax.axis_index("narrow")
-        mine = lax.rem(narrow_at, 2)
-        chip = 2 * (narrow_at // 2)
-        weight_copies = quarter_copies(
-            weight_hbm, weight_ref, weight_sem, (2 - chip + 1 - mine, 2 - chip + mine)
-        )
-        blocks = token_sem.shape[0]
-        block = tokens_hbm.shape[0] // blocks
-        token_copies = [
-            pltpu.make_async_copy(
-                tokens_hbm.at[pl.ds(at * block, block), :],
-                tokens_ref.at[pl.ds(at * block, block), :],
-                token_sem.at[at],
-            )
-            for at in range(blocks)
-        ]
-        weight_copies[0].start()
-        token_copies[0].start()
     loads[0].wait()
     loads[1].wait()
     me = lax.axis_index("wide")
@@ -114,60 +92,32 @@
     loads[3].wait()
     for copy in copies:
         copy.start()
-    if paired:
-        weight_copies[1].start()
-        for copy in token_copies[1:]:
-            copy.start()
-        weight_copies[0].wait()
-        for at, copy in enumerate(token_copies):
-            copy.wait()
-            span = pl.ds(at * block, block)
-            send_ref[span, :] = jnp.dot(tokens_ref[span, :], weight_ref[0], preferred_element_type=F32)
-            copy = pltpu.make_async_copy(send_ref.at[span, :], sums[0].at[span, :], send_sem.at[at])
-            copy.start()
-            copies.append(copy)
-        weight_copies[1].wait()
-        for at in range(blocks):
-            span = pl.ds(at * block, block)
-            sums[1][span, :] = jnp.dot(tokens_ref[span, :], weight_ref[1], preferred_element_type=F32)
     for copy in copies:
         copy.wait()
 
 
-def first_step(choice, mask, down, up, tokens, weight, wide_count, per_device, paired):
+def pack_messages(choice, mask, down, up, wide_count, per_device):
     rank, features = down.shape[1:]
     columns = up.shape[2]
-    row_total = tokens.shape[0]
     count = wide_count * CHUNKS
     hbm = whole_block(pl.ANY)
     operands = [choice, mask, down, up]
     scratch = [VMEM(operand.shape, operand.dtype) for operand in operands]
     scratch += [pltpu.SemaphoreType.DMA((4,)), pltpu.SemaphoreType.DMA((2 * count,))]
     out_shape = [pltpu.HBM((rank // CHUNKS, features + columns), BF16)] * count
-    out_specs = [hbm] * count
-    if paired:
-        operands += [tokens, weight]
-        out_shape += [pltpu.HBM((row_total, columns), F32), VMEM((row_total, columns), F32)]
-        out_specs += [hbm, whole_block()]
-        scratch += [
-            VMEM(tokens.shape, BF16),
-            VMEM((2, features, columns), BF16),
-            VMEM((row_total, columns), F32),
-            pltpu.SemaphoreType.DMA((4,)),
-            pltpu.SemaphoreType.DMA((2,)),
-            pltpu.SemaphoreType.DMA((4,)),
-        ]
+    out_specs = [hbm] * count + [whole_block()]
+    out_shape += [jax.ShapeDtypeStruct((8, 128), F32)]
     out = pl.pallas_call(
-        functools.partial(first_kernel, wide_count, per_device, paired),
+        functools.partial(pack_kernel, wide_count, per_device),
         out_shape=out_shape,
         in_specs=[hbm] * len(operands),
         out_specs=out_specs,
         scratch_shapes=scratch,
         compiler_params=pltpu.CompilerParams(vmem_limit_bytes=LIMIT),
         cost_estimate=SMALL,
-        name="first_step",
+        name="pack_messages",
     )(*[in_hbm(operand) for operand in operands])
-    return [out[shift * CHUNKS : (shift + 1) * CHUNKS] for shift in range(wide_count)], out[count:]
+    return [out[shift * CHUNKS : (shift + 1) * CHUNKS] for shift in range(wide_count)], out[-1]
 
 
 def code_kernel(keep_ref, arrived_ref, code_ref):
@@ -201,52 +151,58 @@
     )(keep, arrived)
 
 
-def near_kernel(tokens_hbm, weight_hbm, ticket_ref, send_hbm, keep_ref, *scratch):
+def dots_kernel(flip, tokens_hbm, weight_hbm, ticket_ref, send_hbm, keep_ref, *scratch):
     tokens_ref, weight_ref, send_ref, token_sem, weight_sem, send_sem = scratch
     narrow_at = lax.axis_index("narrow")
     mine = lax.rem(narrow_at, 2)
-    chip = 2 * (narrow_at // 2)
+    chip = 2 * ((narrow_at // 2) ^ flip)
     weight_copies = quarter_copies(weight_hbm, weight_ref, weight_sem, (chip + 1 - mine, chip + mine))
-    token_copy = pltpu.make_async_copy(tokens_hbm, tokens_ref, token_sem)
+    blocks = token_sem.shape[0]
+    block = tokens_hbm.shape[0] // blocks
+    spans = [pl.ds(at * block, block) for at in range(blocks)]
+    token_copies = [
+        pltpu.make_async_copy(tokens_hbm.at[span, :], tokens_ref.at[span, :], token_sem.at[at])
+        for at, span in enumerate(spans)
+    ]
     weight_copies[0].start()
-    token_copy.start()
+    token_copies[0].start()
+    token_copies[1].start()
+    weight_copies[0].wait()
     weight_copies[1].start()
-    weight_copies[0].wait()
-    token_copy.wait()
-    block = 256
-    spans = [pl.ds(low, block) for low in range(0, tokens_ref.shape[0], block)]
-    for span in spans:
+    copies = []
+    for at, span in enumerate(spans):
+        token_copies[at].wait()
+        if at + 2 < blocks:
+            token_copies[at + 2].start()
         send_ref[span, :] = jnp.dot(tokens_ref[span, :], weight_ref[0], preferred_element_type=F32)
-    send_copy = pltpu.make_async_copy(send_ref, send_hbm, send_sem)
-    send_copy.start()
+        copies.append(pltpu.make_async_copy(send_ref.at[span, :], send_hbm.at[span, :], send_sem.at[at]))
+        copies[-1].start()
     weight_copies[1].wait()
     for span in spans:
         keep_ref[span, :] = jnp.dot(tokens_ref[span, :], weight_ref[1], preferred_element_type=F32)
-    send_copy.wait()
-
-
-def near_columns(tokens, weight, ticket, columns):
+    for copy in copies:
+        copy.wait()
+
+
+def column_dots(tokens, weight, ticket, columns, flip):
     row_total, features = tokens.shape
     hbm = whole_block(pl.ANY)
     return pl.pallas_call(
-        near_kernel,
-        out_shape=[
-            pltpu.HBM((row_total, columns), F32),
-            VMEM((row_total, columns), F32),
-        ],
+        functools.partial(dots_kernel, flip),
+        out_shape=[pltpu.HBM((row_total, columns), F32), VMEM((row_total, columns), F32)],
         in_specs=[hbm] * 3,
         out_specs=[hbm, whole_block()],
         scratch_shapes=[
             VMEM(tokens.shape, BF16),
             VMEM((2, features, columns), BF16),
             VMEM((row_total, columns), F32),
-            pltpu.SemaphoreType.DMA,
+            pltpu.SemaphoreType.DMA((4,)),
             pltpu.SemaphoreType.DMA((2,)),
-            pltpu.SemaphoreType.DMA,
+            pltpu.SemaphoreType.DMA((4,)),
         ],
         compiler_params=pltpu.CompilerParams(vmem_limit_bytes=LIMIT),
-        cost_estimate=SMALL,
-        name="near_columns",
+        cost_estimate=pl.CostEstimate(flops=1 if flip else 10000000000, bytes_accessed=1, transcendentals=0),
+        name="far_columns" if flip else "near_columns",
     )(in_hbm(tokens), in_hbm(weight), ticket)
 
 
@@ -410,16 +366,13 @@
     columns = adapter_up_factors.shape[2]
 
     paired = narrow_count == 4
-    sent, sums = first_step(
+    sent, ticket = pack_messages(
         adapter_choice_index.reshape(1, -1),
         adapter_mask.reshape(1, -1),
         jnp.swapaxes(adapter_down_factors, 1, 2),
         adapter_up_factors,
-        tokens,
-        value_weight,
         wide_count,
         per_device,
-        paired,
     )
     held = [[sent[0][chunk]] for chunk in range(CHUNKS)]
     for chunk in range(CHUNKS):
@@ -444,9 +397,10 @@
     if paired:
         core = [(at, at ^ 1) for at in range(4)]
         across = [(at, at ^ 2) for at in range(4)]
-        far_send, far_keep = sums
+        ticket = lax.ppermute(ticket, "narrow", core)
+        far_send, far_keep = column_dots(tokens, value_weight, ticket, columns, 1)
         code = code_rows(far_keep, lax.ppermute(far_send, "narrow", core))
-        near_send, near_keep = near_columns(tokens, value_weight, code, columns)
+        near_send, near_keep = column_dots(tokens, value_weight, far_keep, columns, 0)
         resident = reload_tokens(tokens, near_keep)
         base = base_rows(
             near_keep, lax.ppermute(near_send, "narrow", core), lax.ppermute(code, "narrow", across)

time: 48.8 us -> 45.8 us (0.939)
  the two profiles are of different devices: /device:TPU:9 before, /device:TPU:0 now
where the time goes in v4:
time: 45.8 us; the launch traced here: 45.5 us
  Pallas kernels  21.5 us (47%)
  waiting for transfers between devices  10.4 us (23%)
  starting transfers between devices  9.97 us (22%)
  local copies, waits for them, and re-layouts  2.47 us (5%)
  other arithmetic  1.07 us (2%)
    pallas_call x2, Pallas kernels, column_dots(): pl.pallas_call(functools.partial(dots_kernel, flip), out_shape=[pltpu.HBM...  12.3 us
    ppermute x1, waiting for transfers between devices, on_device(): part = part + lax.ppermute(part, 'narrow', across)  8.03 us
    ppermute x3, starting transfers between devices, on_device(): held[chunk].append(lax.ppermute(sent[shift][chunk], 'wide', ring))  6.57 us
    pallas_call x1, Pallas kernels, reload_tokens(): pl.pallas_call(reload_kernel, out_shape=VMEM(tokens.shape, BF16), in_spec...  2.24 us
    pallas_call x1, Pallas kernels, pack_messages(): pl.pallas_call(functools.partial(pack_kernel, wide_count, per_device), ou...  2.19 us
    pallas_call x1, Pallas kernels, finish(): pl.pallas_call(functools.partial(finish_kernel, len(parts), features), ou...  1.84 us
    ppermute x1, starting transfers between devices, on_device(): lax.ppermute(code, 'narrow', across)  1.49 us
    pallas_call x1, Pallas kernels, shrink(): pl.pallas_call(functools.partial(shrink_kernel, part_count), out_shape=[j...  1.42 us
  transfers between devices with their start and end apart: 10, of which 3 were waited for; matrix products, arithmetic and copies ran while one was open for 8% of the time, Pallas kernels for 38%

profile of v4, /device:TPU:0, one launch (start us, length us, event | category | flops | bytes accessed | tf_op | source)
XLA Modules:
  0.0 45.5 jit_solution(1133272759630106926)
XLA Ops:
  0.0 2.2 %pack_messages.1 = (bf16[64,2304]{1,0:T(8,128)(2,1)}, bf16[64,2304]{1,0:T(8,128)(2,1)}, bf16[64,2304]{1,0:T(8,128)(2,1)}, bf16[64,2304]{1,0:T(8,128)(2,1)}, f32[8,128]{1,0:T(8,128)S(1)}) custom-call(s32[1,128]{1,0:T(1,128)} %bitcast.5, s32[1,128]{1,0:T(1,128)} %bitcast.4, bf16[2,64,2048]{2,1,0:T(8,128)(2,1)} %bitcast.3, bf16[2,64,256]{2,1,0:T(8,128)(2,1)} %refs_3_.1), custom_call_target="tpu_custom_call" | custom-call | flops 1 | bytes 1 | tf_op jit(solution)/shard_map/pack_messages/pallas_call | solution.py:110
  2.2 0.5 %collective-permute-start = (f32[8,128]{1,0:T(8,128)S(1)}, f32[8,128]{1,0:T(8,128)S(1)}, u32[]{:S(2)}, u32[]{:S(2)}) collective-permute-start(f32[8,128]{1,0:T(8,128)S(1)} %get-tuple-element.16), channel_id=1, source_target_pairs={{0,1},{1,0},{2,3},{3,2},{4,5},{5,4},{6,7},{7,6},{8,9},{9,8},{10,11... | collective-permute-start | bytes 12296 | tf_op jit(solution)/shard_map/ppermute | solution.py:400
  2.7 2.6 %collective-permute-start.4 = (bf16[64,2304]{1,0:T(8,128)(2,1)}, bf16[64,2304]{1,0:T(8,128)(2,1)S(1)}, u32[]{:S(2)}, u32[]{:S(2)}) collective-permute-start(bf16[64,2304]{1,0:T(8,128)(2,1)} %get-tuple-element.22), channel_id=1, source_target_pairs={{0,4},{4,8},{8,12},{12,0},{1,5},{5,9},{9,13},{13,1},{2,6},{6,10},{... | collective-permute-start | bytes 884744 | tf_op jit(solution)/shard_map/ppermute | solution.py:381
  5.4 2.6 %collective-permute-start.5 = (bf16[64,2304]{1,0:T(8,128)(2,1)}, bf16[64,2304]{1,0:T(8,128)(2,1)S(1)}, u32[]{:S(2)}, u32[]{:S(2)}) collective-permute-start(bf16[64,2304]{1,0:T(8,128)(2,1)} %get-tuple-element.23), channel_id=1, source_target_pairs={{0,8},{4,12},{8,0},{12,4},{1,9},{5,13},{9,1},{13,5},{2,10},{6,14},... | collective-permute-start | bytes 884744 | tf_op jit(solution)/shard_map/ppermute | solution.py:381
  7.9 1.3 %collective-permute-start.6 = (bf16[64,2304]{1,0:T(8,128)(2,1)}, bf16[64,2304]{1,0:T(8,128)(2,1)S(1)}, u32[]{:S(2)}, u32[]{:S(2)}) collective-permute-start(bf16[64,2304]{1,0:T(8,128)(2,1)} %get-tuple-element.24), channel_id=1, source_target_pairs={{0,12},{4,0},{8,4},{12,8},{1,13},{5,1},{9,5},{13,9},{2,14},{6,2},{... | collective-permute-start | bytes 884744 | tf_op jit(solution)/shard_map/ppermute | solution.py:381
  9.3 0.7 %dynamic-slice_compare_fusion = pred[32]{0:T(512)(128)(4,1)S(1)} fusion(s32[128]{0:T(128)} %param.12, s32[]{:T(128)S(6)} %select_n.28), kind=kLoop, calls=%fused_computation.20 | loop fusion | flops 32 | bytes 164 | tf_op jit(solution)/shard_map/eq | solution.py:388
  10.0 0.7 %dynamic_slice.11 = s32[32]{0:T(128)S(1)} dynamic-slice(s32[128]{0:T(128)} %param.11, s32[]{:T(128)S(6)} %select_n.28), dynamic_slice_sizes={32} | dynamic-slice | bytes 260 | tf_op jit(solution)/shard_map/dynamic_slice | solution.py:383
  10.8 0.0 collective-permute-done.ticket_ref
  10.8 6.1 %far_columns.1 = (f32[1024,256]{1,0:T(8,128)}, f32[1024,256]{1,0:T(8,128)S(1)}) custom-call(bf16[1024,2048]{1,0:T(8,128)(2,1)} %tokens_hbm.5, bf16[2048,1024]{1,0:T(8,128)(2,1)} %weight_hbm.3, f32[8,128]{1,0:T(8,128)S(1)} %collective-permute-done.ticket_ref), custom_call_target="tpu_custom_call" | custom-call | flops 1 | bytes 1 | tf_op jit(solution)/shard_map/far_columns/pallas_call | solution.py:190
  16.9 0.1 collective-permute-start.2
  17.0 6.1 %near_columns.1 = (f32[1024,256]{1,0:T(8,128)}, f32[1024,256]{1,0:T(8,128)S(1)}) custom-call(bf16[1024,2048]{1,0:T(8,128)(2,1)} %tokens_hbm.5, bf16[2048,1024]{1,0:T(8,128)(2,1)} %weight_hbm.3, f32[1024,256]{1,0:T(8,128)S(1)} %get-tuple-element.17.ticket_ref.keep_ref), custom_call_target="tpu_custom_call" | custom-call | flops 10000000000 | bytes 1 | tf_op jit(solution)/shard_map/near_columns/pallas_call | solution.py:190
  23.1 0.6 %collective-permute-start.1 = (f32[1024,256]{1,0:T(8,128)}, f32[1024,256]{1,0:T(8,128)S(1)}, u32[]{:S(2)}, u32[]{:S(2)}) collective-permute-start(f32[1024,256]{1,0:T(8,128)} %get-tuple-element.19), channel_id=1, source_target_pairs={{0,1},{1,0},{2,3},{3,2},{4,5},{5,4},{6,7},{7,6},{8,9},{9,8},{10,11... | collective-permute-start | bytes 3145736 | tf_op jit(solution)/shard_map/ppermute | solution.py:406
  23.7 0.2 fusion.1
  23.9 0.0 collective-permute-done.2.arrived_ref
  23.9 1.3 %code_rows.1 = s16[1040,256]{1,0:T(8,128)(2,1)} custom-call(f32[1024,256]{1,0:T(8,128)S(1)} %get-tuple-element.17.ticket_ref.keep_ref, f32[1024,256]{1,0:T(8,128)S(1)} %collective-permute-done.2.arrived_ref), custom_call_target="tpu_custom_call" | custom-call | flops 1 | bytes 1 | tf_op jit(solution)/shard_map/code_rows/pallas_call | solution.py:143
  25.2 1.5 %collective-permute-start.3 = (s16[1040,256]{1,0:T(8,128)(2,1)}, s16[1040,256]{1,0:T(8,128)(2,1)S(1)}, u32[]{:S(2)}, u32[]{:S(2)}) collective-permute-start(s16[1040,256]{1,0:T(8,128)(2,1)} %code_rows.1), channel_id=1, source_target_pairs={{0,2},{1,3},{2,0},{3,1},{4,6},{5,7},{6,4},{7,5},{8,10},{9,11},{10,... | collective-permute-start | bytes 1597448 | tf_op jit(solution)/shard_map/ppermute | solution.py:406
  26.7 0.1 fusion.5
  26.8 0.7 %broadcast_in_dim.7 = f32[4,32,32]{2,1,0:T(8,128)} broadcast(f32[4,32]{1,0:T(4,128)S(1)} %fusion.5), dimensions={0,1} | broadcast | bytes 16896 | tf_op jit(solution)/shard_map/broadcast_in_dim | solution.py:395
  27.5 0.9 %reshape.48.chosen_ref = f32[4,1024]{1,0:T(4,128)S(1)} reshape(f32[4,32,32]{2,1,0:T(8,128)} %broadcast_in_dim.7) | data formatting | bytes 32768 | tf_op jit(solution)/shard_map/reshape | solution.py:395
  28.4 0.0 copy-start
  28.4 2.2 %reload_tokens.1.tokens_ref = bf16[1024,2048]{1,0:T(8,128)(2,1)S(1)} custom-call(bf16[1024,2048]{1,0:T(8,128)(2,1)} %tokens_hbm.5, f32[1024,256]{1,0:T(8,128)S(1)} %get-tuple-element.18.keep_ref.ticket_ref), custom_call_target="tpu_custom_call" | custom-call | flops 1 | bytes 1 | tf_op jit(solution)/shard_map/reload_tokens/pallas_call | solution.py:216
  30.7 0.0 copy-start.1
  30.7 0.0 collective-permute-done.4.refs_1_.refs_4_
  30.7 0.0 collective-permute-done.5.refs_2_.refs_5_
  30.7 0.0 collective-permute-done.6.refs_3_.refs_6_
  30.7 0.0 copy-done
  30.8 1.4 %shrink.1 = (f32[64,512]{1,0:T(8,128)S(1)}, f32[64,512]{1,0:T(8,128)S(1)}) custom-call(bf16[1024,2048]{1,0:T(8,128)(2,1)S(1)} %reload_tokens.1.tokens_ref, f32[4,1024]{1,0:T(4,128)S(1)} %reshape.48.chosen_ref, bf16[64,2304]{1,0:T(8,128)(2,1)S(1)} %copy-done, bf16[64,2304]{1,0:T(8,128)(2,1)S(1)} %collective-permute-done.4.refs_1_.refs_4_, ...), custom_call_target="tpu_custom_call" | custom-call | flops 1 | bytes 1 | tf_op jit(solution)/shard_map/shrink/pallas_call | solution.py:286
  32.2 0.1 collective-permute-start.7
  32.3 1.3 %collective-permute-done.7 = f32[64,512]{1,0:T(8,128)S(1)} collective-permute-done((f32[64,512]{1,0:T(8,128)S(1)}, f32[64,512]{1,0:T(8,128)S(1)}, u32[]{:S(2)}, u32[]{:S(2)}) %collective-permute-start.7) | collective-permute-done | bytes 131104 | tf_op jit(solution)/shard_map/ppermute | solution.py:409
  33.6 0.6 %collective-permute-start.8 = (f32[64,512]{1,0:T(8,128)S(1)}, f32[64,512]{1,0:T(8,128)S(1)}, u32[]{:S(2)}, u32[]{:S(2)}) collective-permute-start(f32[64,512]{1,0:T(8,128)S(1)} %add.50), channel_id=1, source_target_pairs={{0,2},{1,3},{2,0},{3,1},{4,6},{5,7},{6,4},{7,5},{8,10},{9,11},{10,... | collective-permute-start | bytes 393224 | tf_op jit(solution)/shard_map/ppermute | solution.py:410
  34.2 8.0 %collective-permute-done.8 = f32[64,512]{1,0:T(8,128)S(1)} collective-permute-done((f32[64,512]{1,0:T(8,128)S(1)}, f32[64,512]{1,0:T(8,128)S(1)}, u32[]{:S(2)}, u32[]{:S(2)}) %collective-permute-start.8) | collective-permute-done | bytes 131104 | tf_op jit(solution)/shard_map/ppermute | solution.py:410
  42.3 0.1 collective-permute-start.9
  42.4 0.0 copy-done.1
  42.4 0.1 dynamic_slice.9.length_ref
  42.5 0.0 collective-permute-done.1.arrived_ref
  42.5 0.0 collective-permute-done.3.code_ref
  42.5 0.2 base_rows.1.refs_0_
  42.7 1.0 %collective-permute-done.9.refs_2_ = f32[64,512]{1,0:T(8,128)S(1)} collective-permute-done((f32[64,512]{1,0:T(8,128)S(1)}, f32[64,512]{1,0:T(8,128)S(1)}, u32[]{:S(2)}, u32[]{:S(2)}) %collective-permute-start.9) | collective-permute-done | bytes 131104 | tf_op jit(solution)/shard_map/ppermute | solution.py:411
  43.7 1.8 %finish.1 = bf16[1024,256]{1,0:T(8,128)(2,1)} custom-call(s32[32]{0:T(128)S(1)} %dynamic_slice.9.length_ref, f32[4,1024]{1,0:T(4,128)S(1)} %reshape.48.chosen_ref, f32[1024,256]{1,0:T(8,128)S(1)} %base_rows.1.refs_0_, f32[64,512]{1,0:T(8,128)S(1)} %add.51.refs_1_, f32[64,512]{1,0:T(8,128)S(1)} %collective-permute-done.9.refs_2_, ...), custom_call_target="tpu_custom_call" | custom-call | flops 1 | bytes 1 | tf_op jit(solution)/shard_map/finish/pallas_call | solution.py:339
  (5 shorter events, 0.1 us)
Async XLA Ops:
  2.2 8.6 %collective-permute-start = (f32[8,128]{1,0:T(8,128)S(1)}, f32[8,128]{1,0:T(8,128)S(1)}, u32[]{:S(2)}, u32[]{:S(2)}) collective-permute-start(f32[8,128]{1,0:T(8,128)S(1)} %get-tuple-element.16), channel_id=1, source_target_pairs={{0,1},{1,0},{2,3},{3,2},{4,5},{5,4},{6,7},{7,6},{8,9},{9,8},{10,11... | collective-permute-start | bytes 12296 | tf_op jit(solution)/shard_map/ppermute | solution.py:400
  2.7 28.0 %collective-permute-start.4 = (bf16[64,2304]{1,0:T(8,128)(2,1)}, bf16[64,2304]{1,0:T(8,128)(2,1)S(1)}, u32[]{:S(2)}, u32[]{:S(2)}) collective-permute-start(bf16[64,2304]{1,0:T(8,128)(2,1)} %get-tuple-element.22), channel_id=1, source_target_pairs={{0,4},{4,8},{8,12},{12,0},{1,5},{5,9},{9,13},{13,1},{2,6},{6,10},{... | collective-permute-start | bytes 884744 | tf_op jit(solution)/shard_map/ppermute | solution.py:381
  5.4 25.4 %collective-permute-start.5 = (bf16[64,2304]{1,0:T(8,128)(2,1)}, bf16[64,2304]{1,0:T(8,128)(2,1)S(1)}, u32[]{:S(2)}, u32[]{:S(2)}) collective-permute-start(bf16[64,2304]{1,0:T(8,128)(2,1)} %get-tuple-element.23), channel_id=1, source_target_pairs={{0,8},{4,12},{8,0},{12,4},{1,9},{5,13},{9,1},{13,5},{2,10},{6,14},... | collective-permute-start | bytes 884744 | tf_op jit(solution)/shard_map/ppermute | solution.py:381
  7.9 22.8 %collective-permute-start.6 = (bf16[64,2304]{1,0:T(8,128)(2,1)}, bf16[64,2304]{1,0:T(8,128)(2,1)S(1)}, u32[]{:S(2)}, u32[]{:S(2)}) collective-permute-start(bf16[64,2304]{1,0:T(8,128)(2,1)} %get-tuple-element.24), channel_id=1, source_target_pairs={{0,12},{4,0},{8,4},{12,8},{1,13},{5,1},{9,5},{13,9},{2,14},{6,2},{... | collective-permute-start | bytes 884744 | tf_op jit(solution)/shard_map/ppermute | solution.py:381
  16.9 7.0 %collective-permute-start.2 = (f32[1024,256]{1,0:T(8,128)}, f32[1024,256]{1,0:T(8,128)S(1)}, u32[]{:S(2)}, u32[]{:S(2)}) collective-permute-start(f32[1024,256]{1,0:T(8,128)} %get-tuple-element.20), channel_id=1, source_target_pairs={{0,1},{1,0},{2,3},{3,2},{4,5},{5,4},{6,7},{7,6},{8,9},{9,8},{10,11... | collective-permute-start | bytes 3145736 | tf_op jit(solution)/shard_map/ppermute | solution.py:402
  23.1 19.3 %collective-permute-start.1 = (f32[1024,256]{1,0:T(8,128)}, f32[1024,256]{1,0:T(8,128)S(1)}, u32[]{:S(2)}, u32[]{:S(2)}) collective-permute-start(f32[1024,256]{1,0:T(8,128)} %get-tuple-element.19), channel_id=1, source_target_pairs={{0,1},{1,0},{2,3},{3,2},{4,5},{5,4},{6,7},{7,6},{8,9},{9,8},{10,11... | collective-permute-start | bytes 3145736 | tf_op jit(solution)/shard_map/ppermute | solution.py:406
  25.2 17.2 %collective-permute-start.3 = (s16[1040,256]{1,0:T(8,128)(2,1)}, s16[1040,256]{1,0:T(8,128)(2,1)S(1)}, u32[]{:S(2)}, u32[]{:S(2)}) collective-permute-start(s16[1040,256]{1,0:T(8,128)(2,1)} %code_rows.1), channel_id=1, source_target_pairs={{0,2},{1,3},{2,0},{3,1},{4,6},{5,7},{6,4},{7,5},{8,10},{9,11},{10,... | collective-permute-start | bytes 1597448 | tf_op jit(solution)/shard_map/ppermute | solution.py:406
  28.4 2.3 %copy-start = (bf16[64,2304]{1,0:T(8,128)(2,1)S(1)}, bf16[64,2304]{1,0:T(8,128)(2,1)}, u32[]{:S(2)}) copy-start(bf16[64,2304]{1,0:T(8,128)(2,1)} %get-tuple-element.21.refs_0_.refs_3_) | copy-start | bytes 884740
  30.7 11.7 %copy-start.1 = (s32[128]{0:T(128)S(1)}, s32[128]{0:T(128)}, u32[]{:S(2)}) copy-start(s32[128]{0:T(128)} %param.13) | copy-start | bytes 1540
  32.2 1.4 %collective-permute-start.7 = (f32[64,512]{1,0:T(8,128)S(1)}, f32[64,512]{1,0:T(8,128)S(1)}, u32[]{:S(2)}, u32[]{:S(2)}) collective-permute-start(f32[64,512]{1,0:T(8,128)S(1)} %get-tuple-element.26), channel_id=1, source_target_pairs={{0,1},{1,0},{2,3},{3,2},{4,5},{5,4},{6,7},{7,6},{8,9},{9,8},{10,11... | collective-permute-start | bytes 393224 | tf_op jit(solution)/shard_map/ppermute | solution.py:409
  33.6 8.6 %collective-permute-start.8 = (f32[64,512]{1,0:T(8,128)S(1)}, f32[64,512]{1,0:T(8,128)S(1)}, u32[]{:S(2)}, u32[]{:S(2)}) collective-permute-start(f32[64,512]{1,0:T(8,128)S(1)} %add.50), channel_id=1, source_target_pairs={{0,2},{1,3},{2,0},{3,1},{4,6},{5,7},{6,4},{7,5},{8,10},{9,11},{10,... | collective-permute-start | bytes 393224 | tf_op jit(solution)/shard_map/ppermute | solution.py:410
  42.3 1.4 %collective-permute-start.9 = (f32[64,512]{1,0:T(8,128)S(1)}, f32[64,512]{1,0:T(8,128)S(1)}, u32[]{:S(2)}, u32[]{:S(2)}) collective-permute-start(f32[64,512]{1,0:T(8,128)S(1)} %add.51.refs_1_), channel_id=1, source_target_pairs={{0,1},{1,0},{2,3},{3,2},{4,5},{5,4},{6,7},{7,6},{8,9},{9,8},{10,11... | collective-permute-start | bytes 393224 | tf_op jit(solution)/shard_map/ppermute | solution.py:411

commit v5 on v4

--- a/solution.py
+++ b/solution.py
@@ -17,6 +17,7 @@
 STEPS = 32767.0
 GRADES = 128.0
 SMALL = pl.CostEstimate(flops=1, bytes_accessed=1, transcendentals=0)
+LARGE = pl.CostEstimate(flops=10**10, bytes_accessed=1, transcendentals=0)
 
 
 def whole_block(array_memory=VMEM):
@@ -120,6 +121,19 @@
     return [out[shift * CHUNKS : (shift + 1) * CHUNKS] for shift in range(wide_count)], out[-1]
 
 
+def grade_of(size):
+    return jnp.ceil(jnp.log(jnp.maximum(size, 2.0**-120)) * (GRADES / math.log(2.0)))
+
+
+def size_of(grade):
+    return jnp.exp2(grade * (1.0 / GRADES)) * (1.0 / STEPS)
+
+
+def coded(total, grade):
+    scaled = total * jnp.exp2(grade * (-1.0 / GRADES)) * STEPS
+    return jnp.clip(jnp.round(scaled), -STEPS, STEPS).astype(jnp.int32).astype(jnp.int16)
+
+
 def code_kernel(keep_ref, arrived_ref, code_ref):
     block = 128
     row_total, columns = keep_ref.shape
@@ -127,11 +141,8 @@
     for at in range(row_total // block):
         span = pl.ds(at * block, block)
         total = keep_ref[span, :] + arrived_ref[span, :]
-        size = jnp.max(jnp.abs(total), axis=1, keepdims=True)
-        grade = jnp.ceil(jnp.log(jnp.maximum(size, 2.0**-120)) * (GRADES / math.log(2.0)))
-        scaled = total * jnp.exp2(grade * (-1.0 / GRADES)) * STEPS
-        scaled = jnp.clip(jnp.round(scaled), -STEPS, STEPS)
-        code_ref[span, :] = scaled.astype(jnp.int32).astype(jnp.int16)
+        grade = grade_of(jnp.max(jnp.abs(total), axis=1, keepdims=True))
+        code_ref[span, :] = coded(total, grade)
         grades.append(jnp.broadcast_to(grade, (block, block)).T[:1, :])
     grades = jnp.concatenate(grades + [jnp.zeros((16 - len(grades), block), F32)], axis=0)
     grades = jnp.concatenate([grades, jnp.zeros((16, columns - block), F32)], axis=1)
@@ -151,29 +162,11 @@
     )(keep, arrived)
 
 
-def dots_kernel(flip, tokens_hbm, weight_hbm, ticket_ref, send_hbm, keep_ref, *scratch):
-    tokens_ref, weight_ref, send_ref, token_sem, weight_sem, send_sem = scratch
-    narrow_at = lax.axis_index("narrow")
-    mine = lax.rem(narrow_at, 2)
-    chip = 2 * ((narrow_at // 2) ^ flip)
-    weight_copies = quarter_copies(weight_hbm, weight_ref, weight_sem, (chip + 1 - mine, chip + mine))
-    blocks = token_sem.shape[0]
-    block = tokens_hbm.shape[0] // blocks
-    spans = [pl.ds(at * block, block) for at in range(blocks)]
-    token_copies = [
-        pltpu.make_async_copy(tokens_hbm.at[span, :], tokens_ref.at[span, :], token_sem.at[at])
-        for at, span in enumerate(spans)
-    ]
-    weight_copies[0].start()
-    token_copies[0].start()
-    token_copies[1].start()
+def pair_dots(tokens_ref, weight_ref, weight_copies, spans, ready, send_ref, keep_ref, send_hbm, send_sem):
     weight_copies[0].wait()
-    weight_copies[1].start()
     copies = []
     for at, span in enumerate(spans):
-        token_copies[at].wait()
-        if at + 2 < blocks:
-            token_copies[at + 2].start()
+        ready(at)
         send_ref[span, :] = jnp.dot(tokens_ref[span, :], weight_ref[0], preferred_element_type=F32)
         copies.append(pltpu.make_async_copy(send_ref.at[span, :], send_hbm.at[span, :], send_sem.at[at]))
         copies[-1].start()
@@ -184,52 +177,104 @@
         copy.wait()
 
 
-def column_dots(tokens, weight, ticket, columns, flip):
+def row_spans(row_total, blocks):
+    return [pl.ds(at * (row_total // blocks), row_total // blocks) for at in range(blocks)]
+
+
+def far_kernel(tokens_hbm, weight_hbm, ticket_ref, send_hbm, keep_ref, tokens_ref, *scratch):
+    weight_ref, send_ref, weight_sem, send_sem, token_sem = scratch
+    narrow_at = lax.axis_index("narrow")
+    mine = lax.rem(narrow_at, 2)
+    chip = 2 * ((narrow_at // 2) ^ 1)
+    weight_copies = quarter_copies(weight_hbm, weight_ref, weight_sem, (chip + 1 - mine, chip + mine))
+    blocks = token_sem.shape[0]
+    spans = row_spans(tokens_hbm.shape[0], blocks)
+    token_copies = [
+        pltpu.make_async_copy(tokens_hbm.at[span, :], tokens_ref.at[span, :], token_sem.at[at])
+        for at, span in enumerate(spans)
+    ]
+    weight_copies[0].start()
+    for copy in token_copies:
+        copy.start()
+    weight_copies[1].start()
+
+    def ready(at):
+        token_copies[at].wait()
+
+    pair_dots(tokens_ref, weight_ref, weight_copies, spans, ready, send_ref, keep_ref, send_hbm, send_sem)
+
+
+def near_kernel(tokens_ref, weight_hbm, ticket_ref, send_hbm, keep_ref, *scratch):
+    weight_ref, send_ref, weight_sem, send_sem = scratch
+    narrow_at = lax.axis_index("narrow")
+    mine = lax.rem(narrow_at, 2)
+    chip = 2 * (narrow_at // 2)
+    weight_copies = quarter_copies(weight_hbm, weight_ref, weight_sem, (chip + 1 - mine, chip + mine))
+    for copy in weight_copies:
+        copy.start()
+    spans = row_spans(tokens_ref.shape[0], send_sem.shape[0])
+    pair_dots(
+        tokens_ref, weight_ref, weight_copies, spans, lambda at: None, send_ref, keep_ref, send_hbm, send_sem
+    )
+
+
+def column_dots(tokens, weight, ticket, columns, far):
     row_total, features = tokens.shape
     hbm = whole_block(pl.ANY)
-    return pl.pallas_call(
-        functools.partial(dots_kernel, flip),
-        out_shape=[pltpu.HBM((row_total, columns), F32), VMEM((row_total, columns), F32)],
-        in_specs=[hbm] * 3,
-        out_specs=[hbm, whole_block()],
-        scratch_shapes=[
-            VMEM(tokens.shape, BF16),
-            VMEM((2, features, columns), BF16),
-            VMEM((row_total, columns), F32),
-            pltpu.SemaphoreType.DMA((4,)),
-            pltpu.SemaphoreType.DMA((2,)),
-            pltpu.SemaphoreType.DMA((4,)),
-        ],
-        compiler_params=pltpu.CompilerParams(vmem_limit_bytes=LIMIT),
-        cost_estimate=pl.CostEstimate(flops=1 if flip else 10000000000, bytes_accessed=1, transcendentals=0),
-        name="far_columns" if flip else "near_columns",
-    )(in_hbm(tokens), in_hbm(weight), ticket)
-
-
-def reload_kernel(tokens_hbm, ticket_ref, tokens_ref, token_sem):
+    blocks = 4
+    out_shape = [pltpu.HBM((row_total, columns), F32), VMEM((row_total, columns), F32)]
+    scratch = [
+        VMEM((2, features, columns), BF16),
+        VMEM((row_total, columns), F32),
+        pltpu.SemaphoreType.DMA((2,)),
+        pltpu.SemaphoreType.DMA((blocks,)),
+    ]
+    if far:
+        out_shape.append(VMEM(tokens.shape, BF16))
+        scratch.append(pltpu.SemaphoreType.DMA((blocks,)))
+    return pl.pallas_call(
+        far_kernel if far else near_kernel,
+        out_shape=out_shape,
+        in_specs=[hbm if far else whole_block(), hbm, hbm],
+        out_specs=[hbm] + [whole_block()] * (len(out_shape) - 1),
+        scratch_shapes=scratch,
+        compiler_params=pltpu.CompilerParams(vmem_limit_bytes=LIMIT),
+        cost_estimate=SMALL if far else LARGE,
+        name="far_columns" if far else "near_columns",
+    )(in_hbm(tokens) if far else tokens, in_hbm(weight), ticket)
+
+
+def reload_kernel(tokens_hbm, chosen_ref, ticket_ref, tokens_ref, mask_ref, token_sem):
     copy = pltpu.make_async_copy(tokens_hbm, tokens_ref, token_sem)
     copy.start()
+    lanes = 128
+    for low in range(0, tokens_ref.shape[0], lanes):
+        for at in range(chosen_ref.shape[0]):
+            row = chosen_ref[pl.ds(at, 1), pl.ds(low, lanes)]
+            column = jnp.broadcast_to(row, (lanes, lanes)).T
+            mask_ref[pl.ds(low, lanes), pl.ds(at * lanes, lanes)] = column.astype(BF16)
     copy.wait()
 
 
-def reload_tokens(tokens, ticket):
+def reload_tokens(tokens, chosen, ticket):
+    hbm = whole_block(pl.ANY)
     return pl.pallas_call(
         reload_kernel,
-        out_shape=VMEM(tokens.shape, BF16),
-        in_specs=[whole_block(pl.ANY)] * 2,
-        out_specs=whole_block(),
+        out_shape=[VMEM(tokens.shape, BF16), VMEM((tokens.shape[0], chosen.shape[0] * 128), BF16)],
+        in_specs=[hbm, whole_block(), hbm],
+        out_specs=[whole_block()] * 2,
         scratch_shapes=[pltpu.SemaphoreType.DMA],
         compiler_params=pltpu.CompilerParams(vmem_limit_bytes=LIMIT),
         cost_estimate=SMALL,
         name="reload_tokens",
-    )(in_hbm(tokens), ticket)
+    )(in_hbm(tokens), chosen, ticket)
 
 
 def base_kernel(keep_ref, arrived_ref, code_ref, out_ref):
     row_total, columns = out_ref.shape
     block = 128
     grades = code_ref[pl.ds(row_total, 16), :].astype(jnp.int32).astype(F32)
-    sizes = jnp.exp2(grades[:, :block] * (1.0 / GRADES)) * (1.0 / STEPS)
+    sizes = size_of(grades[:, :block])
     for at in range(row_total // block):
         span = pl.ds(at * block, block)
         size = jnp.broadcast_to(sizes[at : at + 1, :], (block, block)).T
@@ -250,44 +295,35 @@
     )(keep, arrived, code)
 
 
-def row_parts(refs):
-    if len(refs) == 1:
-        return [(refs[0], 0)]
-    mine = lax.rem(lax.axis_index("narrow"), 2)
-    length = refs[0].shape[1]
-    return [(refs[0], mine * length), (refs[1], (1 - mine) * length)]
-
-
-def shrink_kernel(part_count, tokens_ref, chosen_ref, *refs):
-    messages, outs, stacked = refs[: -part_count - 1], refs[-part_count - 1 : -1], refs[-1]
-    rows = outs[0].shape[0]
+def shrink_kernel(tokens_ref, chosen_ref, *refs):
+    messages, out_ref, stacked = refs[:-2], refs[-2], refs[-1]
+    rows, row_total = out_ref.shape
     features = tokens_ref.shape[1]
     block = 256
     for at, message in enumerate(messages):
         stacked[pl.ds(at * rows, rows), :] = message[:, :features]
-    for out_ref, start in row_parts(outs)[::-1]:
-        for low in range(0, out_ref.shape[1], block):
-            span = pl.ds(pl.multiple_of(start + low, block), block)
-            sums = lax.dot_general(
-                tokens_ref[span, :], stacked[...], (((1,), (1,)), ((), ())), preferred_element_type=F32
-            ).T
-            asked = chosen_ref[:, span] > 0
-            total = None
-            for at in range(len(messages)):
-                term = jnp.where(asked[at : at + 1, :], sums[at * rows : (at + 1) * rows, :], 0.0)
-                total = term if total is None else total + term
-            out_ref[:, pl.ds(low, block)] = total
-
-
-def shrink(tokens, chosen, messages, part_count):
+    for low in range(0, row_total, block):
+        span = pl.ds(low, block)
+        sums = lax.dot_general(
+            tokens_ref[span, :], stacked[...], (((1,), (1,)), ((), ())), preferred_element_type=F32
+        ).T
+        asked = chosen_ref[:, span] > 0
+        total = None
+        for at in range(len(messages)):
+            term = jnp.where(asked[at : at + 1, :], sums[at * rows : (at + 1) * rows, :], 0.0)
+            total = term if total is None else total + term
+        out_ref[:, span] = total
+
+
+def shrink(tokens, chosen, messages):
     row_total, features = tokens.shape
     count = len(messages)
     rows = messages[0].shape[0]
     return pl.pallas_call(
-        functools.partial(shrink_kernel, part_count),
-        out_shape=[jax.ShapeDtypeStruct((rows, row_total // part_count), F32)] * part_count,
+        shrink_kernel,
+        out_shape=jax.ShapeDtypeStruct((rows, row_total), F32),
         in_specs=[whole_block()] * (2 + count),
-        out_specs=[whole_block()] * part_count,
+        out_specs=whole_block(),
         scratch_shapes=[VMEM((count * rows, features), BF16)],
         compiler_params=pltpu.CompilerParams(vmem_limit_bytes=LIMIT),
         cost_estimate=SMALL,
@@ -295,49 +331,67 @@
     )(tokens, chosen, *messages)
 
 
-def finish_kernel(part_count, features, length_ref, chosen_ref, *refs):
-    base_ref, refs = refs[0], refs[1:]
-    parts = refs[:part_count]
-    messages, out_ref, stacked = refs[part_count:-2], refs[-2], refs[-1]
-    rows = parts[0].shape[0]
-    count = len(messages)
-    half = count * rows
+def shrunk_code_kernel(keep_ref, arrived_ref, total_ref, code_ref):
+    rows, row_total = keep_ref.shape
+    total = keep_ref[...] + arrived_ref[...]
+    total_ref[...] = total
+    grade = grade_of(jnp.max(jnp.abs(total), axis=0, keepdims=True))
+    code_ref[pl.ds(0, rows), :] = coded(total, grade)
+    grades = jnp.concatenate([grade, jnp.zeros((15, row_total), F32)], axis=0)
+    code_ref[pl.ds(rows, 16), :] = grades.astype(jnp.int32).astype(jnp.int16)
+
+
+def code_shrunk(keep, arrived):
+    rows, row_total = keep.shape
+    return pl.pallas_call(
+        shrunk_code_kernel,
+        out_shape=[
+            jax.ShapeDtypeStruct((rows, row_total), F32),
+            jax.ShapeDtypeStruct((rows + 16, row_total), jnp.int16),
+        ],
+        in_specs=[whole_block()] * 2,
+        out_specs=[whole_block()] * 2,
+        compiler_params=pltpu.CompilerParams(vmem_limit_bytes=LIMIT),
+        cost_estimate=SMALL,
+        name="code_shrunk",
+    )(keep, arrived)
+
+
+def finish_kernel(crossing, features, length_ref, base_ref, mask_ref, part_ref, *refs):
+    if crossing:
+        code_ref, *refs = refs
+    messages, out_ref, stacked = refs[:-2], refs[-2], refs[-1]
+    rows = part_ref.shape[0]
     for at, message in enumerate(messages):
         factor = message[:, features:]
-        stacked[pl.ds(at * rows, rows), :] = factor
-        stacked[pl.ds(half + at * rows, rows), :] = factor
-    columns = out_ref.shape[1]
+        stacked[pl.ds(2 * at * rows, rows), :] = factor
+        stacked[pl.ds((2 * at + 1) * rows, rows), :] = factor
+    row_total, columns = out_ref.shape
     block = 256
     position = lax.broadcasted_iota(jnp.int32, (LEN, columns), 0)
-    for part_ref, start in row_parts(parts):
-        for low in range(0, part_ref.shape[1], block):
-            first_row = pl.multiple_of(start + low, block)
-            span = pl.ds(first_row, block)
-            shrunk = part_ref[:, pl.ds(low, block)]
-            asked = chosen_ref[:, span] > 0
-            spread = jnp.concatenate(
-                [jnp.where(asked[at : at + 1, :], shrunk, 0.0) for at in range(count)], axis=0
-            )
-            high = spread.astype(BF16)
-            remainder = (spread - high.astype(F32)).astype(BF16)
-            both = jnp.concatenate([high, remainder], axis=0)
-            total = base_ref[span, :] + lax.dot_general(
-                both, stacked[...], (((0,), (0,)), ((), ())), preferred_element_type=F32
-            )
-            for prompt in range(block // LEN):
-                piece = total[prompt * LEN : (prompt + 1) * LEN, :]
-                live = position < length_ref[first_row // LEN + prompt]
-                rows_at = pl.ds(pl.multiple_of(first_row + prompt * LEN, LEN), LEN)
-                out_ref[rows_at, :] = jnp.where(live, piece, 0.0).astype(BF16)
-
-
-def finish(lengths, chosen, base, parts, messages, features):
+    for low in range(0, row_total, block):
+        span = pl.ds(low, block)
+        shrunk = part_ref[:, span]
+        if crossing:
+            size = size_of(code_ref[pl.ds(rows, 16), span].astype(jnp.int32).astype(F32)[:1, :])
+            shrunk = shrunk + code_ref[pl.ds(0, rows), span].astype(jnp.int32).astype(F32) * size
+        high = shrunk.astype(BF16).astype(F32)
+        both = jnp.concatenate([high, shrunk - high], axis=0).T.astype(BF16)
+        spread = jnp.concatenate([both] * len(messages), axis=1) * mask_ref[span, :]
+        total = base_ref[span, :] + jnp.dot(spread, stacked[...], preferred_element_type=F32)
+        for prompt in range(block // LEN):
+            piece = total[prompt * LEN : (prompt + 1) * LEN, :]
+            live = position < length_ref[low // LEN + prompt]
+            out_ref[pl.ds(low + prompt * LEN, LEN), :] = jnp.where(live, piece, 0.0).astype(BF16)
+
+
+def finish(lengths, base, mask, part, code, messages, features):
     row_total, columns = base.shape
     count = len(messages)
     rows = messages[0].shape[0]
-    operands = [chosen, base, *parts, *messages]
-    return pl.pallas_call(
-        functools.partial(finish_kernel, len(parts), features),
+    operands = [base, mask, part, *code, *messages]
+    return pl.pallas_call(
+        functools.partial(finish_kernel, bool(code), features),
         out_shape=jax.ShapeDtypeStruct((row_total, columns), BF16),
         in_specs=[whole_block(pltpu.SMEM)] + [whole_block()] * len(operands),
         out_specs=whole_block(),
@@ -398,22 +452,23 @@
         core = [(at, at ^ 1) for at in range(4)]
         across = [(at, at ^ 2) for at in range(4)]
         ticket = lax.ppermute(ticket, "narrow", core)
-        far_send, far_keep = column_dots(tokens, value_weight, ticket, columns, 1)
+        far_send, far_keep, held_tokens = column_dots(tokens, value_weight, ticket, columns, True)
         code = code_rows(far_keep, lax.ppermute(far_send, "narrow", core))
-        near_send, near_keep = column_dots(tokens, value_weight, far_keep, columns, 0)
-        resident = reload_tokens(tokens, near_keep)
+        near_send, near_keep = column_dots(held_tokens, value_weight, far_keep, columns, False)
+        resident, mask = reload_tokens(tokens, chosen, near_keep)
         base = base_rows(
             near_keep, lax.ppermute(near_send, "narrow", core), lax.ppermute(code, "narrow", across)
         )
-        keep, send = shrink(resident, chosen, held[0], 2)
-        part = keep + lax.ppermute(send, "narrow", core)
-        part = part + lax.ppermute(part, "narrow", across)
-        parts = [part, lax.ppermute(part, "narrow", core)]
+        part = shrink(resident, chosen, held[0])
+        part, shrunk_code = code_shrunk(part, lax.ppermute(part, "narrow", core))
+        crossed = [lax.ppermute(shrunk_code, "narrow", across)]
     else:
         partial_value = jnp.dot(tokens, value_weight, preferred_element_type=F32)
         base = lax.psum_scatter(partial_value, "narrow", scatter_dimension=1, tiled=True)
-        parts = [lax.psum(shrink(tokens, chosen, held[0], 1)[0], "narrow")]
-    return finish(my_lengths, chosen, base, parts, held[0], features)
+        resident, mask = reload_tokens(tokens, chosen, ticket)
+        part = lax.psum(shrink(resident, chosen, held[0]), "narrow")
+        crossed = []
+    return finish(my_lengths, base, mask, part, crossed, held[0], features)
 
 
 def solution(mesh):

time: 45.8 us -> 43.3 us (0.945)
  the two profiles are of different devices: /device:TPU:0 before, /device:TPU:9 now
where the time goes in v5:
time: 43.3 us; the launch traced here: 42.5 us
  Pallas kernels  20.4 us (47%)
  waiting for transfers between devices  12.2 us (28%)
  starting transfers between devices  8.47 us (20%)
  local copies, waits for them, and re-layouts  1 us (2%)
    pallas_call x2, Pallas kernels, column_dots(): pl.pallas_call(far_kernel if far else near_kernel, out_shape=out_shape, i...  10.1 us
    ppermute x3, waiting for transfers between devices, on_device(): held[chunk].append(lax.ppermute(sent[shift][chunk], 'wide', ring))  8.18 us
    ppermute x3, starting transfers between devices, on_device(): held[chunk].append(lax.ppermute(sent[shift][chunk], 'wide', ring))  3.77 us
    ppermute x1, waiting for transfers between devices, on_device(): crossed = [lax.ppermute(shrunk_code, 'narrow', across)]  2.82 us
    pallas_call x1, Pallas kernels, reload_tokens(): pl.pallas_call(reload_kernel, out_shape=[VMEM(tokens.shape, BF16), VMEM((...  2.2 us
    pallas_call x1, Pallas kernels, pack_messages(): pl.pallas_call(functools.partial(pack_kernel, wide_count, per_device), ou...  2.17 us
    pallas_call x1, Pallas kernels, finish(): pl.pallas_call(functools.partial(finish_kernel, bool(code), features), ou...  1.85 us
    pallas_call x1, Pallas kernels, shrink(): pl.pallas_call(shrink_kernel, out_shape=jax.ShapeDtypeStruct((rows, row_t...  1.42 us
  transfers between devices with their start and end apart: 9, of which 4 were waited for; matrix products, arithmetic and copies ran while one was open for 3% of the time, Pallas kernels for 38%

profile of v5, /device:TPU:9, one launch (start us, length us, event | category | flops | bytes accessed | tf_op | source)
XLA Modules:
  0.0 42.5 jit_solution(11060196869885737543)
XLA Ops:
  0.0 2.2 %pack_messages.1 = (bf16[64,2304]{1,0:T(8,128)(2,1)}, bf16[64,2304]{1,0:T(8,128)(2,1)}, bf16[64,2304]{1,0:T(8,128)(2,1)}, bf16[64,2304]{1,0:T(8,128)(2,1)}, f32[8,128]{1,0:T(8,128)S(1)}) custom-call(s32[1,128]{1,0:T(1,128)} %bitcast.4, s32[1,128]{1,0:T(1,128)} %bitcast.5, bf16[2,64,2048]{2,1,0:T(8,128)(2,1)} %bitcast.3, bf16[2,64,256]{2,1,0:T(8,128)(2,1)} %refs_3_.1), custom_call_target="tpu_custom_call" | custom-call | flops 1 | bytes 1 | tf_op jit(solution)/shard_map/pack_messages/pallas_call | solution.py:111
  2.2 0.7 %collective-permute-start = (f32[8,128]{1,0:T(8,128)S(1)}, f32[8,128]{1,0:T(8,128)S(1)}, u32[]{:S(2)}, u32[]{:S(2)}) collective-permute-start(f32[8,128]{1,0:T(8,128)S(1)} %get-tuple-element.19), channel_id=1, source_target_pairs={{0,1},{1,0},{2,3},{3,2},{4,5},{5,4},{6,7},{7,6},{8,9},{9,8},{10,11... | collective-permute-start | bytes 12296 | tf_op jit(solution)/shard_map/ppermute | solution.py:454
  2.9 1.3 %collective-permute-start.4 = (bf16[64,2304]{1,0:T(8,128)(2,1)}, bf16[64,2304]{1,0:T(8,128)(2,1)S(1)}, u32[]{:S(2)}, u32[]{:S(2)}) collective-permute-start(bf16[64,2304]{1,0:T(8,128)(2,1)} %get-tuple-element.28), channel_id=1, source_target_pairs={{0,4},{4,8},{8,12},{12,0},{1,5},{5,9},{9,13},{13,1},{2,6},{6,10},{... | collective-permute-start | bytes 884744 | tf_op jit(solution)/shard_map/ppermute | solution.py:435
  4.2 1.0 %collective-permute-start.5 = (bf16[64,2304]{1,0:T(8,128)(2,1)}, bf16[64,2304]{1,0:T(8,128)(2,1)S(1)}, u32[]{:S(2)}, u32[]{:S(2)}) collective-permute-start(bf16[64,2304]{1,0:T(8,128)(2,1)} %get-tuple-element.29), channel_id=1, source_target_pairs={{0,8},{4,12},{8,0},{12,4},{1,9},{5,13},{9,1},{13,5},{2,10},{6,14},... | collective-permute-start | bytes 884744 | tf_op jit(solution)/shard_map/ppermute | solution.py:435
  5.2 1.5 %collective-permute-start.6 = (bf16[64,2304]{1,0:T(8,128)(2,1)}, bf16[64,2304]{1,0:T(8,128)(2,1)S(1)}, u32[]{:S(2)}, u32[]{:S(2)}) collective-permute-start(bf16[64,2304]{1,0:T(8,128)(2,1)} %get-tuple-element.30), channel_id=1, source_target_pairs={{0,12},{4,0},{8,4},{12,8},{1,13},{5,1},{9,5},{13,9},{2,14},{6,2},{... | collective-permute-start | bytes 884744 | tf_op jit(solution)/shard_map/ppermute | solution.py:435
  6.7 0.7 %dynamic_slice.11 = s32[32]{0:T(128)S(1)} dynamic-slice(s32[128]{0:T(128)} %param.11, s32[]{:T(128)S(6)} %select_n.28), dynamic_slice_sizes={32} | dynamic-slice | bytes 260 | tf_op jit(solution)/shard_map/dynamic_slice | solution.py:437
  7.4 0.0 collective-permute-done.ticket_ref
  7.5 6.3 %far_columns.1 = (f32[1024,256]{1,0:T(8,128)}, f32[1024,256]{1,0:T(8,128)S(1)}, bf16[1024,2048]{1,0:T(8,128)(2,1)S(1)}) custom-call(bf16[1024,2048]{1,0:T(8,128)(2,1)} %tokens_hbm.3, bf16[2048,1024]{1,0:T(8,128)(2,1)} %weight_hbm.3, f32[8,128]{1,0:T(8,128)S(1)} %collective-permute-done.ticket_ref), custom_call_target="tpu_custom_call" | custom-call | flops 1 | bytes 1 | tf_op jit(solution)/shard_map/far_columns/pallas_call | solution.py:235
  13.7 1.0 %collective-permute-start.2 = (f32[1024,256]{1,0:T(8,128)}, f32[1024,256]{1,0:T(8,128)S(1)}, u32[]{:S(2)}, u32[]{:S(2)}) collective-permute-start(f32[1024,256]{1,0:T(8,128)} %get-tuple-element.24), channel_id=1, source_target_pairs={{0,1},{1,0},{2,3},{3,2},{4,5},{5,4},{6,7},{7,6},{8,9},{9,8},{10,11... | collective-permute-start | bytes 3145736 | tf_op jit(solution)/shard_map/ppermute | solution.py:456
  14.7 0.0 copy-start.1
  14.7 3.8 %near_columns.1 = (f32[1024,256]{1,0:T(8,128)}, f32[1024,256]{1,0:T(8,128)S(1)}) custom-call(bf16[1024,2048]{1,0:T(8,128)(2,1)S(1)} %get-tuple-element.20.tokens_ref, bf16[2048,1024]{1,0:T(8,128)(2,1)} %weight_hbm.3, f32[1024,256]{1,0:T(8,128)S(1)} %get-tuple-element.21.ticket_ref.keep_ref), custom_call_target="tpu_custom_call" | custom-call | flops 10000000000 | bytes 1 | tf_op jit(solution)/shard_map/near_columns/pallas_call | solution.py:235
  18.5 0.0 copy-start
  18.6 0.1 collective-permute-start.1
  18.6 0.0 copy-done.1
  18.6 0.1 dynamic-slice_compare_fusion
  18.7 0.2 fusion.1
  18.9 0.0 collective-permute-done.2.arrived_ref
  18.9 1.2 %code_rows.1 = s16[1040,256]{1,0:T(8,128)(2,1)} custom-call(f32[1024,256]{1,0:T(8,128)S(1)} %get-tuple-element.21.ticket_ref.keep_ref, f32[1024,256]{1,0:T(8,128)S(1)} %collective-permute-done.2.arrived_ref), custom_call_target="tpu_custom_call" | custom-call | flops 1 | bytes 1 | tf_op jit(solution)/shard_map/code_rows/pallas_call | solution.py:154
  20.2 1.2 %collective-permute-start.3 = (s16[1040,256]{1,0:T(8,128)(2,1)}, s16[1040,256]{1,0:T(8,128)(2,1)}, u32[]{:S(2)}, u32[]{:S(2)}) collective-permute-start(s16[1040,256]{1,0:T(8,128)(2,1)} %code_rows.1), channel_id=1, source_target_pairs={{0,2},{1,3},{2,0},{3,1},{4,6},{5,7},{6,4},{7,5},{8,10},{9,11},{10,... | collective-permute-start | bytes 1597448 | tf_op jit(solution)/shard_map/ppermute | solution.py:460
  21.4 0.1 fusion.5
  21.4 0.1 broadcast_in_dim.7
  21.5 0.1 reshape.50.chosen_ref
  21.6 2.2 %reload_tokens.1 = (bf16[1024,2048]{1,0:T(8,128)(2,1)S(1)}, bf16[1024,512]{1,0:T(8,128)(2,1)S(1)}) custom-call(bf16[1024,2048]{1,0:T(8,128)(2,1)} %tokens_hbm.3, f32[4,1024]{1,0:T(4,128)S(1)} %reshape.50.chosen_ref, f32[1024,256]{1,0:T(8,128)S(1)} %get-tuple-element.22.keep_ref.ticket_ref), custom_call_target="tpu_custom_call" | custom-call | flops 1 | bytes 1 | tf_op jit(solution)/shard_map/reload_tokens/pallas_call | solution.py:261
  23.8 0.0 copy-start.2
  23.8 0.0 collective-permute-done.4.refs_1_.refs_2_
  23.9 6.0 %collective-permute-done.5.refs_2_.refs_3_ = bf16[64,2304]{1,0:T(8,128)(2,1)S(1)} collective-permute-done((bf16[64,2304]{1,0:T(8,128)(2,1)}, bf16[64,2304]{1,0:T(8,128)(2,1)S(1)}, u32[]{:S(2)}, u32[]{:S(2)}) %collective-permute-start.5) | collective-permute-done | bytes 294944 | tf_op jit(solution)/shard_map/ppermute | solution.py:435
  29.9 2.2 %collective-permute-done.6.refs_3_.refs_4_ = bf16[64,2304]{1,0:T(8,128)(2,1)S(1)} collective-permute-done((bf16[64,2304]{1,0:T(8,128)(2,1)}, bf16[64,2304]{1,0:T(8,128)(2,1)S(1)}, u32[]{:S(2)}, u32[]{:S(2)}) %collective-permute-start.6) | collective-permute-done | bytes 294944 | tf_op jit(solution)/shard_map/ppermute | solution.py:435
  32.0 0.0 copy-done
  32.0 1.4 %shrink.1.keep_ref = f32[64,1024]{1,0:T(8,128)S(1)} custom-call(bf16[1024,2048]{1,0:T(8,128)(2,1)S(1)} %get-tuple-element.26.tokens_ref, f32[4,1024]{1,0:T(4,128)S(1)} %reshape.50.chosen_ref, bf16[64,2304]{1,0:T(8,128)(2,1)S(1)} %copy-done, bf16[64,2304]{1,0:T(8,128)(2,1)S(1)} %collective-permute-done.4.refs_1_.refs_2_, ...), custom_call_target="tpu_custom_call" | custom-call | flops 1 | bytes 1 | tf_op jit(solution)/shard_map/shrink/pallas_call | solution.py:322
  33.5 0.4 %collective-permute-start.7 = (f32[64,1024]{1,0:T(8,128)S(1)}, f32[64,1024]{1,0:T(8,128)S(1)}, u32[]{:S(2)}, u32[]{:S(2)}) collective-permute-start(f32[64,1024]{1,0:T(8,128)S(1)} %shrink.1.keep_ref), channel_id=1, source_target_pairs={{0,1},{1,0},{2,3},{3,2},{4,5},{5,4},{6,7},{7,6},{8,9},{9,8},{10,11... | collective-permute-start | bytes 786440 | tf_op jit(solution)/shard_map/ppermute | solution.py:463
  33.9 1.2 %collective-permute-done.7.arrived_ref = f32[64,1024]{1,0:T(8,128)S(1)} collective-permute-done((f32[64,1024]{1,0:T(8,128)S(1)}, f32[64,1024]{1,0:T(8,128)S(1)}, u32[]{:S(2)}, u32[]{:S(2)}) %collective-permute-start.7) | collective-permute-done | bytes 262176 | tf_op jit(solution)/shard_map/ppermute | solution.py:463
  35.1 0.1 code_shrunk.1
  35.2 1.3 %collective-permute-start.8 = (s16[80,1024]{1,0:T(8,128)(2,1)S(1)}, s16[80,1024]{1,0:T(8,128)(2,1)S(1)}, u32[]{:S(2)}, u32[]{:S(2)}) collective-permute-start(s16[80,1024]{1,0:T(8,128)(2,1)S(1)} %get-tuple-element.32), channel_id=1, source_target_pairs={{0,2},{1,3},{2,0},{3,1},{4,6},{5,7},{6,4},{7,5},{8,10},{9,11},{10,... | collective-permute-start | bytes 491528 | tf_op jit(solution)/shard_map/ppermute | solution.py:464
  36.4 0.0 copy-done.2
  36.4 0.1 dynamic_slice.9.length_ref
  36.5 0.0 collective-permute-done.1.arrived_ref
  36.5 0.0 collective-permute-done.3.code_ref
  36.5 1.3 %base_rows.1.base_ref = f32[1024,256]{1,0:T(8,128)S(1)} custom-call(f32[1024,256]{1,0:T(8,128)S(1)} %get-tuple-element.22.keep_ref.ticket_ref, f32[1024,256]{1,0:T(8,128)S(1)} %collective-permute-done.1.arrived_ref, s16[1040,256]{1,0:T(8,128)(2,1)} %collective-permute-done.3.code_ref), custom_call_target="tpu_custom_call" | custom-call | flops 1 | bytes 1 | tf_op jit(solution)/shard_map/base_rows/pallas_call | solution.py:287
  37.8 2.8 %collective-permute-done.8.refs_0_ = s16[80,1024]{1,0:T(8,128)(2,1)S(1)} collective-permute-done((s16[80,1024]{1,0:T(8,128)(2,1)S(1)}, s16[80,1024]{1,0:T(8,128)(2,1)S(1)}, u32[]{:S(2)}, u32[]{:S(2)}) %collective-permute-start.8) | collective-permute-done | bytes 163872 | tf_op jit(solution)/shard_map/ppermute | solution.py:464
  40.6 1.8 %finish.1 = bf16[1024,256]{1,0:T(8,128)(2,1)} custom-call(s32[32]{0:T(128)S(1)} %dynamic_slice.9.length_ref, f32[1024,256]{1,0:T(8,128)S(1)} %base_rows.1.base_ref, bf16[1024,512]{1,0:T(8,128)(2,1)S(1)} %get-tuple-element.25.mask_ref, f32[64,1024]{1,0:T(8,128)S(1)} %get-tuple-element.31.part_ref, s16[80,1024]{1,0:T(8,128)(2,1)S(1)} %collective-permute-done.8.refs_0_, ...), custom_call_target="tpu_custom_call" | custom-call | flops 1 | bytes 1 | tf_op jit(solution)/shard_map/finish/pallas_call | solution.py:393
  (3 shorter events, 0.0 us)
Async XLA Ops:
  2.2 5.3 %collective-permute-start = (f32[8,128]{1,0:T(8,128)S(1)}, f32[8,128]{1,0:T(8,128)S(1)}, u32[]{:S(2)}, u32[]{:S(2)}) collective-permute-start(f32[8,128]{1,0:T(8,128)S(1)} %get-tuple-element.19), channel_id=1, source_target_pairs={{0,1},{1,0},{2,3},{3,2},{4,5},{5,4},{6,7},{7,6},{8,9},{9,8},{10,11... | collective-permute-start | bytes 12296 | tf_op jit(solution)/shard_map/ppermute | solution.py:454
  2.9 20.9 %collective-permute-start.4 = (bf16[64,2304]{1,0:T(8,128)(2,1)}, bf16[64,2304]{1,0:T(8,128)(2,1)S(1)}, u32[]{:S(2)}, u32[]{:S(2)}) collective-permute-start(bf16[64,2304]{1,0:T(8,128)(2,1)} %get-tuple-element.28), channel_id=1, source_target_pairs={{0,4},{4,8},{8,12},{12,0},{1,5},{5,9},{9,13},{13,1},{2,6},{6,10},{... | collective-permute-start | bytes 884744 | tf_op jit(solution)/shard_map/ppermute | solution.py:435
  4.2 25.6 %collective-permute-start.5 = (bf16[64,2304]{1,0:T(8,128)(2,1)}, bf16[64,2304]{1,0:T(8,128)(2,1)S(1)}, u32[]{:S(2)}, u32[]{:S(2)}) collective-permute-start(bf16[64,2304]{1,0:T(8,128)(2,1)} %get-tuple-element.29), channel_id=1, source_target_pairs={{0,8},{4,12},{8,0},{12,4},{1,9},{5,13},{9,1},{13,5},{2,10},{6,14},... | collective-permute-start | bytes 884744 | tf_op jit(solution)/shard_map/ppermute | solution.py:435
  5.2 26.8 %collective-permute-start.6 = (bf16[64,2304]{1,0:T(8,128)(2,1)}, bf16[64,2304]{1,0:T(8,128)(2,1)S(1)}, u32[]{:S(2)}, u32[]{:S(2)}) collective-permute-start(bf16[64,2304]{1,0:T(8,128)(2,1)} %get-tuple-element.30), channel_id=1, source_target_pairs={{0,12},{4,0},{8,4},{12,8},{1,13},{5,1},{9,5},{13,9},{2,14},{6,2},{... | collective-permute-start | bytes 884744 | tf_op jit(solution)/shard_map/ppermute | solution.py:435
  13.7 5.2 %collective-permute-start.2 = (f32[1024,256]{1,0:T(8,128)}, f32[1024,256]{1,0:T(8,128)S(1)}, u32[]{:S(2)}, u32[]{:S(2)}) collective-permute-start(f32[1024,256]{1,0:T(8,128)} %get-tuple-element.24), channel_id=1, source_target_pairs={{0,1},{1,0},{2,3},{3,2},{4,5},{5,4},{6,7},{7,6},{8,9},{9,8},{10,11... | collective-permute-start | bytes 3145736 | tf_op jit(solution)/shard_map/ppermute | solution.py:456
  14.7 3.9 %copy-start.1 = (s32[128]{0:T(128)S(1)}, s32[128]{0:T(128)}, u32[]{:S(2)}) copy-start(s32[128]{0:T(128)} %param.12) | copy-start | bytes 1540
  18.5 13.5 %copy-start = (bf16[64,2304]{1,0:T(8,128)(2,1)S(1)}, bf16[64,2304]{1,0:T(8,128)(2,1)}, u32[]{:S(2)}) copy-start(bf16[64,2304]{1,0:T(8,128)(2,1)} %get-tuple-element.27.refs_0_.refs_1_) | copy-start | bytes 884740
  18.6 18.0 %collective-permute-start.1 = (f32[1024,256]{1,0:T(8,128)}, f32[1024,256]{1,0:T(8,128)S(1)}, u32[]{:S(2)}, u32[]{:S(2)}) collective-permute-start(f32[1024,256]{1,0:T(8,128)} %get-tuple-element.23), channel_id=1, source_target_pairs={{0,1},{1,0},{2,3},{3,2},{4,5},{5,4},{6,7},{7,6},{8,9},{9,8},{10,11... | collective-permute-start | bytes 3145736 | tf_op jit(solution)/shard_map/ppermute | solution.py:460
  20.2 16.4 %collective-permute-start.3 = (s16[1040,256]{1,0:T(8,128)(2,1)}, s16[1040,256]{1,0:T(8,128)(2,1)}, u32[]{:S(2)}, u32[]{:S(2)}) collective-permute-start(s16[1040,256]{1,0:T(8,128)(2,1)} %code_rows.1), channel_id=1, source_target_pairs={{0,2},{1,3},{2,0},{3,1},{4,6},{5,7},{6,4},{7,5},{8,10},{9,11},{10,... | collective-permute-start | bytes 1597448 | tf_op jit(solution)/shard_map/ppermute | solution.py:460
  23.8 12.6 %copy-start.2 = (s32[128]{0:T(128)S(1)}, s32[128]{0:T(128)}, u32[]{:S(2)}) copy-start(s32[128]{0:T(128)} %param.13) | copy-start | bytes 1540
  33.5 1.6 %collective-permute-start.7 = (f32[64,1024]{1,0:T(8,128)S(1)}, f32[64,1024]{1,0:T(8,128)S(1)}, u32[]{:S(2)}, u32[]{:S(2)}) collective-permute-start(f32[64,1024]{1,0:T(8,128)S(1)} %shrink.1.keep_ref), channel_id=1, source_target_pairs={{0,1},{1,0},{2,3},{3,2},{4,5},{5,4},{6,7},{7,6},{8,9},{9,8},{10,11... | collective-permute-start | bytes 786440 | tf_op jit(solution)/shard_map/ppermute | solution.py:463
  35.2 5.5 %collective-permute-start.8 = (s16[80,1024]{1,0:T(8,128)(2,1)S(1)}, s16[80,1024]{1,0:T(8,128)(2,1)S(1)}, u32[]{:S(2)}, u32[]{:S(2)}) collective-permute-start(s16[80,1024]{1,0:T(8,128)(2,1)S(1)} %get-tuple-element.32), channel_id=1, source_target_pairs={{0,2},{1,3},{2,0},{3,1},{4,6},{5,7},{6,4},{7,5},{8,10},{9,11},{10,... | collective-permute-start | bytes 491528 | tf_op jit(solution)/shard_map/ppermute | solution.py:464

commit v6 on v5

--- a/solution.py
+++ b/solution.py
@@ -22,6 +22,10 @@
 
 def whole_block(array_memory=VMEM):
     return pl.BlockSpec(memory_space=array_memory)
+
+
+def in_vmem(array):
+    return pltpu.with_memory_space_constraint(array, VMEM)
 
 
 def in_hbm(array):
@@ -153,7 +157,7 @@
     row_total, columns = keep.shape
     return pl.pallas_call(
         code_kernel,
-        out_shape=jax.ShapeDtypeStruct((row_total + 16, columns), jnp.int16),
+        out_shape=VMEM((row_total + 16, columns), jnp.int16),
         in_specs=[whole_block()] * 2,
         out_specs=whole_block(),
         compiler_params=pltpu.CompilerParams(vmem_limit_bytes=LIMIT),
@@ -162,23 +166,17 @@
     )(keep, arrived)
 
 
-def pair_dots(tokens_ref, weight_ref, weight_copies, spans, ready, send_ref, keep_ref, send_hbm, send_sem):
-    weight_copies[0].wait()
-    copies = []
-    for at, span in enumerate(spans):
-        ready(at)
+def pair_dots(tokens_ref, weight_ref, weight_copies, send_ref, keep_ref, send_hbm, send_sem):
+    block = 256
+    spans = [pl.ds(low, block) for low in range(0, tokens_ref.shape[0], block)]
+    for span in spans:
         send_ref[span, :] = jnp.dot(tokens_ref[span, :], weight_ref[0], preferred_element_type=F32)
-        copies.append(pltpu.make_async_copy(send_ref.at[span, :], send_hbm.at[span, :], send_sem.at[at]))
-        copies[-1].start()
+    copy = pltpu.make_async_copy(send_ref, send_hbm, send_sem)
+    copy.start()
     weight_copies[1].wait()
     for span in spans:
         keep_ref[span, :] = jnp.dot(tokens_ref[span, :], weight_ref[1], preferred_element_type=F32)
-    for copy in copies:
-        copy.wait()
-
-
-def row_spans(row_total, blocks):
-    return [pl.ds(at * (row_total // blocks), row_total // blocks) for at in range(blocks)]
+    copy.wait()
 
 
 def far_kernel(tokens_hbm, weight_hbm, ticket_ref, send_hbm, keep_ref, tokens_ref, *scratch):
@@ -187,21 +185,13 @@
     mine = lax.rem(narrow_at, 2)
     chip = 2 * ((narrow_at // 2) ^ 1)
     weight_copies = quarter_copies(weight_hbm, weight_ref, weight_sem, (chip + 1 - mine, chip + mine))
-    blocks = token_sem.shape[0]
-    spans = row_spans(tokens_hbm.shape[0], blocks)
-    token_copies = [
-        pltpu.make_async_copy(tokens_hbm.at[span, :], tokens_ref.at[span, :], token_sem.at[at])
-        for at, span in enumerate(spans)
-    ]
+    token_copy = pltpu.make_async_copy(tokens_hbm, tokens_ref, token_sem)
     weight_copies[0].start()
-    for copy in token_copies:
-        copy.start()
+    token_copy.start()
     weight_copies[1].start()
-
-    def ready(at):
-        token_copies[at].wait()
-
-    pair_dots(tokens_ref, weight_ref, weight_copies, spans, ready, send_ref, keep_ref, send_hbm, send_sem)
+    weight_copies[0].wait()
+    token_copy.wait()
+    pair_dots(tokens_ref, weight_ref, weight_copies, send_ref, keep_ref, send_hbm, send_sem)
 
 
 def near_kernel(tokens_ref, weight_hbm, ticket_ref, send_hbm, keep_ref, *scratch):
@@ -212,26 +202,23 @@
     weight_copies = quarter_copies(weight_hbm, weight_ref, weight_sem, (chip + 1 - mine, chip + mine))
     for copy in weight_copies:
         copy.start()
-    spans = row_spans(tokens_ref.shape[0], send_sem.shape[0])
-    pair_dots(
-        tokens_ref, weight_ref, weight_copies, spans, lambda at: None, send_ref, keep_ref, send_hbm, send_sem
-    )
+    weight_copies[0].wait()
+    pair_dots(tokens_ref, weight_ref, weight_copies, send_ref, keep_ref, send_hbm, send_sem)
 
 
 def column_dots(tokens, weight, ticket, columns, far):
     row_total, features = tokens.shape
     hbm = whole_block(pl.ANY)
-    blocks = 4
     out_shape = [pltpu.HBM((row_total, columns), F32), VMEM((row_total, columns), F32)]
     scratch = [
         VMEM((2, features, columns), BF16),
         VMEM((row_total, columns), F32),
         pltpu.SemaphoreType.DMA((2,)),
-        pltpu.SemaphoreType.DMA((blocks,)),
+        pltpu.SemaphoreType.DMA,
     ]
     if far:
         out_shape.append(VMEM(tokens.shape, BF16))
-        scratch.append(pltpu.SemaphoreType.DMA((blocks,)))
+        scratch.append(pltpu.SemaphoreType.DMA)
     return pl.pallas_call(
         far_kernel if far else near_kernel,
         out_shape=out_shape,
@@ -270,9 +257,10 @@
     )(in_hbm(tokens), chosen, ticket)
 
 
-def base_kernel(keep_ref, arrived_ref, code_ref, out_ref):
+def base_kernel(length_ref, keep_ref, arrived_ref, code_ref, out_ref):
     row_total, columns = out_ref.shape
     block = 128
+    position = lax.broadcasted_iota(jnp.int32, (LEN, columns), 0)
     grades = code_ref[pl.ds(row_total, 16), :].astype(jnp.int32).astype(F32)
     sizes = size_of(grades[:, :block])
     for at in range(row_total // block):
@@ -280,55 +268,66 @@
         size = jnp.broadcast_to(sizes[at : at + 1, :], (block, block)).T
         size = jnp.concatenate([size] * (columns // block), axis=1)
         crossed = code_ref[span, :].astype(jnp.int32).astype(F32) * size
-        out_ref[span, :] = keep_ref[span, :] + arrived_ref[span, :] + crossed
-
-
-def base_rows(keep, arrived, code):
+        total = keep_ref[span, :] + arrived_ref[span, :] + crossed
+        for prompt in range(block // LEN):
+            low = at * block + prompt * LEN
+            live = position < length_ref[low // LEN]
+            piece = total[prompt * LEN : (prompt + 1) * LEN, :]
+            out_ref[pl.ds(low, LEN), :] = jnp.where(live, piece, 0.0)
+
+
+def base_rows(lengths, keep, arrived, code):
     return pl.pallas_call(
         base_kernel,
         out_shape=VMEM(keep.shape, F32),
-        in_specs=[whole_block()] * 3,
+        in_specs=[whole_block(pltpu.SMEM)] + [whole_block()] * 3,
         out_specs=whole_block(),
         compiler_params=pltpu.CompilerParams(vmem_limit_bytes=LIMIT),
         cost_estimate=SMALL,
         name="base_rows",
-    )(keep, arrived, code)
-
-
-def shrink_kernel(tokens_ref, chosen_ref, *refs):
-    messages, out_ref, stacked = refs[:-2], refs[-2], refs[-1]
+    )(lengths, keep, arrived, code)
+
+
+def shrink_kernel(start, stacking, tokens_ref, chosen_ref, *refs):
+    if stacking:
+        messages, (out_ref, stacked) = refs[:-2], refs[-2:]
+    else:
+        stacked, out_ref = refs
     rows, row_total = out_ref.shape
     features = tokens_ref.shape[1]
+    count = stacked.shape[0] // rows
     block = 256
-    for at, message in enumerate(messages):
-        stacked[pl.ds(at * rows, rows), :] = message[:, :features]
+    if stacking:
+        for at, message in enumerate(messages):
+            stacked[pl.ds(at * rows, rows), :] = message[:, :features]
     for low in range(0, row_total, block):
-        span = pl.ds(low, block)
+        span = pl.ds(start + low, block)
         sums = lax.dot_general(
             tokens_ref[span, :], stacked[...], (((1,), (1,)), ((), ())), preferred_element_type=F32
         ).T
         asked = chosen_ref[:, span] > 0
         total = None
-        for at in range(len(messages)):
+        for at in range(count):
             term = jnp.where(asked[at : at + 1, :], sums[at * rows : (at + 1) * rows, :], 0.0)
             total = term if total is None else total + term
-        out_ref[:, span] = total
-
-
-def shrink(tokens, chosen, messages):
-    row_total, features = tokens.shape
-    count = len(messages)
-    rows = messages[0].shape[0]
-    return pl.pallas_call(
-        shrink_kernel,
-        out_shape=jax.ShapeDtypeStruct((rows, row_total), F32),
-        in_specs=[whole_block()] * (2 + count),
-        out_specs=whole_block(),
-        scratch_shapes=[VMEM((count * rows, features), BF16)],
+        out_ref[:, pl.ds(low, block)] = total
+
+
+def shrink(tokens, chosen, factors, rows, start, row_total):
+    features = tokens.shape[1]
+    stacking = start == 0
+    out_shape = [jax.ShapeDtypeStruct((rows, row_total), F32)]
+    if stacking:
+        out_shape.append(VMEM((len(factors) * rows, features), BF16))
+    return pl.pallas_call(
+        functools.partial(shrink_kernel, start, stacking),
+        out_shape=out_shape,
+        in_specs=[whole_block()] * (2 + len(factors)),
+        out_specs=[whole_block()] * len(out_shape),
         compiler_params=pltpu.CompilerParams(vmem_limit_bytes=LIMIT),
         cost_estimate=SMALL,
         name="shrink",
-    )(tokens, chosen, *messages)
+    )(tokens, chosen, *factors)
 
 
 def shrunk_code_kernel(keep_ref, arrived_ref, total_ref, code_ref):
@@ -357,10 +356,12 @@
     )(keep, arrived)
 
 
-def finish_kernel(crossing, features, length_ref, base_ref, mask_ref, part_ref, *refs):
+def finish_kernel(start, crossing, features, base_ref, mask_ref, part_ref, *refs):
     if crossing:
         code_ref, *refs = refs
-    messages, out_ref, stacked = refs[:-2], refs[-2], refs[-1]
+    if start:
+        refs = refs[1:]
+    messages, (out_hbm, out_ref, stacked, sem) = refs[:-4], refs[-4:]
     rows = part_ref.shape[0]
     for at, message in enumerate(messages):
         factor = message[:, features:]
@@ -368,38 +369,49 @@
         stacked[pl.ds((2 * at + 1) * rows, rows), :] = factor
     row_total, columns = out_ref.shape
     block = 256
-    position = lax.broadcasted_iota(jnp.int32, (LEN, columns), 0)
+    copies = []
     for low in range(0, row_total, block):
-        span = pl.ds(low, block)
-        shrunk = part_ref[:, span]
+        here = pl.ds(low, block)
+        span = pl.ds(start + low, block)
+        shrunk = part_ref[:, here]
         if crossing:
-            size = size_of(code_ref[pl.ds(rows, 16), span].astype(jnp.int32).astype(F32)[:1, :])
-            shrunk = shrunk + code_ref[pl.ds(0, rows), span].astype(jnp.int32).astype(F32) * size
+            size = size_of(code_ref[pl.ds(rows, 16), here].astype(jnp.int32).astype(F32)[:1, :])
+            shrunk = shrunk + code_ref[pl.ds(0, rows), here].astype(jnp.int32).astype(F32) * size
         high = shrunk.astype(BF16).astype(F32)
         both = jnp.concatenate([high, shrunk - high], axis=0).T.astype(BF16)
         spread = jnp.concatenate([both] * len(messages), axis=1) * mask_ref[span, :]
         total = base_ref[span, :] + jnp.dot(spread, stacked[...], preferred_element_type=F32)
-        for prompt in range(block // LEN):
-            piece = total[prompt * LEN : (prompt + 1) * LEN, :]
-            live = position < length_ref[low // LEN + prompt]
-            out_ref[pl.ds(low + prompt * LEN, LEN), :] = jnp.where(live, piece, 0.0).astype(BF16)
-
-
-def finish(lengths, base, mask, part, code, messages, features):
-    row_total, columns = base.shape
+        out_ref[here, :] = total.astype(BF16)
+        copies.append(pltpu.make_async_copy(out_ref.at[here, :], out_hbm.at[span, :], sem.at[low // block]))
+        copies[-1].start()
+    for copy in copies:
+        copy.wait()
+
+
+def finish(base, mask, part, code, earlier, messages, features, start):
+    columns = base.shape[1]
     count = len(messages)
-    rows = messages[0].shape[0]
-    operands = [base, mask, part, *code, *messages]
-    return pl.pallas_call(
-        functools.partial(finish_kernel, bool(code), features),
-        out_shape=jax.ShapeDtypeStruct((row_total, columns), BF16),
-        in_specs=[whole_block(pltpu.SMEM)] + [whole_block()] * len(operands),
-        out_specs=whole_block(),
-        scratch_shapes=[VMEM((2 * count * rows, columns), BF16)],
+    rows, row_total = part.shape
+    operands = [base, mask, part, *code, *earlier, *messages]
+    hbm = whole_block(pl.ANY)
+    in_specs = [whole_block()] * (3 + len(code))
+    aliases = {len(in_specs): 0} if earlier else {}
+    in_specs += [hbm] * len(earlier) + [whole_block()] * count
+    return pl.pallas_call(
+        functools.partial(finish_kernel, start, bool(code), features),
+        out_shape=jax.ShapeDtypeStruct(base.shape, BF16),
+        in_specs=in_specs,
+        out_specs=hbm,
+        input_output_aliases=aliases,
+        scratch_shapes=[
+            VMEM((row_total, columns), BF16),
+            VMEM((2 * count * rows, columns), BF16),
+            pltpu.SemaphoreType.DMA((row_total // 256,)),
+        ],
         compiler_params=pltpu.CompilerParams(vmem_limit_bytes=LIMIT),
         cost_estimate=SMALL,
         name="finish",
-    )(lengths, *operands)
+    )(*operands)
 
 
 def on_device(
@@ -446,29 +458,45 @@
     )
     granted = first % owner_portion
     chosen_prompt = (matches & (local == granted[:, None])).astype(F32)
-    chosen = jnp.repeat(chosen_prompt, LEN, axis=1)
+    inside = jnp.arange(LEN, dtype=jnp.int32)[None, :] < my_lengths[:, None]
+    chosen = jnp.where(inside[None], chosen_prompt[:, :, None], 0.0).reshape(wide_count, row_total)
 
     if paired:
         core = [(at, at ^ 1) for at in range(4)]
         across = [(at, at ^ 2) for at in range(4)]
         ticket = lax.ppermute(ticket, "narrow", core)
         far_send, far_keep, held_tokens = column_dots(tokens, value_weight, ticket, columns, True)
-        code = code_rows(far_keep, lax.ppermute(far_send, "narrow", core))
+        far_arrived = lax.ppermute(far_send, "narrow", core)
+        code = code_rows(in_vmem(far_keep), in_vmem(far_arrived))
         near_send, near_keep = column_dots(held_tokens, value_weight, far_keep, columns, False)
         resident, mask = reload_tokens(tokens, chosen, near_keep)
         base = base_rows(
-            near_keep, lax.ppermute(near_send, "narrow", core), lax.ppermute(code, "narrow", across)
+            my_lengths,
+            near_keep,
+            lax.ppermute(near_send, "narrow", core),
+            lax.ppermute(code, "narrow", across),
         )
-        part = shrink(resident, chosen, held[0])
-        part, shrunk_code = code_shrunk(part, lax.ppermute(part, "narrow", core))
-        crossed = [lax.ppermute(shrunk_code, "narrow", across)]
+        pieces = 2
     else:
         partial_value = jnp.dot(tokens, value_weight, preferred_element_type=F32)
         base = lax.psum_scatter(partial_value, "narrow", scatter_dimension=1, tiled=True)
+        base = jnp.where(inside.reshape(row_total, 1), base, 0.0)
         resident, mask = reload_tokens(tokens, chosen, ticket)
-        part = lax.psum(shrink(resident, chosen, held[0]), "narrow")
+        pieces = 1
+    rows = adapter_down_factors.shape[2]
+    piece = row_total // pieces
+    factors, values = held[0], []
+    for start in range(0, row_total, piece):
+        part, *stacked = shrink(resident, chosen, factors, rows, start, piece)
+        factors = stacked or factors
         crossed = []
-    return finish(my_lengths, base, mask, part, crossed, held[0], features)
+        if paired:
+            part, shrunk_code = code_shrunk(part, lax.ppermute(part, "narrow", core))
+            crossed = [lax.ppermute(shrunk_code, "narrow", across)]
+        else:
+            part = lax.psum(part, "narrow")
+        values = [finish(base, mask, part, crossed, values, held[0], features, start)]
+    return values[0]
 
 
 def solution(mesh):

time: 43.3 us -> 42.7 us (0.986)
  the two profiles are of different devices: /device:TPU:9 before, /device:TPU:0 now
where the time goes in v6:
time: 42.7 us; the launch traced here: 42.4 us
  Pallas kernels  21.2 us (50%)
  starting transfers between devices  12.3 us (29%)
  waiting for transfers between devices  6.4 us (15%)
  local copies, waits for them, and re-layouts  1.26 us (3%)
  other arithmetic  1.05 us (2%)
    pallas_call x2, Pallas kernels, column_dots(): pl.pallas_call(far_kernel if far else near_kernel, out_shape=out_shape, i...  8.79 us
    ppermute x3, starting transfers between devices, on_device(): held[chunk].append(lax.ppermute(sent[shift][chunk], 'wide', ring))  6.57 us
    ppermute x1, waiting for transfers between devices, on_device(): lax.ppermute(code, 'narrow', across)  5.47 us
    ppermute x2, starting transfers between devices, on_device(): crossed = [lax.ppermute(shrunk_code, 'narrow', across)]  2.49 us
    pallas_call x1, Pallas kernels, code_rows(): pl.pallas_call(code_kernel, out_shape=VMEM((row_total + 16, columns), jnp...  2.44 us
    pallas_call x1, Pallas kernels, pack_messages(): pl.pallas_call(functools.partial(pack_kernel, wide_count, per_device), ou...  2.2 us
    pallas_call x1, Pallas kernels, reload_tokens(): pl.pallas_call(reload_kernel, out_shape=[VMEM(tokens.shape, BF16), VMEM((...  2.2 us
    pallas_call x2, Pallas kernels, finish(): pl.pallas_call(functools.partial(finish_kernel, start, bool(code), featur...  2.17 us
  transfers between devices with their start and end apart: 11, of which 3 were waited for; matrix products, arithmetic and copies ran while one was open for 5% of the time, Pallas kernels for 42%

profile of v6, /device:TPU:0, one launch (start us, length us, event | category | flops | bytes accessed | tf_op | source)
XLA Modules:
  0.0 42.4 jit_solution(10601207431063518252)
XLA Ops:
  0.0 2.2 %pack_messages.1 = (bf16[64,2304]{1,0:T(8,128)(2,1)}, bf16[64,2304]{1,0:T(8,128)(2,1)}, bf16[64,2304]{1,0:T(8,128)(2,1)}, bf16[64,2304]{1,0:T(8,128)(2,1)}, f32[8,128]{1,0:T(8,128)S(1)}) custom-call(s32[1,128]{1,0:T(1,128)} %bitcast.5, s32[1,128]{1,0:T(1,128)} %bitcast.4, bf16[2,64,2048]{2,1,0:T(8,128)(2,1)} %bitcast.3, bf16[2,64,256]{2,1,0:T(8,128)(2,1)} %refs_3_.1), custom_call_target="tpu_custom_call" | custom-call | flops 1 | bytes 1 | tf_op jit(solution)/shard_map/pack_messages/pallas_call | solution.py:115
  2.2 0.5 %collective-permute-start = (f32[8,128]{1,0:T(8,128)S(1)}, f32[8,128]{1,0:T(8,128)S(1)}, u32[]{:S(2)}, u32[]{:S(2)}) collective-permute-start(f32[8,128]{1,0:T(8,128)S(1)} %get-tuple-element.23), channel_id=1, source_target_pairs={{0,1},{1,0},{2,3},{3,2},{4,5},{5,4},{6,7},{7,6},{8,9},{9,8},{10,11... | collective-permute-start | bytes 12296 | tf_op jit(solution)/shard_map/ppermute | solution.py:467
  2.7 2.6 %collective-permute-start.4 = (bf16[64,2304]{1,0:T(8,128)(2,1)}, bf16[64,2304]{1,0:T(8,128)(2,1)S(1)}, u32[]{:S(2)}, u32[]{:S(2)}) collective-permute-start(bf16[64,2304]{1,0:T(8,128)(2,1)} %get-tuple-element.32), channel_id=1, source_target_pairs={{0,4},{4,8},{8,12},{12,0},{1,5},{5,9},{9,13},{13,1},{2,6},{6,10},{... | collective-permute-start | bytes 884744 | tf_op jit(solution)/shard_map/ppermute | solution.py:447
  5.4 2.6 %collective-permute-start.5 = (bf16[64,2304]{1,0:T(8,128)(2,1)}, bf16[64,2304]{1,0:T(8,128)(2,1)S(1)}, u32[]{:S(2)}, u32[]{:S(2)}) collective-permute-start(bf16[64,2304]{1,0:T(8,128)(2,1)} %get-tuple-element.33), channel_id=1, source_target_pairs={{0,8},{4,12},{8,0},{12,4},{1,9},{5,13},{9,1},{13,5},{2,10},{6,14},... | collective-permute-start | bytes 884744 | tf_op jit(solution)/shard_map/ppermute | solution.py:447
  8.0 1.3 %collective-permute-start.6 = (bf16[64,2304]{1,0:T(8,128)(2,1)}, bf16[64,2304]{1,0:T(8,128)(2,1)S(1)}, u32[]{:S(2)}, u32[]{:S(2)}) collective-permute-start(bf16[64,2304]{1,0:T(8,128)(2,1)} %get-tuple-element.34), channel_id=1, source_target_pairs={{0,12},{4,0},{8,4},{12,8},{1,13},{5,1},{9,5},{13,9},{2,14},{6,2},{... | collective-permute-start | bytes 884744 | tf_op jit(solution)/shard_map/ppermute | solution.py:447
  9.3 0.7 %dynamic-slice_compare_fusion = pred[32]{0:T(512)(128)(4,1)S(1)} fusion(s32[128]{0:T(128)} %param.12, s32[]{:T(128)S(6)} %select_n.33), kind=kLoop, calls=%fused_computation.22 | loop fusion | flops 32 | bytes 164 | tf_op jit(solution)/shard_map/eq | solution.py:454
  10.1 0.7 %dynamic_slice.11 = s32[32]{0:T(128)S(1)} dynamic-slice(s32[128]{0:T(128)} %param.11, s32[]{:T(128)S(6)} %select_n.33), dynamic_slice_sizes={32} | dynamic-slice | bytes 260 | tf_op jit(solution)/shard_map/dynamic_slice | solution.py:449
  10.8 0.0 collective-permute-done.ticket_ref
  10.8 5.0 %far_columns.1 = (f32[1024,256]{1,0:T(8,128)}, f32[1024,256]{1,0:T(8,128)S(1)}, bf16[1024,2048]{1,0:T(8,128)(2,1)S(1)}) custom-call(bf16[1024,2048]{1,0:T(8,128)(2,1)} %tokens_hbm.3, bf16[2048,1024]{1,0:T(8,128)(2,1)} %weight_hbm.3, f32[8,128]{1,0:T(8,128)S(1)} %collective-permute-done.ticket_ref), custom_call_target="tpu_custom_call" | custom-call | flops 1 | bytes 1 | tf_op jit(solution)/shard_map/far_columns/pallas_call | solution.py:222
  15.8 0.1 collective-permute-start.2
  15.9 0.0 copy-start.1
  15.9 3.8 %near_columns.1 = (f32[1024,256]{1,0:T(8,128)}, f32[1024,256]{1,0:T(8,128)S(1)}) custom-call(bf16[1024,2048]{1,0:T(8,128)(2,1)S(1)} %get-tuple-element.24.tokens_ref, bf16[2048,1024]{1,0:T(8,128)(2,1)} %weight_hbm.3, f32[1024,256]{1,0:T(8,128)S(1)} %get-tuple-element.25.ticket_ref.keep_ref), custom_call_target="tpu_custom_call" | custom-call | flops 10000000000 | bytes 1 | tf_op jit(solution)/shard_map/near_columns/pallas_call | solution.py:222
  19.7 0.0 copy-start
  19.7 0.6 %collective-permute-start.1 = (f32[1024,256]{1,0:T(8,128)}, f32[1024,256]{1,0:T(8,128)}, u32[]{:S(2)}, u32[]{:S(2)}) collective-permute-start(f32[1024,256]{1,0:T(8,128)} %get-tuple-element.27), channel_id=1, source_target_pairs={{0,1},{1,0},{2,3},{3,2},{4,5},{5,4},{6,7},{7,6},{8,9},{9,8},{10,11... | collective-permute-start | bytes 3145736 | tf_op jit(solution)/shard_map/ppermute | solution.py:476
  20.3 0.2 fusion.1
  20.4 0.0 copy-done.1
  20.4 0.1 dynamic_slice.9.length_ref
  20.5 0.1 fusion.5
  20.6 0.1 broadcast_in_dim.37
  20.7 0.1 broadcast_in_dim.38
  20.8 0.1 lt.48
  20.9 0.0 collective-permute-done.2.arrived_ref
  20.9 2.4 %code_rows.1 = s16[1040,256]{1,0:T(8,128)(2,1)} custom-call(f32[1024,256]{1,0:T(8,128)S(1)} %get-tuple-element.25.ticket_ref.keep_ref, f32[1024,256]{1,0:T(8,128)} %collective-permute-done.2.arrived_ref), custom_call_target="tpu_custom_call" | custom-call | flops 1 | bytes 1 | tf_op jit(solution)/shard_map/code_rows/pallas_call | solution.py:158
  23.3 1.5 %collective-permute-start.3 = (s16[1040,256]{1,0:T(8,128)(2,1)}, s16[1040,256]{1,0:T(8,128)(2,1)S(1)}, u32[]{:S(2)}, u32[]{:S(2)}) collective-permute-start(s16[1040,256]{1,0:T(8,128)(2,1)} %code_rows.1), channel_id=1, source_target_pairs={{0,2},{1,3},{2,0},{3,1},{4,6},{5,7},{6,4},{7,5},{8,10},{9,11},{10,... | collective-permute-start | bytes 1597448 | tf_op jit(solution)/shard_map/ppermute | solution.py:477
  24.8 0.1 broadcast_reduce_fusion
  24.9 0.1 lt.50
  25.0 2.2 %reload_tokens.1 = (bf16[1024,2048]{1,0:T(8,128)(2,1)S(1)}, bf16[1024,512]{1,0:T(8,128)(2,1)S(1)}) custom-call(bf16[1024,2048]{1,0:T(8,128)(2,1)} %tokens_hbm.3, f32[4,1024]{1,0:T(4,128)S(1)} %broadcast_select_fusion.chosen_ref, f32[1024,256]{1,0:T(8,128)S(1)} %get-tuple-element.26.keep_ref.ticket_ref), custom_call_target="tpu_custom_call" | custom-call | flops 1 | bytes 1 | tf_op jit(solution)/shard_map/reload_tokens/pallas_call | solution.py:248
  27.2 0.0 collective-permute-done.4.refs_1_.refs_2_.refs_3_
  27.2 0.7 %collective-permute-done.5.refs_2_.refs_3_.refs_4_ = bf16[64,2304]{1,0:T(8,128)(2,1)S(1)} collective-permute-done((bf16[64,2304]{1,0:T(8,128)(2,1)}, bf16[64,2304]{1,0:T(8,128)(2,1)S(1)}, u32[]{:S(2)}, u32[]{:S(2)}) %collective-permute-start.5) | collective-permute-done | bytes 294944 | tf_op jit(solution)/shard_map/ppermute | solution.py:447
  28.0 0.0 collective-permute-done.6.refs_3_.refs_4_.refs_5_
  28.0 0.0 copy-done
  28.0 0.9 %shrink.2 = (f32[64,512]{1,0:T(8,128)S(1)}, bf16[256,2048]{1,0:T(8,128)(2,1)S(1)}) custom-call(bf16[1024,2048]{1,0:T(8,128)(2,1)S(1)} %get-tuple-element.30.tokens_ref, f32[4,1024]{1,0:T(4,128)S(1)} %broadcast_select_fusion.chosen_ref, bf16[64,2304]{1,0:T(8,128)(2,1)S(1)} %copy-done, bf16[64,2304]{1,0:T(8,128)(2,1)S(1)} %collective-permute-done.4.refs_1_.refs_2_.refs_3_, ...), custom_call_target="tpu_custom_call" | custom-call | flops 1 | bytes 1 | tf_op jit(solution)/shard_map/shrink/pallas_call | solution.py:322
  28.9 0.1 collective-permute-start.9
  28.9 0.9 %shrink.3.keep_ref = f32[64,512]{1,0:T(8,128)S(1)} custom-call(bf16[1024,2048]{1,0:T(8,128)(2,1)S(1)} %get-tuple-element.30.tokens_ref, f32[4,1024]{1,0:T(4,128)S(1)} %broadcast_select_fusion.chosen_ref, bf16[256,2048]{1,0:T(8,128)(2,1)S(1)} %get-tuple-element.35.refs_0_), custom_call_target="tpu_custom_call" | custom-call | flops 1 | bytes 1 | tf_op jit(solution)/shard_map/shrink/pallas_call | solution.py:322
  29.8 0.6 %collective-permute-start.7 = (f32[64,512]{1,0:T(8,128)S(1)}, f32[64,512]{1,0:T(8,128)S(1)}, u32[]{:S(2)}, u32[]{:S(2)}) collective-permute-start(f32[64,512]{1,0:T(8,128)S(1)} %shrink.3.keep_ref), channel_id=1, source_target_pairs={{0,1},{1,0},{2,3},{3,2},{4,5},{5,4},{6,7},{7,6},{8,9},{9,8},{10,11... | collective-permute-start | bytes 393224 | tf_op jit(solution)/shard_map/ppermute | solution.py:494
  30.4 0.0 collective-permute-done.9.arrived_ref
  30.4 0.1 code_shrunk.3
  30.5 1.6 %collective-permute-start.10 = (s16[80,512]{1,0:T(8,128)(2,1)S(1)}, s16[80,512]{1,0:T(8,128)(2,1)S(1)}, u32[]{:S(2)}, u32[]{:S(2)}) collective-permute-start(s16[80,512]{1,0:T(8,128)(2,1)S(1)} %get-tuple-element.40), channel_id=1, source_target_pairs={{0,2},{1,3},{2,0},{3,1},{4,6},{5,7},{6,4},{7,5},{8,10},{9,11},{10,... | collective-permute-start | bytes 245768 | tf_op jit(solution)/shard_map/ppermute | solution.py:495
  32.0 0.0 collective-permute-done.7.arrived_ref
  32.0 0.1 code_shrunk.2
  32.1 0.9 %collective-permute-start.8 = (s16[80,512]{1,0:T(8,128)(2,1)S(1)}, s16[80,512]{1,0:T(8,128)(2,1)S(1)}, u32[]{:S(2)}, u32[]{:S(2)}) collective-permute-start(s16[80,512]{1,0:T(8,128)(2,1)S(1)} %get-tuple-element.37), channel_id=1, source_target_pairs={{0,2},{1,3},{2,0},{3,1},{4,6},{5,7},{6,4},{7,5},{8,10},{9,11},{10,... | collective-permute-start | bytes 245768 | tf_op jit(solution)/shard_map/ppermute | solution.py:495
  33.0 0.0 collective-permute-done.1.arrived_ref
  33.0 5.5 %collective-permute-done.3.code_ref = s16[1040,256]{1,0:T(8,128)(2,1)S(1)} collective-permute-done((s16[1040,256]{1,0:T(8,128)(2,1)}, s16[1040,256]{1,0:T(8,128)(2,1)S(1)}, u32[]{:S(2)}, u32[]{:S(2)}) %collective-permute-start.3) | collective-permute-done | bytes 532512 | tf_op jit(solution)/shard_map/ppermute | solution.py:477
  38.5 1.5 %base_rows.1.base_ref = f32[1024,256]{1,0:T(8,128)S(1)} custom-call(s32[32]{0:T(128)S(1)} %dynamic_slice.9.length_ref, f32[1024,256]{1,0:T(8,128)S(1)} %get-tuple-element.26.keep_ref.ticket_ref, f32[1024,256]{1,0:T(8,128)} %collective-permute-done.1.arrived_ref, s16[1040,256]{1,0:T(8,128)(2,1)S(1)} %collective-permute-done.3.code_ref), custom_call_target="tpu_custom_call" | custom-call | flops 1 | bytes 1 | tf_op jit(solution)/shard_map/base_rows/pallas_call | solution.py:280
  40.0 0.2 collective-permute-done.10.refs_0_
  40.2 1.1 %finish.2.refs_1_ = bf16[1024,256]{1,0:T(8,128)(2,1)} custom-call(f32[1024,256]{1,0:T(8,128)S(1)} %base_rows.1.base_ref, bf16[1024,512]{1,0:T(8,128)(2,1)S(1)} %get-tuple-element.29.mask_ref, f32[64,512]{1,0:T(8,128)S(1)} %get-tuple-element.39.part_ref, s16[80,512]{1,0:T(8,128)(2,1)S(1)} %collective-permute-done.10.refs_0_, bf16[64,2304]{1,0:T(8,128)(2,1)S(1)} %copy-done, ...), custom_call_target="tpu_custom_call" | custom-call | flops 1 | bytes 1 | tf_op jit(solution)/shard_map/finish/pallas_call | solution.py:400
  41.3 0.0 collective-permute-done.8.refs_0_
  41.3 1.1 %finish.3 = bf16[1024,256]{1,0:T(8,128)(2,1)} custom-call(f32[1024,256]{1,0:T(8,128)S(1)} %base_rows.1.base_ref, bf16[1024,512]{1,0:T(8,128)(2,1)S(1)} %get-tuple-element.29.mask_ref, f32[64,512]{1,0:T(8,128)S(1)} %get-tuple-element.36.part_ref, s16[80,512]{1,0:T(8,128)(2,1)S(1)} %collective-permute-done.8.refs_0_, ...), custom_call_target="tpu_custom_call", output_to_operand_aliasing={{}: (4, {})} | custom-call | flops 1 | bytes 1 | tf_op jit(solution)/shard_map/finish/pallas_call | solution.py:400
  (6 shorter events, 0.0 us)
Async XLA Ops:
  2.2 8.6 %collective-permute-start = (f32[8,128]{1,0:T(8,128)S(1)}, f32[8,128]{1,0:T(8,128)S(1)}, u32[]{:S(2)}, u32[]{:S(2)}) collective-permute-start(f32[8,128]{1,0:T(8,128)S(1)} %get-tuple-element.23), channel_id=1, source_target_pairs={{0,1},{1,0},{2,3},{3,2},{4,5},{5,4},{6,7},{7,6},{8,9},{9,8},{10,11... | collective-permute-start | bytes 12296 | tf_op jit(solution)/shard_map/ppermute | solution.py:467
  2.7 24.5 %collective-permute-start.4 = (bf16[64,2304]{1,0:T(8,128)(2,1)}, bf16[64,2304]{1,0:T(8,128)(2,1)S(1)}, u32[]{:S(2)}, u32[]{:S(2)}) collective-permute-start(bf16[64,2304]{1,0:T(8,128)(2,1)} %get-tuple-element.32), channel_id=1, source_target_pairs={{0,4},{4,8},{8,12},{12,0},{1,5},{5,9},{9,13},{13,1},{2,6},{6,10},{... | collective-permute-start | bytes 884744 | tf_op jit(solution)/shard_map/ppermute | solution.py:447
  5.4 22.6 %collective-permute-start.5 = (bf16[64,2304]{1,0:T(8,128)(2,1)}, bf16[64,2304]{1,0:T(8,128)(2,1)S(1)}, u32[]{:S(2)}, u32[]{:S(2)}) collective-permute-start(bf16[64,2304]{1,0:T(8,128)(2,1)} %get-tuple-element.33), channel_id=1, source_target_pairs={{0,8},{4,12},{8,0},{12,4},{1,9},{5,13},{9,1},{13,5},{2,10},{6,14},... | collective-permute-start | bytes 884744 | tf_op jit(solution)/shard_map/ppermute | solution.py:447
  8.0 20.0 %collective-permute-start.6 = (bf16[64,2304]{1,0:T(8,128)(2,1)}, bf16[64,2304]{1,0:T(8,128)(2,1)S(1)}, u32[]{:S(2)}, u32[]{:S(2)}) collective-permute-start(bf16[64,2304]{1,0:T(8,128)(2,1)} %get-tuple-element.34), channel_id=1, source_target_pairs={{0,12},{4,0},{8,4},{12,8},{1,13},{5,1},{9,5},{13,9},{2,14},{6,2},{... | collective-permute-start | bytes 884744 | tf_op jit(solution)/shard_map/ppermute | solution.py:447
  15.8 5.1 %collective-permute-start.2 = (f32[1024,256]{1,0:T(8,128)}, f32[1024,256]{1,0:T(8,128)}, u32[]{:S(2)}, u32[]{:S(2)}) collective-permute-start(f32[1024,256]{1,0:T(8,128)} %get-tuple-element.28), channel_id=1, source_target_pairs={{0,1},{1,0},{2,3},{3,2},{4,5},{5,4},{6,7},{7,6},{8,9},{9,8},{10,11... | collective-permute-start | bytes 3145736 | tf_op jit(solution)/shard_map/ppermute | solution.py:469
  15.9 4.5 %copy-start.1 = (s32[128]{0:T(128)S(1)}, s32[128]{0:T(128)}, u32[]{:S(2)}) copy-start(s32[128]{0:T(128)} %param.13) | copy-start | bytes 1540
  19.7 8.3 %copy-start = (bf16[64,2304]{1,0:T(8,128)(2,1)S(1)}, bf16[64,2304]{1,0:T(8,128)(2,1)}, u32[]{:S(2)}) copy-start(bf16[64,2304]{1,0:T(8,128)(2,1)} %get-tuple-element.31.refs_0_.refs_1_.refs_2_) | copy-start | bytes 884740
  19.7 13.3 %collective-permute-start.1 = (f32[1024,256]{1,0:T(8,128)}, f32[1024,256]{1,0:T(8,128)}, u32[]{:S(2)}, u32[]{:S(2)}) collective-permute-start(f32[1024,256]{1,0:T(8,128)} %get-tuple-element.27), channel_id=1, source_target_pairs={{0,1},{1,0},{2,3},{3,2},{4,5},{5,4},{6,7},{7,6},{8,9},{9,8},{10,11... | collective-permute-start | bytes 3145736 | tf_op jit(solution)/shard_map/ppermute | solution.py:476
  23.3 15.2 %collective-permute-start.3 = (s16[1040,256]{1,0:T(8,128)(2,1)}, s16[1040,256]{1,0:T(8,128)(2,1)S(1)}, u32[]{:S(2)}, u32[]{:S(2)}) collective-permute-start(s16[1040,256]{1,0:T(8,128)(2,1)} %code_rows.1), channel_id=1, source_target_pairs={{0,2},{1,3},{2,0},{3,1},{4,6},{5,7},{6,4},{7,5},{8,10},{9,11},{10,... | collective-permute-start | bytes 1597448 | tf_op jit(solution)/shard_map/ppermute | solution.py:477
  28.9 1.5 %collective-permute-start.9 = (f32[64,512]{1,0:T(8,128)S(1)}, f32[64,512]{1,0:T(8,128)S(1)}, u32[]{:S(2)}, u32[]{:S(2)}) collective-permute-start(f32[64,512]{1,0:T(8,128)S(1)} %get-tuple-element.38.keep_ref), channel_id=1, source_target_pairs={{0,1},{1,0},{2,3},{3,2},{4,5},{5,4},{6,7},{7,6},{8,9},{9,8},{10,11... | collective-permute-start | bytes 393224 | tf_op jit(solution)/shard_map/ppermute | solution.py:494
  29.8 2.2 %collective-permute-start.7 = (f32[64,512]{1,0:T(8,128)S(1)}, f32[64,512]{1,0:T(8,128)S(1)}, u32[]{:S(2)}, u32[]{:S(2)}) collective-permute-start(f32[64,512]{1,0:T(8,128)S(1)} %shrink.3.keep_ref), channel_id=1, source_target_pairs={{0,1},{1,0},{2,3},{3,2},{4,5},{5,4},{6,7},{7,6},{8,9},{9,8},{10,11... | collective-permute-start | bytes 393224 | tf_op jit(solution)/shard_map/ppermute | solution.py:494
  30.5 9.7 %collective-permute-start.10 = (s16[80,512]{1,0:T(8,128)(2,1)S(1)}, s16[80,512]{1,0:T(8,128)(2,1)S(1)}, u32[]{:S(2)}, u32[]{:S(2)}) collective-permute-start(s16[80,512]{1,0:T(8,128)(2,1)S(1)} %get-tuple-element.40), channel_id=1, source_target_pairs={{0,2},{1,3},{2,0},{3,1},{4,6},{5,7},{6,4},{7,5},{8,10},{9,11},{10,... | collective-permute-start | bytes 245768 | tf_op jit(solution)/shard_map/ppermute | solution.py:495
  32.1 9.2 %collective-permute-start.8 = (s16[80,512]{1,0:T(8,128)(2,1)S(1)}, s16[80,512]{1,0:T(8,128)(2,1)S(1)}, u32[]{:S(2)}, u32[]{:S(2)}) collective-permute-start(s16[80,512]{1,0:T(8,128)(2,1)S(1)} %get-tuple-element.37), channel_id=1, source_target_pairs={{0,2},{1,3},{2,0},{3,1},{4,6},{5,7},{6,4},{7,5},{8,10},{9,11},{10,... | collective-permute-start | bytes 245768 | tf_op jit(solution)/shard_map/ppermute | solution.py:495

commit v7 on v6

--- a/solution.py
+++ b/solution.py
@@ -46,17 +46,17 @@
 
 def pack_kernel(wide_count, per_device, *refs):
     message_count = wide_count * CHUNKS
-    loads_in, refs = refs[:4], refs[4:]
+    loads_in, refs = refs[:5], refs[5:]
     messages, refs = refs[:message_count], refs[message_count:]
-    ticket_ref, refs = refs[0], refs[1:]
+    ticket_ref, settings_ref, *refs = refs
     ticket_ref[...] = jnp.zeros_like(ticket_ref)
-    choice_ref, mask_ref, down_ref, up_ref, load_sem, message_sem = refs[:6]
+    choice_ref, mask_ref, down_ref, up_ref, length_ref, load_sem, message_sem = refs
     owner_portion, rank, features = down_ref.shape
     columns = up_ref.shape[2]
     rows = rank // CHUNKS
     loads = [
         pltpu.make_async_copy(source, target, load_sem.at[at])
-        for at, (source, target) in enumerate(zip(loads_in, refs[:4]))
+        for at, (source, target) in enumerate(zip(loads_in, refs[:5]))
     ]
     for copy in loads:
         copy.start()
@@ -97,21 +97,24 @@
     loads[3].wait()
     for copy in copies:
         copy.start()
+    loads[4].wait()
+    for at, source in enumerate((choice_ref, mask_ref, length_ref)):
+        settings_ref[pl.ds(at, 1), :] = source[...]
     for copy in copies:
         copy.wait()
 
 
-def pack_messages(choice, mask, down, up, wide_count, per_device):
+def pack_messages(choice, mask, lengths, down, up, wide_count, per_device):
     rank, features = down.shape[1:]
     columns = up.shape[2]
     count = wide_count * CHUNKS
     hbm = whole_block(pl.ANY)
-    operands = [choice, mask, down, up]
+    operands = [choice, mask, down, up, lengths]
     scratch = [VMEM(operand.shape, operand.dtype) for operand in operands]
-    scratch += [pltpu.SemaphoreType.DMA((4,)), pltpu.SemaphoreType.DMA((2 * count,))]
+    scratch += [pltpu.SemaphoreType.DMA((5,)), pltpu.SemaphoreType.DMA((2 * count,))]
     out_shape = [pltpu.HBM((rank // CHUNKS, features + columns), BF16)] * count
-    out_specs = [hbm] * count + [whole_block()]
-    out_shape += [jax.ShapeDtypeStruct((8, 128), F32)]
+    out_specs = [hbm] * count + [whole_block()] * 2
+    out_shape += [jax.ShapeDtypeStruct((8, 128), F32), jax.ShapeDtypeStruct((3, choice.shape[1]), jnp.int32)]
     out = pl.pallas_call(
         functools.partial(pack_kernel, wide_count, per_device),
         out_shape=out_shape,
@@ -122,7 +125,7 @@
         cost_estimate=SMALL,
         name="pack_messages",
     )(*[in_hbm(operand) for operand in operands])
-    return [out[shift * CHUNKS : (shift + 1) * CHUNKS] for shift in range(wide_count)], out[-1]
+    return [out[shift * CHUNKS : (shift + 1) * CHUNKS] for shift in range(wide_count)], *out[count:]
 
 
 def grade_of(size):
@@ -288,7 +291,14 @@
     )(lengths, keep, arrived, code)
 
 
-def shrink_kernel(start, stacking, tokens_ref, chosen_ref, *refs):
+def piece_start(kind, length):
+    if kind == 0:
+        return 0
+    mine = lax.rem(lax.axis_index("narrow"), 2)
+    return pl.multiple_of((mine if kind == 1 else 1 - mine) * length, length)
+
+
+def shrink_kernel(kind, stacking, tokens_ref, chosen_ref, *refs):
     if stacking:
         messages, (out_ref, stacked) = refs[:-2], refs[-2:]
     else:
@@ -297,11 +307,12 @@
     features = tokens_ref.shape[1]
     count = stacked.shape[0] // rows
     block = 256
+    start = piece_start(kind, row_total)
     if stacking:
         for at, message in enumerate(messages):
             stacked[pl.ds(at * rows, rows), :] = message[:, :features]
     for low in range(0, row_total, block):
-        span = pl.ds(start + low, block)
+        span = pl.ds(pl.multiple_of(start + low, block), block)
         sums = lax.dot_general(
             tokens_ref[span, :], stacked[...], (((1,), (1,)), ((), ())), preferred_element_type=F32
         ).T
@@ -313,14 +324,14 @@
         out_ref[:, pl.ds(low, block)] = total
 
 
-def shrink(tokens, chosen, factors, rows, start, row_total):
+def shrink(tokens, chosen, factors, rows, kind, row_total):
     features = tokens.shape[1]
-    stacking = start == 0
+    stacking = len(factors) > 1
     out_shape = [jax.ShapeDtypeStruct((rows, row_total), F32)]
     if stacking:
         out_shape.append(VMEM((len(factors) * rows, features), BF16))
     return pl.pallas_call(
-        functools.partial(shrink_kernel, start, stacking),
+        functools.partial(shrink_kernel, kind, stacking),
         out_shape=out_shape,
         in_specs=[whole_block()] * (2 + len(factors)),
         out_specs=[whole_block()] * len(out_shape),
@@ -356,10 +367,26 @@
     )(keep, arrived)
 
 
-def finish_kernel(start, crossing, features, base_ref, mask_ref, part_ref, *refs):
-    if crossing:
-        code_ref, *refs = refs
-    if start:
+def sum_kernel(total_ref, code_ref, ticket_ref, out_ref):
+    rows = total_ref.shape[0]
+    size = size_of(code_ref[pl.ds(rows, 16), :].astype(jnp.int32).astype(F32)[:1, :])
+    out_ref[...] = total_ref[...] + code_ref[pl.ds(0, rows), :].astype(jnp.int32).astype(F32) * size
+
+
+def sum_shrunk(total, code, ticket):
+    return pl.pallas_call(
+        sum_kernel,
+        out_shape=jax.ShapeDtypeStruct(total.shape, F32),
+        in_specs=[whole_block()] * 2 + [whole_block(pl.ANY)],
+        out_specs=whole_block(),
+        compiler_params=pltpu.CompilerParams(vmem_limit_bytes=LIMIT),
+        cost_estimate=SMALL,
+        name="sum_shrunk",
+    )(total, code, ticket)
+
+
+def finish_kernel(kind, features, base_ref, mask_ref, part_ref, *refs):
+    if kind == 2:
         refs = refs[1:]
     messages, (out_hbm, out_ref, stacked, sem) = refs[:-4], refs[-4:]
     rows = part_ref.shape[0]
@@ -369,14 +396,12 @@
         stacked[pl.ds((2 * at + 1) * rows, rows), :] = factor
     row_total, columns = out_ref.shape
     block = 256
+    start = piece_start(kind, row_total)
     copies = []
     for low in range(0, row_total, block):
         here = pl.ds(low, block)
-        span = pl.ds(start + low, block)
+        span = pl.ds(pl.multiple_of(start + low, block), block)
         shrunk = part_ref[:, here]
-        if crossing:
-            size = size_of(code_ref[pl.ds(rows, 16), here].astype(jnp.int32).astype(F32)[:1, :])
-            shrunk = shrunk + code_ref[pl.ds(0, rows), here].astype(jnp.int32).astype(F32) * size
         high = shrunk.astype(BF16).astype(F32)
         both = jnp.concatenate([high, shrunk - high], axis=0).T.astype(BF16)
         spread = jnp.concatenate([both] * len(messages), axis=1) * mask_ref[span, :]
@@ -388,17 +413,17 @@
         copy.wait()
 
 
-def finish(base, mask, part, code, earlier, messages, features, start):
+def finish(base, mask, part, earlier, messages, features, kind):
     columns = base.shape[1]
     count = len(messages)
     rows, row_total = part.shape
-    operands = [base, mask, part, *code, *earlier, *messages]
+    operands = [base, mask, part, *earlier, *messages]
     hbm = whole_block(pl.ANY)
-    in_specs = [whole_block()] * (3 + len(code))
+    in_specs = [whole_block()] * 3
     aliases = {len(in_specs): 0} if earlier else {}
     in_specs += [hbm] * len(earlier) + [whole_block()] * count
     return pl.pallas_call(
-        functools.partial(finish_kernel, start, bool(code), features),
+        functools.partial(finish_kernel, kind, features),
         out_shape=jax.ShapeDtypeStruct(base.shape, BF16),
         in_specs=in_specs,
         out_specs=hbm,
@@ -432,9 +457,10 @@
     columns = adapter_up_factors.shape[2]
 
     paired = narrow_count == 4
-    sent, ticket = pack_messages(
+    sent, ticket, settings = pack_messages(
         adapter_choice_index.reshape(1, -1),
         adapter_mask.reshape(1, -1),
+        prompt_token_length.reshape(1, -1),
         jnp.swapaxes(adapter_down_factors, 1, 2),
         adapter_up_factors,
         wide_count,
@@ -446,9 +472,8 @@
             ring = [(at, (at + shift) % wide_count) for at in range(wide_count)]
             held[chunk].append(lax.ppermute(sent[shift][chunk], "wide", ring))
 
-    my_choice = lax.dynamic_slice_in_dim(adapter_choice_index, wide_at * per_device, per_device)
-    my_mask = lax.dynamic_slice_in_dim(adapter_mask, wide_at * per_device, per_device)
-    my_lengths = lax.dynamic_slice_in_dim(prompt_token_length, wide_at * per_device, per_device)
+    my_settings = lax.dynamic_slice_in_dim(settings, wide_at * per_device, per_device, axis=1)
+    my_choice, my_mask, my_lengths = my_settings[0], my_settings[1], my_settings[2]
     owners = (wide_at - jnp.arange(wide_count, dtype=jnp.int32) + wide_count) % wide_count
     local = my_choice[None, :] - owners[:, None] * owner_portion
     matches = (my_mask[None, :] == 1) & (local >= 0) & (local < owner_portion)
@@ -476,27 +501,24 @@
             lax.ppermute(near_send, "narrow", core),
             lax.ppermute(code, "narrow", across),
         )
-        pieces = 2
     else:
         partial_value = jnp.dot(tokens, value_weight, preferred_element_type=F32)
         base = lax.psum_scatter(partial_value, "narrow", scatter_dimension=1, tiled=True)
         base = jnp.where(inside.reshape(row_total, 1), base, 0.0)
         resident, mask = reload_tokens(tokens, chosen, ticket)
-        pieces = 1
     rows = adapter_down_factors.shape[2]
-    piece = row_total // pieces
-    factors, values = held[0], []
-    for start in range(0, row_total, piece):
-        part, *stacked = shrink(resident, chosen, factors, rows, start, piece)
-        factors = stacked or factors
-        crossed = []
-        if paired:
-            part, shrunk_code = code_shrunk(part, lax.ppermute(part, "narrow", core))
-            crossed = [lax.ppermute(shrunk_code, "narrow", across)]
-        else:
-            part = lax.psum(part, "narrow")
-        values = [finish(base, mask, part, crossed, values, held[0], features, start)]
-    return values[0]
+    messages = held[0]
+    if not paired:
+        part = lax.psum(shrink(resident, chosen, messages, rows, 0, row_total)[0], "narrow")
+        return finish(base, mask, part, [], messages, features, 0)
+    half = row_total // 2
+    send, stacked = shrink(resident, chosen, messages, rows, 2, half)
+    (keep,) = shrink(resident, chosen, [stacked], rows, 1, half)
+    total, code = code_shrunk(keep, lax.ppermute(send, "narrow", core))
+    own = sum_shrunk(total, lax.ppermute(code, "narrow", across), base)
+    other = lax.ppermute(own, "narrow", core)
+    values = finish(base, mask, own, [], messages, features, 1)
+    return finish(base, mask, other, [values], messages, features, 2)
 
 
 def solution(mesh):

time: 42.7 us -> 41.9 us (0.981)
  the two profiles are of different devices: /device:TPU:0 before, /device:TPU:9 now
where the time goes in v7:
time: 41.9 us; the launch traced here: 41.6 us
  Pallas kernels  21.1 us (50%)
  starting transfers between devices  9.84 us (23%)
  waiting for transfers between devices  9.66 us (23%)
  local copies, waits for them, and re-layouts  0.52 us (1%)
    pallas_call x2, Pallas kernels, column_dots(): pl.pallas_call(far_kernel if far else near_kernel, out_shape=out_shape, i...  8.79 us
    ppermute x3, waiting for transfers between devices, on_device(): held[chunk].append(lax.ppermute(sent[shift][chunk], 'wide', ring))  8.61 us
    ppermute x3, starting transfers between devices, on_device(): held[chunk].append(lax.ppermute(sent[shift][chunk], 'wide', ring))  3.77 us
    pallas_call x1, Pallas kernels, code_rows(): pl.pallas_call(code_kernel, out_shape=VMEM((row_total + 16, columns), jnp...  2.45 us
    pallas_call x1, Pallas kernels, reload_tokens(): pl.pallas_call(reload_kernel, out_shape=[VMEM(tokens.shape, BF16), VMEM((...  2.2 us
    pallas_call x1, Pallas kernels, pack_messages(): pl.pallas_call(functools.partial(pack_kernel, wide_count, per_device), ou...  2.19 us
    pallas_call x2, Pallas kernels, finish(): pl.pallas_call(functools.partial(finish_kernel, kind, features), out_shap...  2.15 us
    pallas_call x2, Pallas kernels, shrink(): pl.pallas_call(functools.partial(shrink_kernel, kind, stacking), out_shap...  1.78 us
  transfers between devices with their start and end apart: 10, of which 4 were waited for; matrix products, arithmetic and copies ran while one was open for 2% of the time, Pallas kernels for 43%

profile of v7, /device:TPU:9, one launch (start us, length us, event | category | flops | bytes accessed | tf_op | source)
XLA Modules:
  0.0 41.6 jit_solution(6473387059682024792)
XLA Ops:
  0.0 2.2 %pack_messages.1 = (bf16[64,2304]{1,0:T(8,128)(2,1)}, bf16[64,2304]{1,0:T(8,128)(2,1)}, bf16[64,2304]{1,0:T(8,128)(2,1)}, bf16[64,2304]{1,0:T(8,128)(2,1)}, f32[8,128]{1,0:T(8,128)S(1)}, /*index=5*/s32[3,128]{1,0:T(4,128)S(1)}) custom-call(s32[1,128]{1,0:T(1,128)} %bitcast.11, s32[1,128]{1,0:T(1,128)} %bitcast.12, bf16[2,64,2048]{2,1,0:T(8,128)(2,1)} %bitcast.10, ...), custom_call_target="tpu_custom_call" | custom-call | flops 1 | bytes 1 | tf_op jit(solution)/shard_map/pack_messages/pallas_call | solution.py:118
  2.2 0.7 %collective-permute-start = (f32[8,128]{1,0:T(8,128)S(1)}, f32[8,128]{1,0:T(8,128)S(1)}, u32[]{:S(2)}, u32[]{:S(2)}) collective-permute-start(f32[8,128]{1,0:T(8,128)S(1)} %get-tuple-element.23), channel_id=1, source_target_pairs={{0,1},{1,0},{2,3},{3,2},{4,5},{5,4},{6,7},{7,6},{8,9},{9,8},{10,11... | collective-permute-start | bytes 12296 | tf_op jit(solution)/shard_map/ppermute | solution.py:492
  2.9 1.3 %collective-permute-start.4 = (bf16[64,2304]{1,0:T(8,128)(2,1)}, bf16[64,2304]{1,0:T(8,128)(2,1)S(1)}, u32[]{:S(2)}, u32[]{:S(2)}) collective-permute-start(bf16[64,2304]{1,0:T(8,128)(2,1)} %get-tuple-element.32), channel_id=1, source_target_pairs={{0,4},{4,8},{8,12},{12,0},{1,5},{5,9},{9,13},{13,1},{2,6},{6,10},{... | collective-permute-start | bytes 884744 | tf_op jit(solution)/shard_map/ppermute | solution.py:473
  4.2 1.0 %collective-permute-start.5 = (bf16[64,2304]{1,0:T(8,128)(2,1)}, bf16[64,2304]{1,0:T(8,128)(2,1)S(1)}, u32[]{:S(2)}, u32[]{:S(2)}) collective-permute-start(bf16[64,2304]{1,0:T(8,128)(2,1)} %get-tuple-element.33), channel_id=1, source_target_pairs={{0,8},{4,12},{8,0},{12,4},{1,9},{5,13},{9,1},{13,5},{2,10},{6,14},... | collective-permute-start | bytes 884744 | tf_op jit(solution)/shard_map/ppermute | solution.py:473
  5.3 1.5 %collective-permute-start.6 = (bf16[64,2304]{1,0:T(8,128)(2,1)}, bf16[64,2304]{1,0:T(8,128)(2,1)S(1)}, u32[]{:S(2)}, u32[]{:S(2)}) collective-permute-start(bf16[64,2304]{1,0:T(8,128)(2,1)} %get-tuple-element.34), channel_id=1, source_target_pairs={{0,12},{4,0},{8,4},{12,8},{1,13},{5,1},{9,5},{13,9},{2,14},{6,2},{... | collective-permute-start | bytes 884744 | tf_op jit(solution)/shard_map/ppermute | solution.py:473
  6.7 0.1 constant_dynamic-slice_fusion
  6.8 0.0 collective-permute-done.ticket_ref
  6.8 5.0 %far_columns.1 = (f32[1024,256]{1,0:T(8,128)}, f32[1024,256]{1,0:T(8,128)S(1)}, bf16[1024,2048]{1,0:T(8,128)(2,1)S(1)}) custom-call(bf16[1024,2048]{1,0:T(8,128)(2,1)} %tokens_hbm.3, bf16[2048,1024]{1,0:T(8,128)(2,1)} %weight_hbm.3, f32[8,128]{1,0:T(8,128)S(1)} %collective-permute-done.ticket_ref), custom_call_target="tpu_custom_call" | custom-call | flops 1 | bytes 1 | tf_op jit(solution)/shard_map/far_columns/pallas_call | solution.py:225
  11.9 1.0 %collective-permute-start.2 = (f32[1024,256]{1,0:T(8,128)}, f32[1024,256]{1,0:T(8,128)}, u32[]{:S(2)}, u32[]{:S(2)}) collective-permute-start(f32[1024,256]{1,0:T(8,128)} %get-tuple-element.28), channel_id=1, source_target_pairs={{0,1},{1,0},{2,3},{3,2},{4,5},{5,4},{6,7},{7,6},{8,9},{9,8},{10,11... | collective-permute-start | bytes 3145736 | tf_op jit(solution)/shard_map/ppermute | solution.py:494
  12.8 3.8 %near_columns.1 = (f32[1024,256]{1,0:T(8,128)}, f32[1024,256]{1,0:T(8,128)S(1)}) custom-call(bf16[1024,2048]{1,0:T(8,128)(2,1)S(1)} %get-tuple-element.24.tokens_ref, bf16[2048,1024]{1,0:T(8,128)(2,1)} %weight_hbm.3, f32[1024,256]{1,0:T(8,128)S(1)} %get-tuple-element.25.ticket_ref.keep_ref), custom_call_target="tpu_custom_call" | custom-call | flops 10000000000 | bytes 1 | tf_op jit(solution)/shard_map/near_columns/pallas_call | solution.py:225
  16.6 0.0 copy-start
  16.6 0.1 collective-permute-start.1
  16.7 0.2 fusion.1
  16.9 0.1 fusion.5
  17.0 0.1 broadcast_in_dim.34
  17.1 0.1 broadcast_in_dim.35
  17.2 0.1 lt.46
  17.3 0.0 collective-permute-done.2.arrived_ref
  17.3 2.5 %code_rows.1 = s16[1040,256]{1,0:T(8,128)(2,1)} custom-call(f32[1024,256]{1,0:T(8,128)S(1)} %get-tuple-element.25.ticket_ref.keep_ref, f32[1024,256]{1,0:T(8,128)} %collective-permute-done.2.arrived_ref), custom_call_target="tpu_custom_call" | custom-call | flops 1 | bytes 1 | tf_op jit(solution)/shard_map/code_rows/pallas_call | solution.py:161
  19.7 1.2 %collective-permute-start.3 = (s16[1040,256]{1,0:T(8,128)(2,1)}, s16[1040,256]{1,0:T(8,128)(2,1)S(1)}, u32[]{:S(2)}, u32[]{:S(2)}) collective-permute-start(s16[1040,256]{1,0:T(8,128)(2,1)} %code_rows.1), channel_id=1, source_target_pairs={{0,2},{1,3},{2,0},{3,1},{4,6},{5,7},{6,4},{7,5},{8,10},{9,11},{10,... | collective-permute-start | bytes 1597448 | tf_op jit(solution)/shard_map/ppermute | solution.py:502
  20.9 0.1 broadcast_reduce_fusion
  21.0 0.1 lt.48
  21.1 2.2 %reload_tokens.1 = (bf16[1024,2048]{1,0:T(8,128)(2,1)S(1)}, bf16[1024,512]{1,0:T(8,128)(2,1)S(1)}) custom-call(bf16[1024,2048]{1,0:T(8,128)(2,1)} %tokens_hbm.3, f32[4,1024]{1,0:T(4,128)S(1)} %broadcast_select_fusion.chosen_ref, f32[1024,256]{1,0:T(8,128)S(1)} %get-tuple-element.26.keep_ref.ticket_ref), custom_call_target="tpu_custom_call" | custom-call | flops 1 | bytes 1 | tf_op jit(solution)/shard_map/reload_tokens/pallas_call | solution.py:251
  23.3 0.0 collective-permute-done.4.refs_1_.refs_2_
  23.3 6.5 %collective-permute-done.5.refs_2_.refs_3_ = bf16[64,2304]{1,0:T(8,128)(2,1)S(1)} collective-permute-done((bf16[64,2304]{1,0:T(8,128)(2,1)}, bf16[64,2304]{1,0:T(8,128)(2,1)S(1)}, u32[]{:S(2)}, u32[]{:S(2)}) %collective-permute-start.5) | collective-permute-done | bytes 294944 | tf_op jit(solution)/shard_map/ppermute | solution.py:473
  29.9 2.1 %collective-permute-done.6.refs_3_.refs_4_ = bf16[64,2304]{1,0:T(8,128)(2,1)S(1)} collective-permute-done((bf16[64,2304]{1,0:T(8,128)(2,1)}, bf16[64,2304]{1,0:T(8,128)(2,1)S(1)}, u32[]{:S(2)}, u32[]{:S(2)}) %collective-permute-start.6) | collective-permute-done | bytes 294944 | tf_op jit(solution)/shard_map/ppermute | solution.py:473
  32.0 0.0 copy-done
  32.0 0.9 %shrink.2 = (f32[64,512]{1,0:T(8,128)S(1)}, bf16[256,2048]{1,0:T(8,128)(2,1)S(1)}) custom-call(bf16[1024,2048]{1,0:T(8,128)(2,1)S(1)} %get-tuple-element.30.tokens_ref, f32[4,1024]{1,0:T(4,128)S(1)} %broadcast_select_fusion.chosen_ref, bf16[64,2304]{1,0:T(8,128)(2,1)S(1)} %copy-done, bf16[64,2304]{1,0:T(8,128)(2,1)S(1)} %collective-permute-done.4.refs_1_.refs_2_, ...), custom_call_target="tpu_custom_call" | custom-call | flops 1 | bytes 1 | tf_op jit(solution)/shard_map/shrink/pallas_call | solution.py:333
  32.9 0.5 %collective-permute-start.7 = (f32[64,512]{1,0:T(8,128)S(1)}, f32[64,512]{1,0:T(8,128)S(1)}, u32[]{:S(2)}, u32[]{:S(2)}) collective-permute-start(f32[64,512]{1,0:T(8,128)S(1)} %get-tuple-element.36), channel_id=1, source_target_pairs={{0,1},{1,0},{2,3},{3,2},{4,5},{5,4},{6,7},{7,6},{8,9},{9,8},{10,11... | collective-permute-start | bytes 393224 | tf_op jit(solution)/shard_map/ppermute | solution.py:517
  33.4 0.9 %shrink.3.keep_ref = f32[64,512]{1,0:T(8,128)S(1)} custom-call(bf16[1024,2048]{1,0:T(8,128)(2,1)S(1)} %get-tuple-element.30.tokens_ref, f32[4,1024]{1,0:T(4,128)S(1)} %broadcast_select_fusion.chosen_ref, bf16[256,2048]{1,0:T(8,128)(2,1)S(1)} %get-tuple-element.35.refs_0_), custom_call_target="tpu_custom_call" | custom-call | flops 1 | bytes 1 | tf_op jit(solution)/shard_map/shrink/pallas_call | solution.py:333
  34.3 0.1 collective-permute-done.7.arrived_ref
  34.4 0.1 code_shrunk.1
  34.4 1.3 %collective-permute-start.8 = (s16[80,512]{1,0:T(8,128)(2,1)S(1)}, s16[80,512]{1,0:T(8,128)(2,1)S(1)}, u32[]{:S(2)}, u32[]{:S(2)}) collective-permute-start(s16[80,512]{1,0:T(8,128)(2,1)S(1)} %get-tuple-element.38), channel_id=1, source_target_pairs={{0,2},{1,3},{2,0},{3,1},{4,6},{5,7},{6,4},{7,5},{8,10},{9,11},{10,... | collective-permute-start | bytes 245768 | tf_op jit(solution)/shard_map/ppermute | solution.py:518
  35.7 0.0 collective-permute-done.1.arrived_ref
  35.7 0.0 collective-permute-done.3.code_ref
  35.7 1.5 %base_rows.1.ticket_ref.base_ref = f32[1024,256]{1,0:T(8,128)S(1)} custom-call(s32[32]{0:T(128)S(1)} %get-tuple-element.40.length_ref, f32[1024,256]{1,0:T(8,128)S(1)} %get-tuple-element.26.keep_ref.ticket_ref, f32[1024,256]{1,0:T(8,128)} %collective-permute-done.1.arrived_ref, s16[1040,256]{1,0:T(8,128)(2,1)S(1)} %collective-permute-done.3.code_ref), custom_call_target="tpu_custom_call" | custom-call | flops 1 | bytes 1 | tf_op jit(solution)/shard_map/base_rows/pallas_call | solution.py:283
  37.2 0.9 %collective-permute-done.8.code_ref = s16[80,512]{1,0:T(8,128)(2,1)S(1)} collective-permute-done((s16[80,512]{1,0:T(8,128)(2,1)S(1)}, s16[80,512]{1,0:T(8,128)(2,1)S(1)}, u32[]{:S(2)}, u32[]{:S(2)}) %collective-permute-start.8) | collective-permute-done | bytes 81952 | tf_op jit(solution)/shard_map/ppermute | solution.py:518
  38.2 1.3 %collective-permute-start.9 = (f32[64,512]{1,0:T(8,128)S(1)}, f32[64,512]{1,0:T(8,128)S(1)}, u32[]{:S(2)}, u32[]{:S(2)}) collective-permute-start(f32[64,512]{1,0:T(8,128)S(1)} %sum_shrunk.1.part_ref), channel_id=1, source_target_pairs={{0,1},{1,0},{2,3},{3,2},{4,5},{5,4},{6,7},{7,6},{8,9},{9,8},{10,11... | collective-permute-start | bytes 393224 | tf_op jit(solution)/shard_map/ppermute | solution.py:519
  39.5 1.1 %finish.2.refs_0_ = bf16[1024,256]{1,0:T(8,128)(2,1)} custom-call(f32[1024,256]{1,0:T(8,128)S(1)} %base_rows.1.ticket_ref.base_ref, bf16[1024,512]{1,0:T(8,128)(2,1)S(1)} %get-tuple-element.29.mask_ref, f32[64,512]{1,0:T(8,128)S(1)} %sum_shrunk.1.part_ref, bf16[64,2304]{1,0:T(8,128)(2,1)S(1)} %copy-done, ...), custom_call_target="tpu_custom_call" | custom-call | flops 1 | bytes 1 | tf_op jit(solution)/shard_map/finish/pallas_call | solution.py:425
  40.5 0.0 collective-permute-done.9.part_ref
  40.5 1.1 %finish.3 = bf16[1024,256]{1,0:T(8,128)(2,1)} custom-call(f32[1024,256]{1,0:T(8,128)S(1)} %base_rows.1.ticket_ref.base_ref, bf16[1024,512]{1,0:T(8,128)(2,1)S(1)} %get-tuple-element.29.mask_ref, f32[64,512]{1,0:T(8,128)S(1)} %collective-permute-done.9.part_ref, bf16[1024,256]{1,0:T(8,128)(2,1)} %finish.2.refs_0_, ...), custom_call_target="tpu_custom_call", output_to_operand_aliasing={{}: (3, {})} | custom-call | flops 1 | bytes 1 | tf_op jit(solution)/shard_map/finish/pallas_call | solution.py:425
  (9 shorter events, 0.1 us)
Async XLA Ops:
  2.2 4.6 %collective-permute-start = (f32[8,128]{1,0:T(8,128)S(1)}, f32[8,128]{1,0:T(8,128)S(1)}, u32[]{:S(2)}, u32[]{:S(2)}) collective-permute-start(f32[8,128]{1,0:T(8,128)S(1)} %get-tuple-element.23), channel_id=1, source_target_pairs={{0,1},{1,0},{2,3},{3,2},{4,5},{5,4},{6,7},{7,6},{8,9},{9,8},{10,11... | collective-permute-start | bytes 12296 | tf_op jit(solution)/shard_map/ppermute | solution.py:492
  2.9 20.4 %collective-permute-start.4 = (bf16[64,2304]{1,0:T(8,128)(2,1)}, bf16[64,2304]{1,0:T(8,128)(2,1)S(1)}, u32[]{:S(2)}, u32[]{:S(2)}) collective-permute-start(bf16[64,2304]{1,0:T(8,128)(2,1)} %get-tuple-element.32), channel_id=1, source_target_pairs={{0,4},{4,8},{8,12},{12,0},{1,5},{5,9},{9,13},{13,1},{2,6},{6,10},{... | collective-permute-start | bytes 884744 | tf_op jit(solution)/shard_map/ppermute | solution.py:473
  4.2 25.6 %collective-permute-start.5 = (bf16[64,2304]{1,0:T(8,128)(2,1)}, bf16[64,2304]{1,0:T(8,128)(2,1)S(1)}, u32[]{:S(2)}, u32[]{:S(2)}) collective-permute-start(bf16[64,2304]{1,0:T(8,128)(2,1)} %get-tuple-element.33), channel_id=1, source_target_pairs={{0,8},{4,12},{8,0},{12,4},{1,9},{5,13},{9,1},{13,5},{2,10},{6,14},... | collective-permute-start | bytes 884744 | tf_op jit(solution)/shard_map/ppermute | solution.py:473
  5.3 26.7 %collective-permute-start.6 = (bf16[64,2304]{1,0:T(8,128)(2,1)}, bf16[64,2304]{1,0:T(8,128)(2,1)S(1)}, u32[]{:S(2)}, u32[]{:S(2)}) collective-permute-start(bf16[64,2304]{1,0:T(8,128)(2,1)} %get-tuple-element.34), channel_id=1, source_target_pairs={{0,12},{4,0},{8,4},{12,8},{1,13},{5,1},{9,5},{13,9},{2,14},{6,2},{... | collective-permute-start | bytes 884744 | tf_op jit(solution)/shard_map/ppermute | solution.py:473
  11.9 5.4 %collective-permute-start.2 = (f32[1024,256]{1,0:T(8,128)}, f32[1024,256]{1,0:T(8,128)}, u32[]{:S(2)}, u32[]{:S(2)}) collective-permute-start(f32[1024,256]{1,0:T(8,128)} %get-tuple-element.28), channel_id=1, source_target_pairs={{0,1},{1,0},{2,3},{3,2},{4,5},{5,4},{6,7},{7,6},{8,9},{9,8},{10,11... | collective-permute-start | bytes 3145736 | tf_op jit(solution)/shard_map/ppermute | solution.py:494
  16.6 15.3 %copy-start = (bf16[64,2304]{1,0:T(8,128)(2,1)S(1)}, bf16[64,2304]{1,0:T(8,128)(2,1)}, u32[]{:S(2)}) copy-start(bf16[64,2304]{1,0:T(8,128)(2,1)} %get-tuple-element.31.refs_0_.refs_1_) | copy-start | bytes 884740
  16.6 19.1 %collective-permute-start.1 = (f32[1024,256]{1,0:T(8,128)}, f32[1024,256]{1,0:T(8,128)}, u32[]{:S(2)}, u32[]{:S(2)}) collective-permute-start(f32[1024,256]{1,0:T(8,128)} %get-tuple-element.27), channel_id=1, source_target_pairs={{0,1},{1,0},{2,3},{3,2},{4,5},{5,4},{6,7},{7,6},{8,9},{9,8},{10,11... | collective-permute-start | bytes 3145736 | tf_op jit(solution)/shard_map/ppermute | solution.py:501
  19.7 16.0 %collective-permute-start.3 = (s16[1040,256]{1,0:T(8,128)(2,1)}, s16[1040,256]{1,0:T(8,128)(2,1)S(1)}, u32[]{:S(2)}, u32[]{:S(2)}) collective-permute-start(s16[1040,256]{1,0:T(8,128)(2,1)} %code_rows.1), channel_id=1, source_target_pairs={{0,2},{1,3},{2,0},{3,1},{4,6},{5,7},{6,4},{7,5},{8,10},{9,11},{10,... | collective-permute-start | bytes 1597448 | tf_op jit(solution)/shard_map/ppermute | solution.py:502
  32.9 1.5 %collective-permute-start.7 = (f32[64,512]{1,0:T(8,128)S(1)}, f32[64,512]{1,0:T(8,128)S(1)}, u32[]{:S(2)}, u32[]{:S(2)}) collective-permute-start(f32[64,512]{1,0:T(8,128)S(1)} %get-tuple-element.36), channel_id=1, source_target_pairs={{0,1},{1,0},{2,3},{3,2},{4,5},{5,4},{6,7},{7,6},{8,9},{9,8},{10,11... | collective-permute-start | bytes 393224 | tf_op jit(solution)/shard_map/ppermute | solution.py:517
  34.4 3.7 %collective-permute-start.8 = (s16[80,512]{1,0:T(8,128)(2,1)S(1)}, s16[80,512]{1,0:T(8,128)(2,1)S(1)}, u32[]{:S(2)}, u32[]{:S(2)}) collective-permute-start(s16[80,512]{1,0:T(8,128)(2,1)S(1)} %get-tuple-element.38), channel_id=1, source_target_pairs={{0,2},{1,3},{2,0},{3,1},{4,6},{5,7},{6,4},{7,5},{8,10},{9,11},{10,... | collective-permute-start | bytes 245768 | tf_op jit(solution)/shard_map/ppermute | solution.py:518
  38.2 2.3 %collective-permute-start.9 = (f32[64,512]{1,0:T(8,128)S(1)}, f32[64,512]{1,0:T(8,128)S(1)}, u32[]{:S(2)}, u32[]{:S(2)}) collective-permute-start(f32[64,512]{1,0:T(8,128)S(1)} %sum_shrunk.1.part_ref), channel_id=1, source_target_pairs={{0,1},{1,0},{2,3},{3,2},{4,5},{5,4},{6,7},{7,6},{8,9},{9,8},{10,11... | collective-permute-start | bytes 393224 | tf_op jit(solution)/shard_map/ppermute | solution.py:519

commit v8 on v7

--- a/solution.py
+++ b/solution.py
@@ -50,7 +50,7 @@
     messages, refs = refs[:message_count], refs[message_count:]
     ticket_ref, settings_ref, *refs = refs
     ticket_ref[...] = jnp.zeros_like(ticket_ref)
-    choice_ref, mask_ref, down_ref, up_ref, length_ref, load_sem, message_sem = refs
+    choice_ref, mask_ref, down_ref, up_ref, length_ref, load_sem = refs
     owner_portion, rank, features = down_ref.shape
     columns = up_ref.shape[2]
     rows = rank // CHUNKS
@@ -69,39 +69,27 @@
     wanted = (mask_ref[...] == 1) & (local >= 0) & (local < owner_portion)
     top = jnp.float32(2.0**24)
     key = jnp.where(wanted, (prompt * owner_portion + local).astype(F32), top)
-    copies = []
+    adapters = []
+    many = (wide_count, choice.shape[1])
+    reader = lax.rem(me + lax.broadcasted_iota(jnp.int32, many, 0), wide_count)
+    place = lax.broadcasted_iota(jnp.int32, many, 1) - reader * per_device
+    inside = (place >= 0) & (place < per_device)
+    firsts = jnp.min(jnp.where(inside, key, top), axis=1, keepdims=True)
+    found = jnp.where(firsts < top, firsts, 0.0).astype(jnp.int32)
     for shift in range(wide_count):
-        reader = lax.rem(me + shift, wide_count)
-        low = reader * per_device
-        inside = (prompt >= low) & (prompt < low + per_device)
-        first = jnp.min(jnp.where(inside, key, top))
-        found = jnp.where(first < top, first, 0.0).astype(jnp.int32)
-        adapter = lax.rem(found, owner_portion)
-        for chunk in range(CHUNKS):
-            at = shift * CHUNKS + chunk
-            out = messages[at]
-            span = pl.ds(chunk * rows, rows)
-            copies.append(
-                pltpu.make_async_copy(
-                    down_ref.at[adapter, span, :], out.at[:, pl.ds(0, features)], message_sem.at[2 * at]
-                )
-            )
-            copies.append(
-                pltpu.make_async_copy(
-                    up_ref.at[adapter, span, :],
-                    out.at[:, pl.ds(features, columns)],
-                    message_sem.at[2 * at + 1],
-                )
-            )
+        adapter = lax.rem(found[shift, 0], owner_portion)
+        adapters.append(adapter)
     loads[2].wait()
     loads[3].wait()
-    for copy in copies:
-        copy.start()
+    for at, adapter in enumerate(adapters):
+        for chunk in range(CHUNKS):
+            out = messages[at * CHUNKS + chunk]
+            span = pl.ds(chunk * rows, rows)
+            out[:, pl.ds(0, features)] = down_ref[adapter, span, :]
+            out[:, pl.ds(features, columns)] = up_ref[adapter, span, :]
     loads[4].wait()
     for at, source in enumerate((choice_ref, mask_ref, length_ref)):
         settings_ref[pl.ds(at, 1), :] = source[...]
-    for copy in copies:
-        copy.wait()
 
 
 def pack_messages(choice, mask, lengths, down, up, wide_count, per_device):
@@ -111,9 +99,9 @@
     hbm = whole_block(pl.ANY)
     operands = [choice, mask, down, up, lengths]
     scratch = [VMEM(operand.shape, operand.dtype) for operand in operands]
-    scratch += [pltpu.SemaphoreType.DMA((5,)), pltpu.SemaphoreType.DMA((2 * count,))]
-    out_shape = [pltpu.HBM((rank // CHUNKS, features + columns), BF16)] * count
-    out_specs = [hbm] * count + [whole_block()] * 2
+    scratch += [pltpu.SemaphoreType.DMA((5,))]
+    out_shape = [VMEM((rank // CHUNKS, features + columns), BF16)] * count
+    out_specs = [whole_block()] * (count + 2)
     out_shape += [jax.ShapeDtypeStruct((8, 128), F32), jax.ShapeDtypeStruct((3, choice.shape[1]), jnp.int32)]
     out = pl.pallas_call(
         functools.partial(pack_kernel, wide_count, per_device),

time: 41.9 us -> 41.8 us (level)
  no operation moved by 1% of the time
where the time goes in v8:
time: 41.8 us; the launch traced here: 41.5 us
  Pallas kernels  21.1 us (50%)
  starting transfers between devices  9.87 us (24%)
  waiting for transfers between devices  9.66 us (23%)
  local copies, waits for them, and re-layouts  0.52 us (1%)
    pallas_call x2, Pallas kernels, column_dots(): pl.pallas_call(far_kernel if far else near_kernel, out_shape=out_shape, i...  8.78 us
    ppermute x3, waiting for transfers between devices, on_device(): held[chunk].append(lax.ppermute(sent[shift][chunk], 'wide', ring))  8.61 us
    ppermute x3, starting transfers between devices, on_device(): held[chunk].append(lax.ppermute(sent[shift][chunk], 'wide', ring))  3.77 us
    pallas_call x1, Pallas kernels, code_rows(): pl.pallas_call(code_kernel, out_shape=VMEM((row_total + 16, columns), jnp...  2.46 us
    pallas_call x1, Pallas kernels, reload_tokens(): pl.pallas_call(reload_kernel, out_shape=[VMEM(tokens.shape, BF16), VMEM((...  2.2 us
    pallas_call x2, Pallas kernels, finish(): pl.pallas_call(functools.partial(finish_kernel, kind, features), out_shap...  2.15 us
    pallas_call x1, Pallas kernels, pack_messages(): pl.pallas_call(functools.partial(pack_kernel, wide_count, per_device), ou...  2.11 us
    pallas_call x2, Pallas kernels, shrink(): pl.pallas_call(functools.partial(shrink_kernel, kind, stacking), out_shap...  1.78 us
  transfers between devices with their start and end apart: 10, of which 4 were waited for; matrix products, arithmetic and copies ran while one was open for 2% of the time, Pallas kernels for 43%

profile of v8, /device:TPU:9, one launch (start us, length us, event | category | flops | bytes accessed | tf_op | source)
XLA Modules:
  0.0 41.5 jit_solution(16407222847204968657)
XLA Ops:
  0.0 2.1 %pack_messages.1 = (bf16[64,2304]{1,0:T(8,128)(2,1)S(1)}, bf16[64,2304]{1,0:T(8,128)(2,1)}, bf16[64,2304]{1,0:T(8,128)(2,1)}, bf16[64,2304]{1,0:T(8,128)(2,1)}, ...) custom-call(s32[1,128]{1,0:T(1,128)} %bitcast.11, s32[1,128]{1,0:T(1,128)} %bitcast.12, bf16[2,64,2048]{2,1,0:T(8,128)(2,1)} %bitcast.10, ...), custom_call_target="tpu_custom_call" | custom-call | flops 1 | bytes 1 | tf_op jit(solution)/shard_map/pack_messages/pallas_call | solution.py:106
  2.1 0.7 %collective-permute-start = (f32[8,128]{1,0:T(8,128)S(1)}, f32[8,128]{1,0:T(8,128)S(1)}, u32[]{:S(2)}, u32[]{:S(2)}) collective-permute-start(f32[8,128]{1,0:T(8,128)S(1)} %get-tuple-element.23), channel_id=1, source_target_pairs={{0,1},{1,0},{2,3},{3,2},{4,5},{5,4},{6,7},{7,6},{8,9},{9,8},{10,11... | collective-permute-start | bytes 12296 | tf_op jit(solution)/shard_map/ppermute | solution.py:480
  2.9 1.3 %collective-permute-start.4 = (bf16[64,2304]{1,0:T(8,128)(2,1)}, bf16[64,2304]{1,0:T(8,128)(2,1)S(1)}, u32[]{:S(2)}, u32[]{:S(2)}) collective-permute-start(bf16[64,2304]{1,0:T(8,128)(2,1)} %get-tuple-element.32), channel_id=1, source_target_pairs={{0,4},{4,8},{8,12},{12,0},{1,5},{5,9},{9,13},{13,1},{2,6},{6,10},{... | collective-permute-start | bytes 884744 | tf_op jit(solution)/shard_map/ppermute | solution.py:461
  4.2 1.0 %collective-permute-start.5 = (bf16[64,2304]{1,0:T(8,128)(2,1)}, bf16[64,2304]{1,0:T(8,128)(2,1)S(1)}, u32[]{:S(2)}, u32[]{:S(2)}) collective-permute-start(bf16[64,2304]{1,0:T(8,128)(2,1)} %get-tuple-element.33), channel_id=1, source_target_pairs={{0,8},{4,12},{8,0},{12,4},{1,9},{5,13},{9,1},{13,5},{2,10},{6,14},... | collective-permute-start | bytes 884744 | tf_op jit(solution)/shard_map/ppermute | solution.py:461
  5.2 1.5 %collective-permute-start.6 = (bf16[64,2304]{1,0:T(8,128)(2,1)}, bf16[64,2304]{1,0:T(8,128)(2,1)S(1)}, u32[]{:S(2)}, u32[]{:S(2)}) collective-permute-start(bf16[64,2304]{1,0:T(8,128)(2,1)} %get-tuple-element.34), channel_id=1, source_target_pairs={{0,12},{4,0},{8,4},{12,8},{1,13},{5,1},{9,5},{13,9},{2,14},{6,2},{... | collective-permute-start | bytes 884744 | tf_op jit(solution)/shard_map/ppermute | solution.py:461
  6.6 0.1 constant_dynamic-slice_fusion
  6.7 0.0 collective-permute-done.ticket_ref
  6.7 5.0 %far_columns.1 = (f32[1024,256]{1,0:T(8,128)}, f32[1024,256]{1,0:T(8,128)S(1)}, bf16[1024,2048]{1,0:T(8,128)(2,1)S(1)}) custom-call(bf16[1024,2048]{1,0:T(8,128)(2,1)} %tokens_hbm.3, bf16[2048,1024]{1,0:T(8,128)(2,1)} %weight_hbm.3, f32[8,128]{1,0:T(8,128)S(1)} %collective-permute-done.ticket_ref), custom_call_target="tpu_custom_call" | custom-call | flops 1 | bytes 1 | tf_op jit(solution)/shard_map/far_columns/pallas_call | solution.py:213
  11.8 1.0 %collective-permute-start.2 = (f32[1024,256]{1,0:T(8,128)}, f32[1024,256]{1,0:T(8,128)}, u32[]{:S(2)}, u32[]{:S(2)}) collective-permute-start(f32[1024,256]{1,0:T(8,128)} %get-tuple-element.28), channel_id=1, source_target_pairs={{0,1},{1,0},{2,3},{3,2},{4,5},{5,4},{6,7},{7,6},{8,9},{9,8},{10,11... | collective-permute-start | bytes 3145736 | tf_op jit(solution)/shard_map/ppermute | solution.py:482
  12.8 3.8 %near_columns.1 = (f32[1024,256]{1,0:T(8,128)}, f32[1024,256]{1,0:T(8,128)S(1)}) custom-call(bf16[1024,2048]{1,0:T(8,128)(2,1)S(1)} %get-tuple-element.24.tokens_ref, bf16[2048,1024]{1,0:T(8,128)(2,1)} %weight_hbm.3, f32[1024,256]{1,0:T(8,128)S(1)} %get-tuple-element.25.ticket_ref.keep_ref), custom_call_target="tpu_custom_call" | custom-call | flops 10000000000 | bytes 1 | tf_op jit(solution)/shard_map/near_columns/pallas_call | solution.py:213
  16.5 0.1 collective-permute-start.1
  16.6 0.2 fusion.1
  16.8 0.1 fusion.5
  16.9 0.1 broadcast_in_dim.34
  17.0 0.1 broadcast_in_dim.35
  17.1 0.1 lt.46
  17.2 0.0 collective-permute-done.2.arrived_ref
  17.2 2.5 %code_rows.1 = s16[1040,256]{1,0:T(8,128)(2,1)} custom-call(f32[1024,256]{1,0:T(8,128)S(1)} %get-tuple-element.25.ticket_ref.keep_ref, f32[1024,256]{1,0:T(8,128)} %collective-permute-done.2.arrived_ref), custom_call_target="tpu_custom_call" | custom-call | flops 1 | bytes 1 | tf_op jit(solution)/shard_map/code_rows/pallas_call | solution.py:149
  19.6 1.2 %collective-permute-start.3 = (s16[1040,256]{1,0:T(8,128)(2,1)}, s16[1040,256]{1,0:T(8,128)(2,1)S(1)}, u32[]{:S(2)}, u32[]{:S(2)}) collective-permute-start(s16[1040,256]{1,0:T(8,128)(2,1)} %code_rows.1), channel_id=1, source_target_pairs={{0,2},{1,3},{2,0},{3,1},{4,6},{5,7},{6,4},{7,5},{8,10},{9,11},{10,... | collective-permute-start | bytes 1597448 | tf_op jit(solution)/shard_map/ppermute | solution.py:490
  20.8 0.1 broadcast_reduce_fusion
  21.0 0.1 lt.48
  21.0 2.2 %reload_tokens.1 = (bf16[1024,2048]{1,0:T(8,128)(2,1)S(1)}, bf16[1024,512]{1,0:T(8,128)(2,1)S(1)}) custom-call(bf16[1024,2048]{1,0:T(8,128)(2,1)} %tokens_hbm.3, f32[4,1024]{1,0:T(4,128)S(1)} %broadcast_select_fusion.chosen_ref, f32[1024,256]{1,0:T(8,128)S(1)} %get-tuple-element.26.keep_ref.ticket_ref), custom_call_target="tpu_custom_call" | custom-call | flops 1 | bytes 1 | tf_op jit(solution)/shard_map/reload_tokens/pallas_call | solution.py:239
  23.3 0.0 collective-permute-done.4.refs_1_.refs_2_
  23.3 6.5 %collective-permute-done.5.refs_2_.refs_3_ = bf16[64,2304]{1,0:T(8,128)(2,1)S(1)} collective-permute-done((bf16[64,2304]{1,0:T(8,128)(2,1)}, bf16[64,2304]{1,0:T(8,128)(2,1)S(1)}, u32[]{:S(2)}, u32[]{:S(2)}) %collective-permute-start.5) | collective-permute-done | bytes 294944 | tf_op jit(solution)/shard_map/ppermute | solution.py:461
  29.8 2.1 %collective-permute-done.6.refs_3_.refs_4_ = bf16[64,2304]{1,0:T(8,128)(2,1)S(1)} collective-permute-done((bf16[64,2304]{1,0:T(8,128)(2,1)}, bf16[64,2304]{1,0:T(8,128)(2,1)S(1)}, u32[]{:S(2)}, u32[]{:S(2)}) %collective-permute-start.6) | collective-permute-done | bytes 294944 | tf_op jit(solution)/shard_map/ppermute | solution.py:461
  31.9 0.9 %shrink.2 = (f32[64,512]{1,0:T(8,128)S(1)}, bf16[256,2048]{1,0:T(8,128)(2,1)S(1)}) custom-call(bf16[1024,2048]{1,0:T(8,128)(2,1)S(1)} %get-tuple-element.30.tokens_ref, f32[4,1024]{1,0:T(4,128)S(1)} %broadcast_select_fusion.chosen_ref, bf16[64,2304]{1,0:T(8,128)(2,1)S(1)} %get-tuple-element.31.refs_0_.refs_1_, ...), custom_call_target="tpu_custom_call" | custom-call | flops 1 | bytes 1 | tf_op jit(solution)/shard_map/shrink/pallas_call | solution.py:321
  32.8 0.5 %collective-permute-start.7 = (f32[64,512]{1,0:T(8,128)S(1)}, f32[64,512]{1,0:T(8,128)S(1)}, u32[]{:S(2)}, u32[]{:S(2)}) collective-permute-start(f32[64,512]{1,0:T(8,128)S(1)} %get-tuple-element.36), channel_id=1, source_target_pairs={{0,1},{1,0},{2,3},{3,2},{4,5},{5,4},{6,7},{7,6},{8,9},{9,8},{10,11... | collective-permute-start | bytes 393224 | tf_op jit(solution)/shard_map/ppermute | solution.py:505
  33.3 0.9 %shrink.3.keep_ref = f32[64,512]{1,0:T(8,128)S(1)} custom-call(bf16[1024,2048]{1,0:T(8,128)(2,1)S(1)} %get-tuple-element.30.tokens_ref, f32[4,1024]{1,0:T(4,128)S(1)} %broadcast_select_fusion.chosen_ref, bf16[256,2048]{1,0:T(8,128)(2,1)S(1)} %get-tuple-element.35.refs_0_), custom_call_target="tpu_custom_call" | custom-call | flops 1 | bytes 1 | tf_op jit(solution)/shard_map/shrink/pallas_call | solution.py:321
  34.2 0.1 collective-permute-done.7.arrived_ref
  34.3 0.1 code_shrunk.1
  34.4 1.3 %collective-permute-start.8 = (s16[80,512]{1,0:T(8,128)(2,1)S(1)}, s16[80,512]{1,0:T(8,128)(2,1)S(1)}, u32[]{:S(2)}, u32[]{:S(2)}) collective-permute-start(s16[80,512]{1,0:T(8,128)(2,1)S(1)} %get-tuple-element.38), channel_id=1, source_target_pairs={{0,2},{1,3},{2,0},{3,1},{4,6},{5,7},{6,4},{7,5},{8,10},{9,11},{10,... | collective-permute-start | bytes 245768 | tf_op jit(solution)/shard_map/ppermute | solution.py:506
  35.6 0.0 collective-permute-done.1.arrived_ref
  35.6 0.0 collective-permute-done.3.code_ref
  35.6 1.5 %base_rows.1.ticket_ref.base_ref = f32[1024,256]{1,0:T(8,128)S(1)} custom-call(s32[32]{0:T(128)S(1)} %get-tuple-element.40.length_ref, f32[1024,256]{1,0:T(8,128)S(1)} %get-tuple-element.26.keep_ref.ticket_ref, f32[1024,256]{1,0:T(8,128)} %collective-permute-done.1.arrived_ref, s16[1040,256]{1,0:T(8,128)(2,1)S(1)} %collective-permute-done.3.code_ref), custom_call_target="tpu_custom_call" | custom-call | flops 1 | bytes 1 | tf_op jit(solution)/shard_map/base_rows/pallas_call | solution.py:271
  37.1 0.9 %collective-permute-done.8.code_ref = s16[80,512]{1,0:T(8,128)(2,1)S(1)} collective-permute-done((s16[80,512]{1,0:T(8,128)(2,1)S(1)}, s16[80,512]{1,0:T(8,128)(2,1)S(1)}, u32[]{:S(2)}, u32[]{:S(2)}) %collective-permute-start.8) | collective-permute-done | bytes 81952 | tf_op jit(solution)/shard_map/ppermute | solution.py:506
  38.1 1.3 %collective-permute-start.9 = (f32[64,512]{1,0:T(8,128)S(1)}, f32[64,512]{1,0:T(8,128)S(1)}, u32[]{:S(2)}, u32[]{:S(2)}) collective-permute-start(f32[64,512]{1,0:T(8,128)S(1)} %sum_shrunk.1.part_ref), channel_id=1, source_target_pairs={{0,1},{1,0},{2,3},{3,2},{4,5},{5,4},{6,7},{7,6},{8,9},{9,8},{10,11... | collective-permute-start | bytes 393224 | tf_op jit(solution)/shard_map/ppermute | solution.py:507
  39.4 1.1 %finish.2.refs_0_ = bf16[1024,256]{1,0:T(8,128)(2,1)} custom-call(f32[1024,256]{1,0:T(8,128)S(1)} %base_rows.1.ticket_ref.base_ref, bf16[1024,512]{1,0:T(8,128)(2,1)S(1)} %get-tuple-element.29.mask_ref, f32[64,512]{1,0:T(8,128)S(1)} %sum_shrunk.1.part_ref, bf16[64,2304]{1,0:T(8,128)(2,1)S(1)} %get-tuple-element.31.refs_0_.refs_1_, ...), custom_call_target="tpu_custom_call" | custom-call | flops 1 | bytes 1 | tf_op jit(solution)/shard_map/finish/pallas_call | solution.py:413
  40.5 0.0 collective-permute-done.9.part_ref
  40.5 1.1 %finish.3 = bf16[1024,256]{1,0:T(8,128)(2,1)} custom-call(f32[1024,256]{1,0:T(8,128)S(1)} %base_rows.1.ticket_ref.base_ref, bf16[1024,512]{1,0:T(8,128)(2,1)S(1)} %get-tuple-element.29.mask_ref, f32[64,512]{1,0:T(8,128)S(1)} %collective-permute-done.9.part_ref, bf16[1024,256]{1,0:T(8,128)(2,1)} %finish.2.refs_0_, ...), custom_call_target="tpu_custom_call", output_to_operand_aliasing={{}: (3, {})} | custom-call | flops 1 | bytes 1 | tf_op jit(solution)/shard_map/finish/pallas_call | solution.py:413
  (9 shorter events, 0.1 us)
Async XLA Ops:
  2.1 4.6 %collective-permute-start = (f32[8,128]{1,0:T(8,128)S(1)}, f32[8,128]{1,0:T(8,128)S(1)}, u32[]{:S(2)}, u32[]{:S(2)}) collective-permute-start(f32[8,128]{1,0:T(8,128)S(1)} %get-tuple-element.23), channel_id=1, source_target_pairs={{0,1},{1,0},{2,3},{3,2},{4,5},{5,4},{6,7},{7,6},{8,9},{9,8},{10,11... | collective-permute-start | bytes 12296 | tf_op jit(solution)/shard_map/ppermute | solution.py:480
  2.9 20.4 %collective-permute-start.4 = (bf16[64,2304]{1,0:T(8,128)(2,1)}, bf16[64,2304]{1,0:T(8,128)(2,1)S(1)}, u32[]{:S(2)}, u32[]{:S(2)}) collective-permute-start(bf16[64,2304]{1,0:T(8,128)(2,1)} %get-tuple-element.32), channel_id=1, source_target_pairs={{0,4},{4,8},{8,12},{12,0},{1,5},{5,9},{9,13},{13,1},{2,6},{6,10},{... | collective-permute-start | bytes 884744 | tf_op jit(solution)/shard_map/ppermute | solution.py:461
  4.2 25.6 %collective-permute-start.5 = (bf16[64,2304]{1,0:T(8,128)(2,1)}, bf16[64,2304]{1,0:T(8,128)(2,1)S(1)}, u32[]{:S(2)}, u32[]{:S(2)}) collective-permute-start(bf16[64,2304]{1,0:T(8,128)(2,1)} %get-tuple-element.33), channel_id=1, source_target_pairs={{0,8},{4,12},{8,0},{12,4},{1,9},{5,13},{9,1},{13,5},{2,10},{6,14},... | collective-permute-start | bytes 884744 | tf_op jit(solution)/shard_map/ppermute | solution.py:461
  5.2 26.7 %collective-permute-start.6 = (bf16[64,2304]{1,0:T(8,128)(2,1)}, bf16[64,2304]{1,0:T(8,128)(2,1)S(1)}, u32[]{:S(2)}, u32[]{:S(2)}) collective-permute-start(bf16[64,2304]{1,0:T(8,128)(2,1)} %get-tuple-element.34), channel_id=1, source_target_pairs={{0,12},{4,0},{8,4},{12,8},{1,13},{5,1},{9,5},{13,9},{2,14},{6,2},{... | collective-permute-start | bytes 884744 | tf_op jit(solution)/shard_map/ppermute | solution.py:461
  11.8 5.4 %collective-permute-start.2 = (f32[1024,256]{1,0:T(8,128)}, f32[1024,256]{1,0:T(8,128)}, u32[]{:S(2)}, u32[]{:S(2)}) collective-permute-start(f32[1024,256]{1,0:T(8,128)} %get-tuple-element.28), channel_id=1, source_target_pairs={{0,1},{1,0},{2,3},{3,2},{4,5},{5,4},{6,7},{7,6},{8,9},{9,8},{10,11... | collective-permute-start | bytes 3145736 | tf_op jit(solution)/shard_map/ppermute | solution.py:482
  16.5 19.1 %collective-permute-start.1 = (f32[1024,256]{1,0:T(8,128)}, f32[1024,256]{1,0:T(8,128)}, u32[]{:S(2)}, u32[]{:S(2)}) collective-permute-start(f32[1024,256]{1,0:T(8,128)} %get-tuple-element.27), channel_id=1, source_target_pairs={{0,1},{1,0},{2,3},{3,2},{4,5},{5,4},{6,7},{7,6},{8,9},{9,8},{10,11... | collective-permute-start | bytes 3145736 | tf_op jit(solution)/shard_map/ppermute | solution.py:489
  19.6 16.0 %collective-permute-start.3 = (s16[1040,256]{1,0:T(8,128)(2,1)}, s16[1040,256]{1,0:T(8,128)(2,1)S(1)}, u32[]{:S(2)}, u32[]{:S(2)}) collective-permute-start(s16[1040,256]{1,0:T(8,128)(2,1)} %code_rows.1), channel_id=1, source_target_pairs={{0,2},{1,3},{2,0},{3,1},{4,6},{5,7},{6,4},{7,5},{8,10},{9,11},{10,... | collective-permute-start | bytes 1597448 | tf_op jit(solution)/shard_map/ppermute | solution.py:490
  32.8 1.5 %collective-permute-start.7 = (f32[64,512]{1,0:T(8,128)S(1)}, f32[64,512]{1,0:T(8,128)S(1)}, u32[]{:S(2)}, u32[]{:S(2)}) collective-permute-start(f32[64,512]{1,0:T(8,128)S(1)} %get-tuple-element.36), channel_id=1, source_target_pairs={{0,1},{1,0},{2,3},{3,2},{4,5},{5,4},{6,7},{7,6},{8,9},{9,8},{10,11... | collective-permute-start | bytes 393224 | tf_op jit(solution)/shard_map/ppermute | solution.py:505
  34.4 3.7 %collective-permute-start.8 = (s16[80,512]{1,0:T(8,128)(2,1)S(1)}, s16[80,512]{1,0:T(8,128)(2,1)S(1)}, u32[]{:S(2)}, u32[]{:S(2)}) collective-permute-start(s16[80,512]{1,0:T(8,128)(2,1)S(1)} %get-tuple-element.38), channel_id=1, source_target_pairs={{0,2},{1,3},{2,0},{3,1},{4,6},{5,7},{6,4},{7,5},{8,10},{9,11},{10,... | collective-permute-start | bytes 245768 | tf_op jit(solution)/shard_map/ppermute | solution.py:506
  38.1 2.3 %collective-permute-start.9 = (f32[64,512]{1,0:T(8,128)S(1)}, f32[64,512]{1,0:T(8,128)S(1)}, u32[]{:S(2)}, u32[]{:S(2)}) collective-permute-start(f32[64,512]{1,0:T(8,128)S(1)} %sum_shrunk.1.part_ref), channel_id=1, source_target_pairs={{0,1},{1,0},{2,3},{3,2},{4,5},{5,4},{6,7},{7,6},{8,9},{9,8},{10,11... | collective-permute-start | bytes 393224 | tf_op jit(solution)/shard_map/ppermute | solution.py:507
